TPU v7x, 32 devices: a whole 2x2x4 slice. The times are simulated.
32 devices in a mesh: parts: 2 (over x), dp: 2 (over core), fsdp: 8 (over z, y).
Axes of the slice: x: 2, y: 2, z: 4, core: 2. Of those that a mesh axis runs over, the one named last changes fastest.
Arguments:
- tokens: bfloat16 [16, 256, 8192], P(('parts', 'dp'), None, 'fsdp'), parts along dimension 0, may hold values from -6 to 6
- lengths: int32 [4, 4], P(('parts', 'dp')), parts along dimension 0, may hold values from 1 to 256, 640 in all within a row
- gate_weight: bfloat16 [8192, 14336], P(None, 'fsdp'), may hold values from -0.0625 to 0.0625
- hidden_grad: bfloat16 [16, 256, 14336], P(('parts', 'dp'), None, 'fsdp'), parts along dimension 0, may hold values from -6 to 6
- in_proj: bfloat16 [8192, 64], replicated, may hold values from -0.0625 to 0.0625
- out_proj: bfloat16 [14336, 64], P('fsdp'), may hold values from -0.046875 to 0.046875
- query_sketch: bfloat16 [1024, 4096], P('fsdp', 'dp'), may hold values from -0.1796875 to 0.1796875
Outputs:
- train_sketch: float32 [16, 4096], P(('parts', 'dp'), 'fsdp'), parts along dimension 0
- scores: float32 [16, 1024], P(('parts', 'dp'), 'fsdp'), parts along dimension 0
There are 2 independent parts, one for each index of `parts`. A program takes and returns all parts, laid end to end along the dimension named above; an argument that names none is the same for every part. Nothing has to cross between parts.
Inputs may be any that keep to these rules, and one draw needn't show every extreme that they name: Each row of lengths holds the lengths of one dp index's 4 examples; every row sums to exactly 640 and its largest entry is 256.
All inputs are finite; a program needn't handle non-finite values.
Results may differ from a plain program's by a relative error of at most 0.0042.
Values may be sent and summed in bfloat16 or wider, within the bound.
No kernel may reach another device: no remote copies, remote signals or barrier semaphores. Data moves between devices by JAX's collectives and lax.ppermute only.
A program may use at most 128 MiB of HBM per device.

v0:
```python
import math

import jax
import jax.numpy as jnp
from jax import lax
from jax.sharding import PartitionSpec as P


def on_device(tokens, lengths, gate_weight, hidden_grad, in_proj, out_proj, query_sketch):
    examples, seq_len, shard_width = tokens.shape
    rank_in = in_proj.shape[1]
    rank_out = out_proj.shape[1]
    flat_rows = tokens.reshape(examples * seq_len, shard_width)
    flat_grads = hidden_grad.reshape(examples * seq_len, hidden_grad.shape[2])
    seq_lens = lengths.reshape(examples)
    example_ids = jnp.arange(examples, dtype=jnp.int32)
    position = jnp.arange(seq_len, dtype=jnp.int32)
    live_mask = (
        (position[None, :] < seq_lens[:, None]).astype(jnp.float32).reshape(examples * seq_len)
    )
    row_example = jnp.arange(examples * seq_len, dtype=jnp.int32) // seq_len
    owners = (row_example[:, None] == example_ids[None, :]).astype(jnp.float32) * live_mask[:, None]
    row_count = flat_rows.shape[0]
    block_cols = lax.all_gather(flat_rows, "fsdp", axis=1, tiled=True)
    gate_pre = jnp.dot(block_cols, gate_weight, preferred_element_type=jnp.float32)
    left_proj = jnp.dot(block_cols, in_proj, preferred_element_type=jnp.float32)
    up_grad = (flat_grads.astype(jnp.float32) * jax.nn.silu(gate_pre)).astype(jnp.bfloat16)
    right_proj = jnp.dot(up_grad, out_proj, preferred_element_type=jnp.float32)
    norm_scale = 1.0 / math.sqrt(seq_len)
    right_total = lax.psum(right_proj, "fsdp")
    weighted = (owners[:, :, None] * right_total[:, None, :]).reshape(
        row_count, examples * rank_out
    )
    product = jnp.einsum("ri,rk->ik", left_proj, weighted, precision=lax.Precision.HIGHEST)
    product = product.reshape(rank_in, examples, rank_out).transpose(1, 0, 2)
    sketch = (product * norm_scale).reshape(examples, rank_in * rank_out)
    share_cols = sketch.shape[1] // lax.axis_size("fsdp")
    own_cols = lax.dynamic_slice_in_dim(sketch, lax.axis_index("fsdp") * share_cols, share_cols, 1)
    sketch_half = sketch.astype(jnp.bfloat16)
    queries = lax.all_gather(query_sketch, "dp", axis=1, tiled=True)
    scores = jnp.einsum("ek,qk->eq", sketch_half, queries, preferred_element_type=jnp.float32)
    return (own_cols, scores)


def solution(mesh):
    return jax.shard_map(
        on_device,
        mesh=mesh,
        in_specs=(
            P(("parts", "dp"), None, "fsdp"),
            P(("parts", "dp"), None),
            P(None, "fsdp"),
            P(("parts", "dp"), None, "fsdp"),
            P(),
            P("fsdp", None),
            P("fsdp", "dp"),
        ),
        out_specs=(P(("parts", "dp"), "fsdp"), P(("parts", "dp"), "fsdp")),
        check_vma=False,
    )
```

profile of v0, /device:TPU:0, one launch (start us, length us, event | category | flops | bytes accessed | tf_op | source)
XLA Modules:
  0.0 364.4 jit_solution(15126176696196302406)
XLA Ops:
  8.0 0.0 copy-start
  8.0 0.0 all-gather.3.cloned.1.call-start
  8.1 0.7 all-gather.3.cloned.1.call-update
  8.7 0.0 copy-start.1
  8.8 0.0 copy-start.2
  8.8 0.0 all-reduce.2.cloned.1.call-start
  8.8 232.5 %all-gather.3.cloned.1.call-done = bf16[1024,8192]{1,0:T(8,128)(2,1)} async-done(((bf16[1024,1024]{1,0:T(8,128)(2,1)}), bf16[1024,8192]{1,0:T(8,128)(2,1)}) %all-gather.3.cloned.1.call-update) | async-done | bytes 16777232 | tf_op jit(solution)/shard_map/all_gather | solution.py:24
  241.4 39.2 %fusion = bf16[1024,1792]{1,0:T(8,128)(2,1)S(1)} fusion(bf16[4,256,1792]{2,1,0:T(8,128)(2,1)} %param.10, bf16[1024,8192]{1,0:T(8,128)(2,1)} %all-gather.3.cloned.1.call-done, bf16[8192,1792]{1,0:T(8,128)(2,1)} %param.9), kind=kOutput, calls=%fused_computation.1 | convolution fusion | flops 30077616128 | bytes 53477376 | tf_op jit(solution)/shard_map/dot_general | solution.py:25
  280.6 0.0 copy-done.1
  280.6 1.9 fusion.12
  282.5 0.0 all-reduce.2.cloned.1.call-update
  282.5 0.0 all-gather.5.cloned.1.call-start
  282.6 0.5 all-gather.5.cloned.1.call-update
  283.1 0.0 copy-done.2
  283.1 0.1 convert_bitcast_fusion
  283.2 0.0 copy-done
  283.2 11.1 %convolution_bitcast_fusion = f32[1024,64,1]{0,1,2:T(8,128)S(1)} fusion(bf16[1024,8192]{1,0:T(8,128)(2,1)} %all-gather.3.cloned.1.call-done, bf16[8192,64]{0,1:T(8,128)(2,1)S(1)} %copy-done), kind=kOutput, calls=%fused_computation.2 | convolution fusion | flops 1073741824 | bytes 18087936 | tf_op jit(solution)/shard_map/dot_general | solution.py:26
  294.4 57.1 %all-reduce.2.cloned.1.call-done = f32[1024,64]{0,1:T(8,128)} async-done(((f32[1024,64]{0,1:T(8,128)}), f32[1024,64]{0,1:T(8,128)}) %all-reduce.2.cloned.1.call-update) | async-done | bytes 262160 | tf_op jit(solution)/shard_map/psum | solution.py:30
  351.4 2.6 fusion.1
  354.0 0.1 reshape.87
  354.1 0.6 constant_dynamic-slice_fusion
  354.7 0.0 all-gather.5.cloned.1.call-done
  354.7 2.2 fusion.6
  (3 shorter events, 0.0 us)
Async XLA Ops:
  8.0 275.2 %copy-start = (bf16[8192,64]{0,1:T(8,128)(2,1)S(1)}, bf16[8192,64]{0,1:T(8,128)(2,1)}, u32[]{:S(2)}) copy-start(bf16[8192,64]{0,1:T(8,128)(2,1)} %param.11) | copy-start | bytes 3145732
  8.0 233.3 %all-gather.3.cloned.1.call-start = ((), (), s32[]{:S(2)}) async-start(), calls=%async_computation | async-start | bytes 18874368 | tf_op jit(solution)/shard_map/all_gather | solution.py:24
  8.7 271.8 %copy-start.1 = (bf16[1792,64]{0,1:T(8,128)(2,1)S(1)}, bf16[1792,64]{0,1:T(8,128)(2,1)}, u32[]{:S(2)}) copy-start(bf16[1792,64]{0,1:T(8,128)(2,1)} %param.12) | copy-start | bytes 688132
  8.8 274.4 %copy-start.2 = (s32[1,4]{1,0:T(1,128)S(1)}, s32[1,4]{1,0:T(1,128)}, u32[]{:S(2)}) copy-start(s32[1,4]{1,0:T(1,128)} %param.8) | copy-start | bytes 52
  8.8 342.7 %all-reduce.2.cloned.1.call-start = ((), (), s32[]{:S(2)}) async-start(), calls=%async_computation.1 | async-start | bytes 524288 | tf_op jit(solution)/shard_map/psum | solution.py:30
  282.5 72.2 %all-gather.5.cloned.1.call-start = ((), (), s32[]{:S(2)}) async-start(), calls=%async_computation.2 | async-start | bytes 1572864 | tf_op jit(solution)/shard_map/all_gather | solution.py:40
Sparse Core Ops, SparseCore 0:
  11.0 230.2 all-gather.2
  282.7 68.7 all-reduce.1
Sparse Core Ops, SparseCore 1:
  284.6 7.1 all-gather.4
where the time goes:
time: 365 us; the launch traced here: 364 us
  waiting for transfers between devices  291 us (80%)
  matrix products  57 us (16%)
  between operations  15.6 us (4%)
    all_gather x1, waiting for transfers between devices, on_device(): block_cols = lax.all_gather(flat_rows, 'fsdp', axis=1, tiled=True)  233 us
    psum x1, waiting for transfers between devices, on_device(): right_total = lax.psum(right_proj, 'fsdp')  57.1 us
    dot_general x1, matrix products, on_device(): jnp.dot(block_cols, gate_weight, preferred_element_type=jnp.float32)  39.2 us
    dot_general x1, matrix products, on_device(): left_proj = jnp.dot(block_cols, in_proj, preferred_element_type=jnp.float32)  11.1 us
  transfers between devices with their start and end apart: 3, of which 2 were waited for; matrix products, arithmetic and copies ran while one was open for 4% of the time, Pallas kernels for 0%

commit v1 on v0

v1 whole, which is shorter than its diff:
```python
import math

import jax
import jax.numpy as jnp
from jax import lax
from jax.sharding import PartitionSpec as P

LIVE = 640
CHUNKS = 2


def ring_order(size, folded):
    if folded:
        return list(range(0, size, 2)) + list(range(size - 1, 0, -2))
    return list(range(size))


def pack_matrix(lengths, seq_len, dtype):
    seq_lens = lengths.reshape(-1)
    ends = jnp.cumsum(seq_lens)
    rows = jnp.arange(LIVE, dtype=jnp.int32)
    example = jnp.sum((rows[:, None] >= ends[None, :]).astype(jnp.int32), axis=1)
    starts = ends - seq_lens
    owners = example[:, None] == jnp.arange(seq_lens.shape[0], dtype=jnp.int32)[None, :]
    start = jnp.sum(jnp.where(owners, starts[None, :], 0), axis=1)
    source = example * seq_len + rows - start
    slots = jnp.arange(seq_lens.shape[0] * seq_len, dtype=jnp.int32)
    return (source[:, None] == slots[None, :]).astype(dtype), owners


def on_device(order, tokens, lengths, gate_weight, hidden_grad, in_proj, out_proj, query_sketch):
    examples, seq_len, width = tokens.shape
    rank_in, rank_out = in_proj.shape[1], out_proj.shape[1]
    size = len(order)
    cw = [(order[i], order[(i + 1) % size]) for i in range(size)]
    ccw = [(d, s) for s, d in cw]
    place = [0] * size
    for i, d in enumerate(order):
        place[d] = i
    me = jnp.asarray(place, jnp.int32)[lax.axis_index("fsdp")]
    order_ids = jnp.asarray(order, jnp.int32)

    pick, owners = pack_matrix(lengths, seq_len, tokens.dtype)
    flat_rows = tokens.reshape(examples * seq_len, width)
    flat_grads = hidden_grad.reshape(examples * seq_len, -1)
    rows_of = LIVE // CHUNKS
    picks = [pick[c * rows_of : (c + 1) * rows_of] for c in range(CHUNKS)]
    queries = lax.all_gather(query_sketch, "dp", axis=1, tiled=True)

    own = [jnp.dot(p, flat_rows, preferred_element_type=jnp.float32).astype(tokens.dtype) for p in picks]
    gate = [None] * CHUNKS
    left = [None] * CHUNKS

    def absorb(c, block, step):
        source = order_ids[lax.rem(me - step + size, size)]
        weight = lax.dynamic_slice_in_dim(gate_weight, source * width, width, 0)
        proj = lax.dynamic_slice_in_dim(in_proj, source * width, width, 0)
        g = jnp.dot(block, weight, preferred_element_type=jnp.float32)
        l = jnp.dot(block, proj, preferred_element_type=jnp.float32)
        gate[c] = g if gate[c] is None else gate[c] + g
        left[c] = l if left[c] is None else left[c] + l

    right_going, left_going = list(own), list(own)
    for step in range(1, size // 2 + 1):
        last = step == size // 2
        new_right, new_left = list(right_going), list(left_going)
        for c in range(CHUNKS):
            if not last or c % 2 == 0:
                new_right[c] = lax.ppermute(right_going[c], "fsdp", cw)
            if not last or c % 2 == 1:
                new_left[c] = lax.ppermute(left_going[c], "fsdp", ccw)
        for c in range(CHUNKS):
            if step == 1:
                absorb(c, own[c], 0)
            else:
                absorb(c, right_going[c], step - 1)
                absorb(c, left_going[c], 1 - step)
        right_going, left_going = new_right, new_left
    grads = [jnp.dot(p, flat_grads, preferred_element_type=jnp.float32) for p in picks]
    for c in range(CHUNKS):
        absorb(c, (right_going if c % 2 == 0 else left_going)[c], size // 2)

    total = None
    for c in range(CHUNKS):
        up_grad = (grads[c] * jax.nn.silu(gate[c])).astype(jnp.bfloat16)
        right = jnp.dot(up_grad, out_proj, preferred_element_type=jnp.float32)
        owned = owners[c * rows_of : (c + 1) * rows_of]
        weighted = jnp.where(owned[:, :, None], right[:, None, :], 0.0)
        weighted = weighted.reshape(rows_of, examples * rank_out)
        part = jnp.einsum("ri,rk->ik", left[c], weighted, precision=lax.Precision.HIGHEST)
        total = part if total is None else total + part
    hop = 1
    while hop < size:
        total = total + lax.ppermute(total, "fsdp", [(i, i ^ hop) for i in range(size)])
        hop *= 2
    sketch = total.reshape(rank_in, examples, rank_out).transpose(1, 0, 2)
    sketch = (sketch * (1.0 / math.sqrt(seq_len))).reshape(examples, rank_in * rank_out)
    share = sketch.shape[1] // size
    own_cols = lax.dynamic_slice_in_dim(sketch, lax.axis_index("fsdp") * share, share, 1)
    scores = jnp.einsum(
        "ek,qk->eq", sketch.astype(jnp.bfloat16), queries, preferred_element_type=jnp.float32
    )
    return (own_cols, scores)


def solution(mesh):
    size = mesh.shape["fsdp"]
    order = ring_order(size, folded=mesh.shape["parts"] == 2)

    def per_device(*args):
        return on_device(order, *args)

    return jax.shard_map(
        per_device,
        mesh=mesh,
        in_specs=(
            P(("parts", "dp"), None, "fsdp"),
            P(("parts", "dp"), None),
            P(None, "fsdp"),
            P(("parts", "dp"), None, "fsdp"),
            P(),
            P("fsdp", None),
            P("fsdp", "dp"),
        ),
        out_specs=(P(("parts", "dp"), "fsdp"), P(("parts", "dp"), "fsdp")),
        check_vma=False,
    )
```

time: 365 us -> 171 us (0.47)
  waiting for transfers between devices: 291 us -> 23.9 us
  matrix products: 57 us -> 93.7 us
  starting transfers between devices: 0.12 us -> 22.5 us
  between operations: 15.6 us -> 24.9 us
    all_gather x1 -> x0, waiting for transfers between devices: 233 us -> none  [on_device(): block_cols = lax.all_gather(flat_rows, 'fsdp', axis=1, tiled=True)]
    psum x1 -> x0, waiting for transfers between devices: 57.1 us -> none  [on_device(): right_total = lax.psum(right_proj, 'fsdp')]
    dot_general x5 -> x39, matrix products: 57 us -> 93.7 us  [the longest x14 53.2 us: absorb(): g = jnp.dot(block, weight, preferred_element_type=jnp.float32)]
    ppermute x0 -> x17, waiting for transfers between devices: none -> 23.9 us  [the longest x7 10.9 us: on_device(): new_right[c] = lax.ppermute(right_going[c], 'fsdp', cw)]
    ppermute x0 -> x17, starting transfers between devices: none -> 22.5 us  [the longest x7 13.1 us: on_device(): new_left[c] = lax.ppermute(left_going[c], 'fsdp', ccw)]
  transfers between devices with their start and end apart: 3 -> 18, of which waited for: 2 -> 5; matrix products, arithmetic and copies ran while one was open for 4% -> 54% of each run, Pallas kernels for 0% -> 0%
where the time goes in v1:
time: 171 us; the launch traced here: 170 us
  matrix products  93.7 us (55%)
  between operations  24.9 us (15%)
  waiting for transfers between devices  23.9 us (14%)
  starting transfers between devices  22.5 us (13%)
  other arithmetic  2.31 us (1%)
  local copies, waits for them, and re-layouts  2.3 us (1%)
    dot_general x14, matrix products, absorb(): g = jnp.dot(block, weight, preferred_element_type=jnp.float32)  53.2 us
    dot_general x16, matrix products, absorb(): l = jnp.dot(block, proj, preferred_element_type=jnp.float32)  15.3 us
    ppermute x7, starting transfers between devices, on_device(): new_left[c] = lax.ppermute(left_going[c], 'fsdp', ccw)  13.1 us
    ppermute x7, waiting for transfers between devices, on_device(): new_right[c] = lax.ppermute(right_going[c], 'fsdp', cw)  10.9 us
    dot_general x2, matrix products, on_device(): right = jnp.dot(up_grad, out_proj, preferred_element_type=jnp.float32)  10.6 us
    dot_general x2, matrix products, on_device(): jnp.dot(p, flat_grads, preferred_element_type=jnp.float32)  8.02 us
    ppermute x3, waiting for transfers between devices, on_device(): lax.ppermute(total, 'fsdp', [(i, i ^ hop) for i in range(size)])  7.01 us
    ppermute x3, starting transfers between devices, on_device(): lax.ppermute(total, 'fsdp', [(i, i ^ hop) for i in range(size)])  6.9 us
  transfers between devices with their start and end apart: 18, of which 5 were waited for; matrix products, arithmetic and copies ran while one was open for 54% of the time, Pallas kernels for 0%

profile of v1, /device:TPU:0, one launch (start us, length us, event | category | flops | bytes accessed | tf_op | source)
XLA Modules:
  0.0 169.7 jit_solution(15855958815348083540)
XLA Ops:
  11.2 3.0 %collective-permute-start.8 = (bf16[320,1024]{1,0:T(8,128)(2,1)}, bf16[320,1024]{1,0:T(8,128)(2,1)}, u32[]{:S(2)}, u32[]{:S(2)}) collective-permute-start(bf16[320,1024]{1,0:T(8,128)(2,1)} %convolution_convert_fusion), channel_id=1, source_target_pairs={{2,0},{4,2},{6,4},{7,6},{5,7},{3,5},{1,3},{0,1},{10,8},{12,10},{14... | collective-permute-start | bytes 1966088 | tf_op jit(solution)/shard_map/ppermute | solution.py:71
  16.0 2.0 %collective-permute-start.1 = (bf16[320,1024]{1,0:T(8,128)(2,1)}, bf16[320,1024]{1,0:T(8,128)(2,1)}, u32[]{:S(2)}, u32[]{:S(2)}) collective-permute-start(bf16[320,1024]{1,0:T(8,128)(2,1)} %convolution_convert_fusion.1), channel_id=1, source_target_pairs={{2,0},{4,2},{6,4},{7,6},{5,7},{3,5},{1,3},{0,1},{10,8},{12,10},{14... | collective-permute-start | bytes 1966088 | tf_op jit(solution)/shard_map/ppermute | solution.py:71
  25.2 5.3 %fusion.28 = f32[320,1792]{1,0:T(8,128)} fusion(bf16[320,1024]{1,0:T(8,128)(2,1)} %convolution_convert_fusion, bf16[8192,1792]{1,0:T(8,128)(2,1)} %param.11, s32[]{:T(128)S(6)} %select_n.108), kind=kOutput, calls=%fused_computation.28 | convolution fusion | flops 1174405120 | bytes 6619140 | tf_op jit(solution)/shard_map/dot_general | solution.py:58
  30.5 5.2 %fusion.30 = f32[320,1792]{1,0:T(8,128)} fusion(bf16[320,1024]{1,0:T(8,128)(2,1)} %convolution_convert_fusion.1, bf16[8192,1792]{1,0:T(8,128)(2,1)} %param.11, s32[]{:T(128)S(6)} %select_n.108), kind=kOutput, calls=%fused_computation.30 | convolution fusion | flops 1174405120 | bytes 6619140 | tf_op jit(solution)/shard_map/dot_general | solution.py:58
  35.7 2.9 %fusion.90 = f32[320,1792]{1,0:T(8,128)} fusion(bf16[1024,1792]{1,0:T(8,128)(2,1)S(1)} %bitcast.81, pred[640,1024]{1,0:T(32,128)(4,1)S(1)} %copy-done.6), kind=kOutput, calls=%fused_computation.70 | convolution fusion | flops 1174405120 | bytes 6291456 | tf_op jit(solution)/shard_map/dot_general | solution.py:79
  46.0 5.1 %fusion.93 = f32[320,1792]{1,0:T(8,128)} fusion(bf16[1024,1792]{1,0:T(8,128)(2,1)} %bitcast.80, pred[640,1024]{1,0:T(32,128)(4,1)S(1)} %copy-done.6), kind=kOutput, calls=%fused_computation.73 | convolution fusion | flops 1174405120 | bytes 6291456 | tf_op jit(solution)/shard_map/dot_general | solution.py:79
  51.1 2.0 %collective-permute-start.10 = (bf16[320,1024]{1,0:T(8,128)(2,1)}, bf16[320,1024]{1,0:T(8,128)(2,1)}, u32[]{:S(2)}, u32[]{:S(2)}) collective-permute-start(bf16[320,1024]{1,0:T(8,128)(2,1)} %collective-permute-done.8), channel_id=1, source_target_pairs={{2,0},{4,2},{6,4},{7,6},{5,7},{3,5},{1,3},{0,1},{10,8},{12,10},{14... | collective-permute-start | bytes 1966088 | tf_op jit(solution)/shard_map/ppermute | solution.py:71
  53.2 1.9 %collective-permute-start.3 = (bf16[320,1024]{1,0:T(8,128)(2,1)}, bf16[320,1024]{1,0:T(8,128)(2,1)S(1)}, u32[]{:S(2)}, u32[]{:S(2)}) collective-permute-start(bf16[320,1024]{1,0:T(8,128)(2,1)} %collective-permute-done.1), channel_id=1, source_target_pairs={{2,0},{4,2},{6,4},{7,6},{5,7},{3,5},{1,3},{0,1},{10,8},{12,10},{14... | collective-permute-start | bytes 1966088 | tf_op jit(solution)/shard_map/ppermute | solution.py:71
  58.0 3.7 %fusion.20 = f32[320,1792]{1,0:T(8,128)S(1)} fusion(bf16[320,1024]{1,0:T(8,128)(2,1)} %collective-permute-done.8, bf16[8192,1792]{1,0:T(8,128)(2,1)} %param.11, s32[]{:T(128)S(6)} %select_n.112), kind=kOutput, calls=%fused_computation.20 | convolution fusion | flops 1174405120 | bytes 6619140 | tf_op jit(solution)/shard_map/dot_general | solution.py:58
  61.8 3.7 %fusion.22 = f32[320,1792]{1,0:T(8,128)S(1)} fusion(bf16[320,1024]{1,0:T(8,128)(2,1)} %collective-permute-done.1, bf16[8192,1792]{1,0:T(8,128)(2,1)} %param.11, s32[]{:T(128)S(6)} %select_n.112), kind=kOutput, calls=%fused_computation.22 | convolution fusion | flops 1174405120 | bytes 6619140 | tf_op jit(solution)/shard_map/dot_general | solution.py:58
  66.3 3.8 %fusion.41 = f32[320,1792]{1,0:T(8,128)S(1)} fusion(f32[320,1792]{1,0:T(8,128)S(1)} %fusion.20, f32[320,1792]{1,0:T(8,128)S(1)} %copy-done.4, bf16[320,1024]{1,0:T(8,128)(2,1)} %collective-permute-done.7, bf16[8192,1792]{1,0:T(8,128)(2,1)} %param.11, s32[]{:T(128)S(6)} %select_n.110), kind=kOutput, calls=%fused_computation.35 | convolution fusion | flops 1175552000 | bytes 11206660 | tf_op jit(solution)/shard_map/dot_general | solution.py:58
  70.1 3.6 %fusion.35 = f32[320,1792]{1,0:T(8,128)S(1)} fusion(f32[320,1792]{1,0:T(8,128)S(1)} %fusion.22, f32[320,1792]{1,0:T(8,128)S(1)} %copy-done.3, bf16[320,1024]{1,0:T(8,128)(2,1)S(1)} %collective-permute-done, bf16[8192,1792]{1,0:T(8,128)(2,1)} %param.11, s32[]{:T(128)S(6)} %select_n.110), kind=kOutput, calls=%fused_computation.33 | convolution fusion | flops 1175552000 | bytes 11206660 | tf_op jit(solution)/shard_map/dot_general | solution.py:58
  75.1 2.0 %collective-permute-start.12 = (bf16[320,1024]{1,0:T(8,128)(2,1)}, bf16[320,1024]{1,0:T(8,128)(2,1)}, u32[]{:S(2)}, u32[]{:S(2)}) collective-permute-start(bf16[320,1024]{1,0:T(8,128)(2,1)} %collective-permute-done.10), channel_id=1, source_target_pairs={{2,0},{4,2},{6,4},{7,6},{5,7},{3,5},{1,3},{0,1},{10,8},{12,10},{14... | collective-permute-start | bytes 1966088 | tf_op jit(solution)/shard_map/ppermute | solution.py:71
  77.1 5.9 %collective-permute-done.3 = bf16[320,1024]{1,0:T(8,128)(2,1)S(1)} collective-permute-done((bf16[320,1024]{1,0:T(8,128)(2,1)}, bf16[320,1024]{1,0:T(8,128)(2,1)S(1)}, u32[]{:S(2)}, u32[]{:S(2)}) %collective-permute-start.3) | collective-permute-done | bytes 655392 | tf_op jit(solution)/shard_map/ppermute | solution.py:71
  83.1 1.9 %collective-permute-start.5 = (bf16[320,1024]{1,0:T(8,128)(2,1)S(1)}, bf16[320,1024]{1,0:T(8,128)(2,1)}, u32[]{:S(2)}, u32[]{:S(2)}) collective-permute-start(bf16[320,1024]{1,0:T(8,128)(2,1)S(1)} %collective-permute-done.3), channel_id=1, source_target_pairs={{2,0},{4,2},{6,4},{7,6},{5,7},{3,5},{1,3},{0,1},{10,8},{12,10},{14... | collective-permute-start | bytes 1966088 | tf_op jit(solution)/shard_map/ppermute | solution.py:71
  86.9 5.3 %fusion.12 = f32[320,1792]{1,0:T(8,128)} fusion(bf16[320,1024]{1,0:T(8,128)(2,1)} %collective-permute-done.10, bf16[8192,1792]{1,0:T(8,128)(2,1)} %param.11, s32[]{:T(128)S(6)} %select_n.116), kind=kOutput, calls=%fused_computation.12 | convolution fusion | flops 1174405120 | bytes 6619140 | tf_op jit(solution)/shard_map/dot_general | solution.py:58
  92.3 2.8 %fusion.14 = f32[320,1792]{1,0:T(8,128)} fusion(bf16[320,1024]{1,0:T(8,128)(2,1)S(1)} %collective-permute-done.3, bf16[8192,1792]{1,0:T(8,128)(2,1)S(1)} %bitcast.75, s32[]{:T(128)S(6)} %select_n.116), kind=kOutput, calls=%fused_computation.14 | convolution fusion | flops 1174405120 | bytes 6619140 | tf_op jit(solution)/shard_map/dot_general | solution.py:58
  96.8 3.1 %fusion.53 = f32[320,1792]{1,0:T(8,128)S(1)} fusion(f32[320,1792]{1,0:T(8,128)} %fusion.12, f32[320,1792]{1,0:T(8,128)S(1)} %fusion.41, bf16[320,1024]{1,0:T(8,128)(2,1)S(1)} %collective-permute-done.9, bf16[8192,1792]{1,0:T(8,128)(2,1)S(1)} %bitcast.75, s32[]{:T(128)S(6)} %select_n.114), kind=kOutput, calls=%fused_computation.39 | convolution fusion | flops 1175552000 | bytes 11206660 | tf_op jit(solution)/shard_map/dot_general | solution.py:58
  100.6 3.1 %fusion.47 = f32[320,1792]{1,0:T(8,128)S(1)} fusion(f32[320,1792]{1,0:T(8,128)} %fusion.14, f32[320,1792]{1,0:T(8,128)S(1)} %fusion.35, bf16[320,1024]{1,0:T(8,128)(2,1)S(1)} %collective-permute-done.2, bf16[8192,1792]{1,0:T(8,128)(2,1)S(1)} %bitcast.75, s32[]{:T(128)S(6)} %select_n.114), kind=kOutput, calls=%fused_computation.37 | convolution fusion | flops 1175552000 | bytes 11206660 | tf_op jit(solution)/shard_map/dot_general | solution.py:58
  104.1 10.9 %collective-permute-done.4 = bf16[320,1024]{1,0:T(8,128)(2,1)S(1)} collective-permute-done((bf16[320,1024]{1,0:T(8,128)(2,1)S(1)}, bf16[320,1024]{1,0:T(8,128)(2,1)S(1)}, u32[]{:S(2)}, u32[]{:S(2)}) %collective-permute-start.4) | collective-permute-done | bytes 655392 | tf_op jit(solution)/shard_map/ppermute | solution.py:69
  117.9 3.9 %fusion.4 = f32[320,1792]{1,0:T(8,128)} fusion(bf16[320,1024]{1,0:T(8,128)(2,1)} %collective-permute-done.12, bf16[8192,1792]{1,0:T(8,128)(2,1)S(1)} %bitcast.75, s32[]{:T(128)S(6)} %select_n.120), kind=kOutput, calls=%fused_computation.4 | convolution fusion | flops 1174405120 | bytes 6619140 | tf_op jit(solution)/shard_map/dot_general | solution.py:58
  121.8 2.5 %fusion.6 = f32[320,1792]{1,0:T(8,128)S(1)} fusion(bf16[320,1024]{1,0:T(8,128)(2,1)} %collective-permute-done.5, bf16[8192,1792]{1,0:T(8,128)(2,1)S(1)} %bitcast.75, s32[]{:T(128)S(6)} %select_n.120), kind=kOutput, calls=%fused_computation.6 | convolution fusion | flops 1174405120 | bytes 6619140 | tf_op jit(solution)/shard_map/dot_general | solution.py:58
  124.3 4.5 %fusion.65 = f32[320,1792]{1,0:T(8,128)} fusion(f32[320,1792]{1,0:T(8,128)} %fusion.4, f32[320,1792]{1,0:T(8,128)S(1)} %fusion.53, bf16[320,1024]{1,0:T(8,128)(2,1)S(1)} %collective-permute-done.11, bf16[8192,1792]{1,0:T(8,128)(2,1)S(1)} %bitcast.75, s32[]{:T(128)S(6)} %select_n.118), kind=kOutput, calls=%fused_computation.43 | convolution fusion | flops 1175552000 | bytes 11206660 | tf_op jit(solution)/shard_map/dot_general | solution.py:58
  129.5 2.8 %fusion.59 = f32[320,1792]{1,0:T(8,128)} fusion(f32[320,1792]{1,0:T(8,128)S(1)} %fusion.6, f32[320,1792]{1,0:T(8,128)S(1)} %fusion.47, bf16[320,1024]{1,0:T(8,128)(2,1)S(1)} %collective-permute-done.4, bf16[8192,1792]{1,0:T(8,128)(2,1)S(1)} %bitcast.75, s32[]{:T(128)S(6)} %select_n.118), kind=kOutput, calls=%fused_computation.41 | convolution fusion | flops 1175552000 | bytes 11206660 | tf_op jit(solution)/shard_map/dot_general | solution.py:58
  132.4 5.1 %fusion.79 = f32[320,64]{0,1:T(8,128)S(1)} fusion(bf16[1792,64]{0,1:T(8,128)(2,1)S(1)} %copy-done.9, f32[320,1792]{1,0:T(8,128)} %fusion.93, f32[320,1792]{1,0:T(8,128)} %fusion.59, bf16[320,1024]{1,0:T(8,128)(2,1)S(1)} %collective-permute-done.6, bf16[8192,1792]{1,0:T(8,128)(2,1)} %param.11, s32[]{:T(128)S(6)} %select_n.122), kind=kOutput, calls=%fused_computation.51 | convolution fusion | flops 1251819520 | bytes 9224196 | tf_op jit(solution)/shard_map/dot_general | solution.py:86
  138.4 5.5 %fusion.82 = f32[320,64]{0,1:T(8,128)S(1)} fusion(bf16[1792,64]{0,1:T(8,128)(2,1)} %param.14, f32[320,1792]{1,0:T(8,128)} %fusion.90, f32[320,1792]{1,0:T(8,128)} %fusion.65, bf16[320,1024]{1,0:T(8,128)(2,1)} %collective-permute-done.13, bf16[8192,1792]{1,0:T(8,128)(2,1)} %param.11, s32[]{:T(128)S(6)} %select_n.122), kind=kOutput, calls=%fused_computation.52 | convolution fusion | flops 1251819520 | bytes 9224196 | tf_op jit(solution)/shard_map/dot_general | solution.py:86
  145.9 2.0 %collective-permute-start.14 = (f32[64,256]{1,0:T(8,128)S(1)}, f32[64,256]{1,0:T(8,128)S(1)}, u32[]{:S(2)}, u32[]{:S(2)}) collective-permute-start(f32[64,256]{1,0:T(8,128)S(1)} %convolution_add_fusion.10), channel_id=1, source_target_pairs={{0,1},{1,0},{2,3},{3,2},{4,5},{5,4},{6,7},{7,6},{8,9},{9,8},{10,11... | collective-permute-start | bytes 196616 | tf_op jit(solution)/shard_map/ppermute | solution.py:94
  147.9 2.3 %collective-permute-done.14 = f32[64,256]{1,0:T(8,128)S(1)} collective-permute-done((f32[64,256]{1,0:T(8,128)S(1)}, f32[64,256]{1,0:T(8,128)S(1)}, u32[]{:S(2)}, u32[]{:S(2)}) %collective-permute-start.14) | collective-permute-done | bytes 65568 | tf_op jit(solution)/shard_map/ppermute | solution.py:94
  152.1 2.5 %collective-permute-done.15 = f32[64,256]{1,0:T(8,128)S(1)} collective-permute-done((f32[64,256]{1,0:T(8,128)S(1)}, f32[64,256]{1,0:T(8,128)S(1)}, u32[]{:S(2)}, u32[]{:S(2)}) %collective-permute-start.15) | collective-permute-done | bytes 65568 | tf_op jit(solution)/shard_map/ppermute | solution.py:94
  154.6 3.0 %collective-permute-start.16 = (f32[64,256]{1,0:T(8,128)S(1)}, f32[64,256]{1,0:T(8,128)S(1)}, u32[]{:S(2)}, u32[]{:S(2)}) collective-permute-start(f32[64,256]{1,0:T(8,128)S(1)} %add.339), channel_id=1, source_target_pairs={{0,4},{1,5},{2,6},{3,7},{4,0},{5,1},{6,2},{7,3},{8,12},{9,13},{10,... | collective-permute-start | bytes 196616 | tf_op jit(solution)/shard_map/ppermute | solution.py:94
  157.6 2.2 %collective-permute-done.16 = f32[64,256]{1,0:T(8,128)S(1)} collective-permute-done((f32[64,256]{1,0:T(8,128)S(1)}, f32[64,256]{1,0:T(8,128)S(1)}, u32[]{:S(2)}, u32[]{:S(2)}) %collective-permute-start.16) | collective-permute-done | bytes 65568 | tf_op jit(solution)/shard_map/ppermute | solution.py:94
  160.7 2.2 %fusion.118 = f32[4,128]{1,0:T(4,128)} fusion(bf16[128,4096]{1,0:T(8,128)(2,1)} %all-gather.2.cloned.1.call-done, f32[4,4096]{1,0:T(4,128)S(1)} %reshape.88), kind=kOutput, calls=%fused_computation.101 | convolution fusion | flops 4210688 | bytes 1116160 | tf_op jit(solution)/shard_map/ek,qk->eq/dot_general | solution.py:100
  (99 shorter events, 29.1 us)
Async XLA Ops:
  7.2 153.5 %all-gather.2.cloned.1.call-start = ((), (), s32[]{:S(2)}) async-start(), calls=%async_computation | async-start | bytes 1572864 | tf_op jit(solution)/shard_map/all_gather | solution.py:48
  9.5 4.8 %copy-start.5 = (pred[640,1024]{1,0:T(32,128)(4,1)}, pred[640,1024]{1,0:T(32,128)(4,1)S(1)}, u32[]{:S(2)}) copy-start(pred[640,1024]{1,0:T(32,128)(4,1)S(1)} %iota_compare_fusion) | copy-start | bytes 1966084
  11.2 6.8 %copy-start.10 = (s32[8]{0:T(128)S(1)}, s32[8]{0:T(128)}, u32[]{:S(2)}) copy-start(s32[8]{0:T(128)} %constant.95.clone) | copy-start | bytes 100
  11.2 12.6 %copy-start.7 = (s32[8]{0:T(128)S(1)}, s32[8]{0:T(128)}, u32[]{:S(2)}) copy-start(s32[8]{0:T(128)} %constant.96.clone) | copy-start | bytes 100
  11.2 39.9 %collective-permute-start.8 = (bf16[320,1024]{1,0:T(8,128)(2,1)}, bf16[320,1024]{1,0:T(8,128)(2,1)}, u32[]{:S(2)}, u32[]{:S(2)}) collective-permute-start(bf16[320,1024]{1,0:T(8,128)(2,1)} %convolution_convert_fusion), channel_id=1, source_target_pairs={{2,0},{4,2},{6,4},{7,6},{5,7},{3,5},{1,3},{0,1},{10,8},{12,10},{14... | collective-permute-start | bytes 1966088 | tf_op jit(solution)/shard_map/ppermute | solution.py:71
  14.2 38.9 %collective-permute-start.7 = (bf16[320,1024]{1,0:T(8,128)(2,1)}, bf16[320,1024]{1,0:T(8,128)(2,1)}, u32[]{:S(2)}, u32[]{:S(2)}) collective-permute-start(bf16[320,1024]{1,0:T(8,128)(2,1)} %convolution_convert_fusion), channel_id=1, source_target_pairs={{0,2},{2,4},{4,6},{6,7},{7,5},{5,3},{3,1},{1,0},{8,10},{10,12},{12... | collective-permute-start | bytes 1966088 | tf_op jit(solution)/shard_map/ppermute | solution.py:69
  16.0 37.2 %collective-permute-start.1 = (bf16[320,1024]{1,0:T(8,128)(2,1)}, bf16[320,1024]{1,0:T(8,128)(2,1)}, u32[]{:S(2)}, u32[]{:S(2)}) collective-permute-start(bf16[320,1024]{1,0:T(8,128)(2,1)} %convolution_convert_fusion.1), channel_id=1, source_target_pairs={{2,0},{4,2},{6,4},{7,6},{5,7},{3,5},{1,3},{0,1},{10,8},{12,10},{14... | collective-permute-start | bytes 1966088 | tf_op jit(solution)/shard_map/ppermute | solution.py:71
  17.9 47.6 %collective-permute-start = (bf16[320,1024]{1,0:T(8,128)(2,1)}, bf16[320,1024]{1,0:T(8,128)(2,1)S(1)}, u32[]{:S(2)}, u32[]{:S(2)}) collective-permute-start(bf16[320,1024]{1,0:T(8,128)(2,1)} %convolution_convert_fusion.1), channel_id=1, source_target_pairs={{0,2},{2,4},{4,6},{6,7},{7,5},{5,3},{3,1},{1,0},{8,10},{10,12},{12... | collective-permute-start | bytes 1966088 | tf_op jit(solution)/shard_map/ppermute | solution.py:69
  30.5 5.2 %copy-start.6 = (pred[640,1024]{1,0:T(32,128)(4,1)S(1)}, pred[640,1024]{1,0:T(32,128)(4,1)}, u32[]{:S(2)}) copy-start(pred[640,1024]{1,0:T(32,128)(4,1)} %copy-done.5) | copy-start | bytes 1966084
  30.5 5.2 %copy-start.8 = (bf16[4,256,1792]{2,1,0:T(8,128)(2,1)S(1)}, bf16[4,256,1792]{2,1,0:T(8,128)(2,1)}, u32[]{:S(2)}) copy-start(bf16[4,256,1792]{2,1,0:T(8,128)(2,1)} %param.12) | copy-start | bytes 11010052
  46.0 46.2 %slice-start = ((s8[29360128]{0:T(1024)(128)(4,1)}), s8[4194304]{0:T(1024)(128)(4,1)S(1)}, s32[]{:S(2)}) async-start(s8[29360128]{0:T(1024)(128)(4,1)} %bitcast.74), calls=%async_computation.1 | async-start | bytes 8388608
  51.1 41.1 %slice-start.1 = ((s8[29360128]{0:T(1024)(128)(4,1)}), s8[4194304]{0:T(1024)(128)(4,1)S(1)}, s32[]{:S(2)}) async-start(s8[29360128]{0:T(1024)(128)(4,1)} %bitcast.74), calls=%async_computation.2 | async-start | bytes 8388608
  51.1 24.0 %collective-permute-start.10 = (bf16[320,1024]{1,0:T(8,128)(2,1)}, bf16[320,1024]{1,0:T(8,128)(2,1)}, u32[]{:S(2)}, u32[]{:S(2)}) collective-permute-start(bf16[320,1024]{1,0:T(8,128)(2,1)} %collective-permute-done.8), channel_id=1, source_target_pairs={{2,0},{4,2},{6,4},{7,6},{5,7},{3,5},{1,3},{0,1},{10,8},{12,10},{14... | collective-permute-start | bytes 1966088 | tf_op jit(solution)/shard_map/ppermute | solution.py:71
  53.1 33.7 %collective-permute-start.9 = (bf16[320,1024]{1,0:T(8,128)(2,1)}, bf16[320,1024]{1,0:T(8,128)(2,1)S(1)}, u32[]{:S(2)}, u32[]{:S(2)}) collective-permute-start(bf16[320,1024]{1,0:T(8,128)(2,1)} %collective-permute-done.7), channel_id=1, source_target_pairs={{0,2},{2,4},{4,6},{6,7},{7,5},{5,3},{3,1},{1,0},{8,10},{10,12},{12... | collective-permute-start | bytes 1966088 | tf_op jit(solution)/shard_map/ppermute | solution.py:69
  53.2 29.9 %collective-permute-start.3 = (bf16[320,1024]{1,0:T(8,128)(2,1)}, bf16[320,1024]{1,0:T(8,128)(2,1)S(1)}, u32[]{:S(2)}, u32[]{:S(2)}) collective-permute-start(bf16[320,1024]{1,0:T(8,128)(2,1)} %collective-permute-done.1), channel_id=1, source_target_pairs={{2,0},{4,2},{6,4},{7,6},{5,7},{3,5},{1,3},{0,1},{10,8},{12,10},{14... | collective-permute-start | bytes 1966088 | tf_op jit(solution)/shard_map/ppermute | solution.py:71
  58.0 34.2 %slice-start.2 = ((s8[29360128]{0:T(1024)(128)(4,1)}), s8[4194304]{0:T(1024)(128)(4,1)S(1)}, s32[]{:S(2)}) async-start(s8[29360128]{0:T(1024)(128)(4,1)} %bitcast.74), calls=%async_computation.3 | async-start | bytes 8388608
  61.7 4.5 %copy-start.4 = (f32[320,1792]{1,0:T(8,128)S(1)}, f32[320,1792]{1,0:T(8,128)}, u32[]{:S(2)}) copy-start(f32[320,1792]{1,0:T(8,128)} %fusion.28) | copy-start | bytes 6881284
  61.8 30.5 %slice-start.3 = ((s8[29360128]{0:T(1024)(128)(4,1)}), s8[4194304]{0:T(1024)(128)(4,1)S(1)}, s32[]{:S(2)}) async-start(s8[29360128]{0:T(1024)(128)(4,1)} %bitcast.74), calls=%async_computation.4 | async-start | bytes 8388608
  65.5 29.5 %collective-permute-start.2 = (bf16[320,1024]{1,0:T(8,128)(2,1)S(1)}, bf16[320,1024]{1,0:T(8,128)(2,1)S(1)}, u32[]{:S(2)}, u32[]{:S(2)}) collective-permute-start(bf16[320,1024]{1,0:T(8,128)(2,1)S(1)} %collective-permute-done), channel_id=1, source_target_pairs={{0,2},{2,4},{4,6},{6,7},{7,5},{5,3},{3,1},{1,0},{8,10},{10,12},{12... | collective-permute-start | bytes 1966088 | tf_op jit(solution)/shard_map/ppermute | solution.py:69
  66.2 26.0 %slice-start.4 = ((s8[29360128]{0:T(1024)(128)(4,1)}), s8[4194304]{0:T(1024)(128)(4,1)S(1)}, s32[]{:S(2)}) async-start(s8[29360128]{0:T(1024)(128)(4,1)} %bitcast.74), calls=%async_computation.5 | async-start | bytes 8388608
  70.1 22.2 %slice-start.5 = ((s8[29360128]{0:T(1024)(128)(4,1)}), s8[4194304]{0:T(1024)(128)(4,1)S(1)}, s32[]{:S(2)}) async-start(s8[29360128]{0:T(1024)(128)(4,1)} %bitcast.74), calls=%async_computation.6 | async-start | bytes 8388608
  75.1 28.6 %collective-permute-start.12 = (bf16[320,1024]{1,0:T(8,128)(2,1)}, bf16[320,1024]{1,0:T(8,128)(2,1)}, u32[]{:S(2)}, u32[]{:S(2)}) collective-permute-start(bf16[320,1024]{1,0:T(8,128)(2,1)} %collective-permute-done.10), channel_id=1, source_target_pairs={{2,0},{4,2},{6,4},{7,6},{5,7},{3,5},{1,3},{0,1},{10,8},{12,10},{14... | collective-permute-start | bytes 1966088 | tf_op jit(solution)/shard_map/ppermute | solution.py:71
  83.1 33.4 %collective-permute-start.5 = (bf16[320,1024]{1,0:T(8,128)(2,1)S(1)}, bf16[320,1024]{1,0:T(8,128)(2,1)}, u32[]{:S(2)}, u32[]{:S(2)}) collective-permute-start(bf16[320,1024]{1,0:T(8,128)(2,1)S(1)} %collective-permute-done.3), channel_id=1, source_target_pairs={{2,0},{4,2},{6,4},{7,6},{5,7},{3,5},{1,3},{0,1},{10,8},{12,10},{14... | collective-permute-start | bytes 1966088 | tf_op jit(solution)/shard_map/ppermute | solution.py:71
  86.4 5.8 %slice-start.6 = ((s8[29360128]{0:T(1024)(128)(4,1)}), s8[4194304]{0:T(1024)(128)(4,1)S(1)}, s32[]{:S(2)}) async-start(s8[29360128]{0:T(1024)(128)(4,1)} %bitcast.74), calls=%async_computation.7 | async-start | bytes 8388608
  86.8 37.5 %collective-permute-start.11 = (bf16[320,1024]{1,0:T(8,128)(2,1)S(1)}, bf16[320,1024]{1,0:T(8,128)(2,1)S(1)}, u32[]{:S(2)}, u32[]{:S(2)}) collective-permute-start(bf16[320,1024]{1,0:T(8,128)(2,1)S(1)} %collective-permute-done.9), channel_id=1, source_target_pairs={{0,2},{2,4},{4,6},{6,7},{7,5},{5,3},{3,1},{1,0},{8,10},{10,12},{12... | collective-permute-start | bytes 1966088 | tf_op jit(solution)/shard_map/ppermute | solution.py:69
  95.1 20.0 %collective-permute-start.4 = (bf16[320,1024]{1,0:T(8,128)(2,1)S(1)}, bf16[320,1024]{1,0:T(8,128)(2,1)S(1)}, u32[]{:S(2)}, u32[]{:S(2)}) collective-permute-start(bf16[320,1024]{1,0:T(8,128)(2,1)S(1)} %collective-permute-done.2), channel_id=1, source_target_pairs={{0,2},{2,4},{4,6},{6,7},{7,5},{5,3},{3,1},{1,0},{8,10},{10,12},{12... | collective-permute-start | bytes 1966088 | tf_op jit(solution)/shard_map/ppermute | solution.py:69
  103.7 34.7 %collective-permute-start.13 = (bf16[320,1024]{1,0:T(8,128)(2,1)}, bf16[320,1024]{1,0:T(8,128)(2,1)}, u32[]{:S(2)}, u32[]{:S(2)}) collective-permute-start(bf16[320,1024]{1,0:T(8,128)(2,1)} %collective-permute-done.12), channel_id=1, source_target_pairs={{2,0},{4,2},{6,4},{7,6},{5,7},{3,5},{1,3},{0,1},{10,8},{12,10},{14... | collective-permute-start | bytes 1966088 | tf_op jit(solution)/shard_map/ppermute | solution.py:71
  115.0 17.3 %collective-permute-start.6 = (bf16[320,1024]{1,0:T(8,128)(2,1)S(1)}, bf16[320,1024]{1,0:T(8,128)(2,1)S(1)}, u32[]{:S(2)}, u32[]{:S(2)}) collective-permute-start(bf16[320,1024]{1,0:T(8,128)(2,1)S(1)} %collective-permute-done.4), channel_id=1, source_target_pairs={{0,2},{2,4},{4,6},{6,7},{7,5},{5,3},{3,1},{1,0},{8,10},{10,12},{12... | collective-permute-start | bytes 1966088 | tf_op jit(solution)/shard_map/ppermute | solution.py:69
  138.4 24.5 %copy-start.1 = (bf16[4,256,1024]{2,1,0:T(8,128)(2,1)S(1)}, bf16[4,256,1024]{2,1,0:T(8,128)(2,1)}, u32[]{:S(2)}) copy-start(bf16[4,256,1024]{2,1,0:T(8,128)(2,1)} %param.9) | copy-start | bytes 6291460
  145.9 4.3 %collective-permute-start.14 = (f32[64,256]{1,0:T(8,128)S(1)}, f32[64,256]{1,0:T(8,128)S(1)}, u32[]{:S(2)}, u32[]{:S(2)}) collective-permute-start(f32[64,256]{1,0:T(8,128)S(1)} %convolution_add_fusion.10), channel_id=1, source_target_pairs={{0,1},{1,0},{2,3},{3,2},{4,5},{5,4},{6,7},{7,6},{8,9},{9,8},{10,11... | collective-permute-start | bytes 196616 | tf_op jit(solution)/shard_map/ppermute | solution.py:94
  150.2 4.3 %collective-permute-start.15 = (f32[64,256]{1,0:T(8,128)S(1)}, f32[64,256]{1,0:T(8,128)S(1)}, u32[]{:S(2)}, u32[]{:S(2)}) collective-permute-start(f32[64,256]{1,0:T(8,128)S(1)} %add.338), channel_id=1, source_target_pairs={{0,2},{1,3},{2,0},{3,1},{4,6},{5,7},{6,4},{7,5},{8,10},{9,11},{10,... | collective-permute-start | bytes 196616 | tf_op jit(solution)/shard_map/ppermute | solution.py:94
  154.6 5.3 %collective-permute-start.16 = (f32[64,256]{1,0:T(8,128)S(1)}, f32[64,256]{1,0:T(8,128)S(1)}, u32[]{:S(2)}, u32[]{:S(2)}) collective-permute-start(f32[64,256]{1,0:T(8,128)S(1)} %add.339), channel_id=1, source_target_pairs={{0,4},{1,5},{2,6},{3,7},{4,0},{5,1},{6,2},{7,3},{8,12},{9,13},{10,... | collective-permute-start | bytes 196616 | tf_op jit(solution)/shard_map/ppermute | solution.py:94
  (4 other events, 11.9 us)
Sparse Core Ops, SparseCore 0:
  18.1 10.7 all-gather.1

commit v2 on v0

v2 whole, which is shorter than its diff:
```python
import functools
import math

import jax
import jax.numpy as jnp
from jax import lax
from jax.experimental import pallas as pl
from jax.experimental.pallas import tpu as pltpu
from jax.sharding import PartitionSpec as P

LIVE = 640
VMEM = 48 << 20
NT = (((1,), (1,)), ((), ()))
TN = (((0,), (0,)), ((), ()))


def ring_order(size, folded):
    if folded:
        return list(range(0, size, 2)) + list(range(size - 1, 0, -2))
    return list(range(size))


def dot(a, b):
    return jnp.dot(a, b, preferred_element_type=jnp.float32)


def row_sources(lens, examples, seq_len):
    row = lax.broadcasted_iota(jnp.int32, (LIVE, 1), 0)
    slot, owner, start = row, jnp.zeros_like(row), jnp.int32(0)
    for e in range(1, examples):
        start = start + lens[0, e - 1]
        slot = jnp.where(row >= start, row - start + e * seq_len, slot)
        owner = jnp.where(row >= start, e, owner)
    return slot, owner


def pack_kernel(examples, seq_len, lens, x_ref, out_ref, pick):
    @pl.when(pl.program_id(0) == 0)
    def _():
        slot, _ = row_sources(lens, examples, seq_len)
        columns = lax.broadcasted_iota(jnp.int32, (LIVE, examples * seq_len), 1)
        pick[...] = jnp.where(columns == slot, 1.0, 0.0).astype(pick.dtype)

    out_ref[...] = dot(pick[...], x_ref[...]).astype(out_ref.dtype)


def pack(lengths, rows, examples, seq_len, first, count, tile):
    slots = rows.shape[0]
    return pl.pallas_call(
        functools.partial(pack_kernel, examples, seq_len),
        out_shape=jax.ShapeDtypeStruct((LIVE, count), rows.dtype),
        grid=(count // tile,),
        in_specs=[
            pl.BlockSpec(memory_space=pltpu.SMEM),
            pl.BlockSpec((slots, tile), lambda j: (0, first // tile + j)),
        ],
        out_specs=pl.BlockSpec((LIVE, tile), lambda j: (0, j)),
        scratch_shapes=[pltpu.VMEM((LIVE, slots), rows.dtype)],
        compiler_params=pltpu.CompilerParams(vmem_limit_bytes=VMEM),
        cost_estimate=pl.CostEstimate(
            flops=2 * LIVE * slots * count, bytes_accessed=2 * (slots + LIVE) * count, transcendentals=0
        ),
    )(lengths, rows)


def products(xs, weights, halves):
    total = None
    for k, weight in enumerate(weights):
        part = xs[k * halves].shape[1]
        for h in range(halves):
            term = dot(xs[k * halves + h][...], weight[h * part : (h + 1) * part, :])
            total = term if total is None else total + term
    return total


def projections(xs, projs, halves):
    total = None
    for k, proj in enumerate(projs):
        part = xs[k * halves].shape[1]
        for h in range(halves):
            term = lax.dot_general(
                xs[k * halves + h][...],
                proj[:, h * part : (h + 1) * part],
                NT,
                preferred_element_type=jnp.float32,
            )
            total = term if total is None else total + term
    return total


def absorb_kernel(blocks, halves, first, where, *refs):
    xs, refs = refs[: blocks * halves], refs[blocks * halves :]
    weights, projs, refs = refs[:blocks], refs[blocks : 2 * blocks], refs[2 * blocks :]
    if first:
        gate_out, left_out = refs
    else:
        gate_in, left_in, gate_out, left_out = refs
    gate = products(xs, weights, halves)
    gate_out[...] = gate if first else gate_in[...] + gate

    @pl.when(pl.program_id(0) == 0)
    def _():
        left = projections(xs, projs, halves)
        left_out[...] = left if first else left_in[...] + left


def block_specs(xs, weight, proj_t, steps, halves, tile):
    width = xs[0].shape[1] * halves
    pick_w = [pl.BlockSpec((width, tile), lambda j, w, k=k: (w[k], j)) for k in steps]
    pick_p = [pl.BlockSpec((proj_t.shape[0], width), lambda j, w, k=k: (0, w[k])) for k in steps]
    return [pl.BlockSpec(x.shape, lambda j, w: (0, 0)) for x in xs] + pick_w + pick_p


def absorb(where, xs, weight, proj_t, state, steps, halves, tile):
    hidden, rank = weight.shape[1], proj_t.shape[0]
    depth = xs[0].shape[1] * halves * len(steps)
    blocks = len(steps)
    gate_spec = pl.BlockSpec((LIVE, tile), lambda j, w: (0, j))
    left_spec = pl.BlockSpec((LIVE, rank), lambda j, w: (0, 0))
    specs = block_specs(xs, weight, proj_t, steps, halves, tile)
    args = [where, *xs, *[weight] * blocks, *[proj_t] * blocks]
    aliases = {}
    if state is not None:
        aliases = {len(args): 0, len(args) + 1: 1}
        specs = specs + [gate_spec, left_spec]
        args = args + list(state)
    return pl.pallas_call(
        functools.partial(absorb_kernel, blocks, halves, state is None),
        out_shape=[
            jax.ShapeDtypeStruct((LIVE, hidden), jnp.float32),
            jax.ShapeDtypeStruct((LIVE, rank), jnp.float32),
        ],
        grid_spec=pltpu.PrefetchScalarGridSpec(
            num_scalar_prefetch=1,
            grid=(hidden // tile,),
            in_specs=specs,
            out_specs=[gate_spec, left_spec],
        ),
        input_output_aliases=aliases,
        compiler_params=pltpu.CompilerParams(vmem_limit_bytes=VMEM),
        cost_estimate=pl.CostEstimate(
            flops=2 * LIVE * depth * (hidden + 256),
            bytes_accessed=2 * depth * (hidden + LIVE) + 8 * LIVE * hidden,
            transcendentals=0,
        ),
    )(*args)


def finish_kernel(examples, seq_len, halves, where, lens, *refs):
    xs, refs = refs[:halves], refs[halves:]
    weight, proj, gate_in, left_in, grads, out_t, sketch_out, right = refs
    step = pl.program_id(0)
    gate = gate_in[...] + products(xs, [weight], halves)
    up_grad = (grads[...].astype(jnp.float32) * jax.nn.silu(gate)).astype(jnp.bfloat16)
    term = lax.dot_general(up_grad, out_t[...], NT, preferred_element_type=jnp.float32)

    @pl.when(step == 0)
    def _():
        right[...] = term

    @pl.when(step > 0)
    def _():
        right[...] += term

    @pl.when(step == pl.num_programs(0) - 1)
    def _():
        left = left_in[...] + projections(xs, [proj], halves)
        _, owner = row_sources(lens, examples, seq_len)
        total = right[...]
        weighted = jnp.concatenate([jnp.where(owner == e, total, 0.0) for e in range(examples)], axis=1)
        sketch_out[...] = lax.dot_general(
            left * (1.0 / math.sqrt(seq_len)),
            weighted,
            TN,
            precision=lax.Precision.HIGHEST,
            preferred_element_type=jnp.float32,
        )


def finish(where, lengths, xs, weight, proj_t, state, grads, out_t, steps, halves, tile, examples, seq_len):
    hidden, rank_in, rank_out = weight.shape[1], proj_t.shape[0], out_t.shape[0]
    depth = xs[0].shape[1] * halves
    gate_spec = pl.BlockSpec((LIVE, tile), lambda j, w: (0, j))
    return pl.pallas_call(
        functools.partial(finish_kernel, examples, seq_len, halves),
        out_shape=jax.ShapeDtypeStruct((rank_in, examples * rank_out), jnp.float32),
        grid_spec=pltpu.PrefetchScalarGridSpec(
            num_scalar_prefetch=1,
            grid=(hidden // tile,),
            in_specs=[pl.BlockSpec(memory_space=pltpu.SMEM)]
            + block_specs(xs, weight, proj_t, steps, halves, tile)
            + [
                gate_spec,
                pl.BlockSpec((LIVE, rank_in), lambda j, w: (0, 0)),
                gate_spec,
                pl.BlockSpec((rank_out, tile), lambda j, w: (0, j)),
            ],
            out_specs=pl.BlockSpec((rank_in, examples * rank_out), lambda j, w: (0, 0)),
            scratch_shapes=[pltpu.VMEM((LIVE, rank_out), jnp.float32)],
        ),
        compiler_params=pltpu.CompilerParams(vmem_limit_bytes=VMEM),
        cost_estimate=pl.CostEstimate(
            flops=2 * LIVE * (depth + 256) * (hidden + 256),
            bytes_accessed=2 * depth * (hidden + LIVE) + 6 * LIVE * hidden,
            transcendentals=LIVE * hidden,
        ),
    )(where, lengths, *xs, weight, proj_t, *state, grads, out_t)


def on_device(order, tokens, lengths, gate_weight, hidden_grad, in_proj, out_proj, query_sketch):
    examples, seq_len, width = tokens.shape
    hidden = hidden_grad.shape[2]
    rank_in, rank_out = in_proj.shape[1], out_proj.shape[1]
    size = len(order)
    half = size // 2
    right_way = [(order[i], order[(i + 1) % size]) for i in range(size)]
    left_way = [(d, s) for s, d in right_way]
    table = [[0] * size for _ in range(size)]
    for i, d in enumerate(order):
        table[d] = [order[(i - step) % size] for step in range(size)]
    where = jnp.asarray(table, jnp.int32)[lax.axis_index("fsdp")]
    tile = 256 if hidden % 256 == 0 else hidden
    halves = 2
    part = width // halves

    flat_rows = tokens.reshape(examples * seq_len, width)
    flat_grads = hidden_grad.reshape(examples * seq_len, hidden)
    own = [pack(lengths, flat_rows, examples, seq_len, h * part, part, part) for h in range(halves)]
    proj_t, out_t = in_proj.T, out_proj.T

    going = {"r": list(own), "l": list(own)}
    state = None
    for step in range(1, half + 1):
        arrived = {"r": [None] * halves, "l": [None] * halves}
        for h in range(halves):
            if step < half or h == 0:
                arrived["r"][h] = lax.ppermute(going["r"][h], "fsdp", right_way)
            if step < half or h == 1:
                arrived["l"][h] = lax.ppermute(going["l"][h], "fsdp", left_way)
        if step == 1:
            state = absorb(where, own, gate_weight, proj_t, None, [0], halves, tile)
            grads = pack(lengths, flat_grads, examples, seq_len, 0, hidden, tile)
            other = lax.ppermute(query_sketch, "dp", [(0, 1), (1, 0)])
        else:
            xs = going["r"] + going["l"]
            steps = [step - 1, size - step + 1]
            state = absorb(where, xs, gate_weight, proj_t, state, steps, halves, tile)
        going = arrived
    xs = [going["r"][0], going["l"][1]]
    total = finish(
        where, lengths, xs, gate_weight, proj_t, state, grads, out_t, [half], halves, tile, examples, seq_len
    )
    hop = 1
    while hop < size:
        total = total + lax.ppermute(total, "fsdp", [(i, i ^ hop) for i in range(size)])
        hop *= 2
    sketch = total.reshape(rank_in, examples, rank_out).transpose(1, 0, 2)
    sketch = sketch.reshape(examples, rank_in * rank_out)
    share = sketch.shape[1] // size
    own_cols = lax.dynamic_slice_in_dim(sketch, lax.axis_index("fsdp") * share, share, 1)
    first = lax.axis_index("dp") == 0
    queries = jnp.concatenate(
        [jnp.where(first, query_sketch, other), jnp.where(first, other, query_sketch)], axis=1
    )
    scores = jnp.einsum(
        "ek,qk->eq", sketch.astype(jnp.bfloat16), queries, preferred_element_type=jnp.float32
    )
    return (own_cols, scores)


def solution(mesh):
    order = ring_order(mesh.shape["fsdp"], folded=mesh.shape["parts"] == 2)

    def per_device(*args):
        return on_device(order, *args)

    return jax.shard_map(
        per_device,
        mesh=mesh,
        in_specs=(
            P(("parts", "dp"), None, "fsdp"),
            P(("parts", "dp"), None),
            P(None, "fsdp"),
            P(("parts", "dp"), None, "fsdp"),
            P(),
            P("fsdp", None),
            P("fsdp", "dp"),
        ),
        out_specs=(P(("parts", "dp"), "fsdp"), P(("parts", "dp"), "fsdp")),
        check_vma=False,
    )
```

time: 365 us -> 136 us (0.37)
  waiting for transfers between devices: 291 us -> 41.8 us
  Pallas kernels: 0 us -> 64.9 us
  matrix products: 57 us -> 0.96 us
  starting transfers between devices: 0.12 us -> 21.8 us
  between operations: 15.6 us -> 0.75 us
    all_gather x2 -> x0, waiting for transfers between devices: 233 us -> none  [the longest x1 233 us: on_device(): block_cols = lax.all_gather(flat_rows, 'fsdp', axis=1, tiled=True)]
    pallas_call x0 -> x8, Pallas kernels: none -> 64.9 us  [the longest x4 47.1 us: absorb(): pl.pallas_call(functools.partial(absorb_kernel, blocks, halves, state is...]
    psum x1 -> x0, waiting for transfers between devices: 57.1 us -> none  [on_device(): right_total = lax.psum(right_proj, 'fsdp')]
    dot_general x5 -> x1, matrix products: 57 us -> 0.96 us  [on_device(): jnp.einsum('ek,qk->eq', sketch.astype(jnp.bfloat16), queries, preferred_e...]
    ppermute x0 -> x18, waiting for transfers between devices: none -> 41.8 us  [the longest x7 28.4 us: on_device(): arrived['r'][h] = lax.ppermute(going['r'][h], 'fsdp', right_way)]
    ppermute x0 -> x18, starting transfers between devices: none -> 21.8 us  [the longest x7 15.5 us: on_device(): arrived['r'][h] = lax.ppermute(going['r'][h], 'fsdp', right_way)]
  transfers between devices with their start and end apart: 3 -> 18, of which waited for: 2 -> 13; matrix products, arithmetic and copies ran while one was open for 4% -> 1% of each run, Pallas kernels for 0% -> 47%
where the time goes in v2:
time: 136 us; the launch traced here: 135 us
  Pallas kernels  64.9 us (48%)
  waiting for transfers between devices  41.8 us (31%)
  starting transfers between devices  21.8 us (16%)
  local copies, waits for them, and re-layouts  3.88 us (3%)
    pallas_call x4, Pallas kernels, absorb(): pl.pallas_call(functools.partial(absorb_kernel, blocks, halves, state is...  47.1 us
    ppermute x7, waiting for transfers between devices, on_device(): arrived['r'][h] = lax.ppermute(going['r'][h], 'fsdp', right_way)  28.4 us
    ppermute x7, starting transfers between devices, on_device(): arrived['r'][h] = lax.ppermute(going['r'][h], 'fsdp', right_way)  15.5 us
    pallas_call x1, Pallas kernels, finish(): pl.pallas_call(functools.partial(finish_kernel, examples, seq_len, halves...  10.1 us
    pallas_call x3, Pallas kernels, pack(): pl.pallas_call(functools.partial(pack_kernel, examples, seq_len), out_sha...  7.68 us
    ppermute x7, waiting for transfers between devices, on_device(): arrived['l'][h] = lax.ppermute(going['l'][h], 'fsdp', left_way)  6.71 us
    ppermute x3, waiting for transfers between devices, on_device(): lax.ppermute(total, 'fsdp', [(i, i ^ hop) for i in range(size)])  6.67 us
    ppermute x3, starting transfers between devices, on_device(): lax.ppermute(total, 'fsdp', [(i, i ^ hop) for i in range(size)])  6.11 us
  transfers between devices with their start and end apart: 18, of which 13 were waited for; matrix products, arithmetic and copies ran while one was open for 1% of the time, Pallas kernels for 47%

profile of v2, /device:TPU:0, one launch (start us, length us, event | category | flops | bytes accessed | tf_op | source)
XLA Modules:
  0.0 135.2 jit_solution(16238026043351411893)
XLA Ops:
  0.6 1.7 %copy-done.1 = bf16[4,256,1024]{2,1,0:T(8,128)(2,1)S(1)} copy-done((bf16[4,256,1024]{2,1,0:T(8,128)(2,1)S(1)}, bf16[4,256,1024]{2,1,0:T(8,128)(2,1)}, u32[]{:S(2)}) %copy-start.1) | copy-done | bytes 2097176
  3.0 1.4 %shard_map.95.refs_0_ = bf16[640,512]{1,0:T(8,128)(2,1)S(1)} custom-call(s32[1,4]{1,0:T(1,128)S(1)} %copy-done.3, bf16[1024,1024]{1,0:T(8,128)(2,1)S(1)} %bitcast.15), custom_call_target="tpu_custom_call" | custom-call | flops 671088640 | bytes 1703936 | tf_op jit(solution)/shard_map/pallas_call | solution.py:49
  4.4 3.1 %collective-permute-start = (bf16[640,512]{1,0:T(8,128)(2,1)S(1)}, bf16[640,512]{1,0:T(8,128)(2,1)}, u32[]{:S(2)}, u32[]{:S(2)}) collective-permute-start(bf16[640,512]{1,0:T(8,128)(2,1)S(1)} %shard_map.95.refs_0_), channel_id=1, source_target_pairs={{0,2},{2,4},{4,6},{6,7},{7,5},{5,3},{3,1},{1,0},{8,10},{10,12},{12... | collective-permute-start | bytes 1966088 | tf_op jit(solution)/shard_map/ppermute | solution.py:237
  7.5 1.4 %shard_map.96.refs_1_ = bf16[640,512]{1,0:T(8,128)(2,1)S(1)} custom-call(s32[1,4]{1,0:T(1,128)S(1)} %copy-done.3, bf16[1024,1024]{1,0:T(8,128)(2,1)S(1)} %bitcast.16), custom_call_target="tpu_custom_call" | custom-call | flops 671088640 | bytes 1703936 | tf_op jit(solution)/shard_map/pallas_call | solution.py:49
  8.9 2.0 %collective-permute-start.8 = (bf16[640,512]{1,0:T(8,128)(2,1)S(1)}, bf16[640,512]{1,0:T(8,128)(2,1)}, u32[]{:S(2)}, u32[]{:S(2)}) collective-permute-start(bf16[640,512]{1,0:T(8,128)(2,1)S(1)} %shard_map.96.refs_1_), channel_id=1, source_target_pairs={{0,2},{2,4},{4,6},{6,7},{7,5},{5,3},{3,1},{1,0},{8,10},{10,12},{12... | collective-permute-start | bytes 1966088 | tf_op jit(solution)/shard_map/ppermute | solution.py:237
  11.0 12.1 %collective-permute-done.refs_0_ = bf16[640,512]{1,0:T(8,128)(2,1)} collective-permute-done((bf16[640,512]{1,0:T(8,128)(2,1)S(1)}, bf16[640,512]{1,0:T(8,128)(2,1)}, u32[]{:S(2)}, u32[]{:S(2)}) %collective-permute-start) | collective-permute-done | bytes 655392 | tf_op jit(solution)/shard_map/ppermute | solution.py:237
  23.1 2.1 %collective-permute-start.1 = (bf16[640,512]{1,0:T(8,128)(2,1)}, bf16[640,512]{1,0:T(8,128)(2,1)S(1)}, u32[]{:S(2)}, u32[]{:S(2)}) collective-permute-start(bf16[640,512]{1,0:T(8,128)(2,1)} %collective-permute-done.refs_0_), channel_id=1, source_target_pairs={{0,2},{2,4},{4,6},{6,7},{7,5},{5,3},{3,1},{1,0},{8,10},{10,12},{12... | collective-permute-start | bytes 1966088 | tf_op jit(solution)/shard_map/ppermute | solution.py:237
  25.2 1.5 %collective-permute-done.4.refs_3_ = bf16[640,512]{1,0:T(8,128)(2,1)} collective-permute-done((bf16[640,512]{1,0:T(8,128)(2,1)S(1)}, bf16[640,512]{1,0:T(8,128)(2,1)}, u32[]{:S(2)}, u32[]{:S(2)}) %collective-permute-start.4) | collective-permute-done | bytes 655392 | tf_op jit(solution)/shard_map/ppermute | solution.py:239
  26.7 10.4 %collective-permute-done.8.refs_1_ = bf16[640,512]{1,0:T(8,128)(2,1)} collective-permute-done((bf16[640,512]{1,0:T(8,128)(2,1)S(1)}, bf16[640,512]{1,0:T(8,128)(2,1)}, u32[]{:S(2)}, u32[]{:S(2)}) %collective-permute-start.8) | collective-permute-done | bytes 655392 | tf_op jit(solution)/shard_map/ppermute | solution.py:237
  37.1 2.1 %collective-permute-start.9 = (bf16[640,512]{1,0:T(8,128)(2,1)}, bf16[640,512]{1,0:T(8,128)(2,1)}, u32[]{:S(2)}, u32[]{:S(2)}) collective-permute-start(bf16[640,512]{1,0:T(8,128)(2,1)} %collective-permute-done.8.refs_1_), channel_id=1, source_target_pairs={{0,2},{2,4},{4,6},{6,7},{7,5},{5,3},{3,1},{1,0},{8,10},{10,12},{12... | collective-permute-start | bytes 1966088 | tf_op jit(solution)/shard_map/ppermute | solution.py:237
  39.2 1.5 %collective-permute-done.11.refs_2_ = bf16[640,512]{1,0:T(8,128)(2,1)} collective-permute-done((bf16[640,512]{1,0:T(8,128)(2,1)S(1)}, bf16[640,512]{1,0:T(8,128)(2,1)}, u32[]{:S(2)}, u32[]{:S(2)}) %collective-permute-start.11) | collective-permute-done | bytes 655392 | tf_op jit(solution)/shard_map/ppermute | solution.py:239
  40.8 0.7 dynamic-slice_bitcast_fusion.where
  41.5 9.2 %shard_map.97 = (f32[640,1792]{1,0:T(8,128)}, f32[640,64]{1,0:T(8,128)S(1)}) custom-call(s32[8]{0:T(128)S(1)} %dynamic-slice_bitcast_fusion.where, bf16[640,512]{1,0:T(8,128)(2,1)S(1)} %shard_map.95.refs_0_, bf16[640,512]{1,0:T(8,128)(2,1)S(1)} %shard_map.96.refs_1_, bf16[8192,1792]{1,0:T(8,128)(2,1)} %refs_2_.3, bf16[64,8192]{1,0:T(8,128)(2,1)S(1)} %bitcast.7), custom_call_target="tpu_custom_call" | custom-call | flops 2684354560 | bytes 14155776 | tf_op jit(solution)/shard_map/pallas_call | solution.py:127
  51.1 2.1 %collective-permute-start.2 = (bf16[640,512]{1,0:T(8,128)(2,1)S(1)}, bf16[640,512]{1,0:T(8,128)(2,1)S(1)}, u32[]{:S(2)}, u32[]{:S(2)}) collective-permute-start(bf16[640,512]{1,0:T(8,128)(2,1)S(1)} %collective-permute-done.1.refs_0_), channel_id=1, source_target_pairs={{0,2},{2,4},{4,6},{6,7},{7,5},{5,3},{3,1},{1,0},{8,10},{10,12},{12... | collective-permute-start | bytes 1966088 | tf_op jit(solution)/shard_map/ppermute | solution.py:237
  53.2 1.6 %collective-permute-done.5.refs_3_ = bf16[640,512]{1,0:T(8,128)(2,1)} collective-permute-done((bf16[640,512]{1,0:T(8,128)(2,1)}, bf16[640,512]{1,0:T(8,128)(2,1)}, u32[]{:S(2)}, u32[]{:S(2)}) %collective-permute-start.5) | collective-permute-done | bytes 655392 | tf_op jit(solution)/shard_map/ppermute | solution.py:239
  54.8 4.9 %shard_map.101.refs_6_ = bf16[640,1792]{1,0:T(8,128)(2,1)S(1)} custom-call(s32[1,4]{1,0:T(1,128)S(1)} %copy-done.4, bf16[1024,1792]{1,0:T(8,128)(2,1)S(1)} %bitcast.18), custom_call_target="tpu_custom_call" | custom-call | flops 2348810240 | bytes 5963776 | tf_op jit(solution)/shard_map/pallas_call | solution.py:49
  59.7 5.5 %collective-permute-done.9.refs_1_ = bf16[640,512]{1,0:T(8,128)(2,1)} collective-permute-done((bf16[640,512]{1,0:T(8,128)(2,1)}, bf16[640,512]{1,0:T(8,128)(2,1)}, u32[]{:S(2)}, u32[]{:S(2)}) %collective-permute-start.9) | collective-permute-done | bytes 655392 | tf_op jit(solution)/shard_map/ppermute | solution.py:237
  65.2 2.1 %collective-permute-start.10 = (bf16[640,512]{1,0:T(8,128)(2,1)}, bf16[640,512]{1,0:T(8,128)(2,1)S(1)}, u32[]{:S(2)}, u32[]{:S(2)}) collective-permute-start(bf16[640,512]{1,0:T(8,128)(2,1)} %collective-permute-done.9.refs_1_), channel_id=1, source_target_pairs={{0,2},{2,4},{4,6},{6,7},{7,5},{5,3},{3,1},{1,0},{8,10},{10,12},{12... | collective-permute-start | bytes 1966088 | tf_op jit(solution)/shard_map/ppermute | solution.py:237
  67.3 1.5 %collective-permute-done.12.refs_2_ = bf16[640,512]{1,0:T(8,128)(2,1)} collective-permute-done((bf16[640,512]{1,0:T(8,128)(2,1)}, bf16[640,512]{1,0:T(8,128)(2,1)}, u32[]{:S(2)}, u32[]{:S(2)}) %collective-permute-start.12) | collective-permute-done | bytes 655392 | tf_op jit(solution)/shard_map/ppermute | solution.py:239
  68.8 13.0 %shard_map.98 = (f32[640,1792]{1,0:T(8,128)}, f32[640,64]{1,0:T(8,128)S(1)}) custom-call(s32[8]{0:T(128)S(1)} %dynamic-slice_bitcast_fusion.where, bf16[640,512]{1,0:T(8,128)(2,1)} %collective-permute-done.refs_0_, bf16[640,512]{1,0:T(8,128)(2,1)} %collective-permute-done.8.refs_1_, ...), custom_call_target="tpu_custom_call", output_to_operand_aliasing={{0}: (9, {}), {1}: (10, {})} | custom-call | flops 5368709120 | bytes 19136512 | tf_op jit(solution)/shard_map/pallas_call | solution.py:127
  81.8 2.0 %collective-permute-start.3 = (bf16[640,512]{1,0:T(8,128)(2,1)S(1)}, bf16[640,512]{1,0:T(8,128)(2,1)S(1)}, u32[]{:S(2)}, u32[]{:S(2)}) collective-permute-start(bf16[640,512]{1,0:T(8,128)(2,1)S(1)} %collective-permute-done.2.refs_0_), channel_id=1, source_target_pairs={{0,2},{2,4},{4,6},{6,7},{7,5},{5,3},{3,1},{1,0},{8,10},{10,12},{12... | collective-permute-start | bytes 1966088 | tf_op jit(solution)/shard_map/ppermute | solution.py:237
  83.9 12.8 %shard_map.99 = (f32[640,1792]{1,0:T(8,128)}, f32[640,64]{1,0:T(8,128)S(1)}) custom-call(s32[8]{0:T(128)S(1)} %dynamic-slice_bitcast_fusion.where, bf16[640,512]{1,0:T(8,128)(2,1)S(1)} %collective-permute-done.1.refs_0_, bf16[640,512]{1,0:T(8,128)(2,1)} %collective-permute-done.9.refs_1_, ...), custom_call_target="tpu_custom_call", output_to_operand_aliasing={{0}: (9, {}), {1}: (10, {})} | custom-call | flops 5368709120 | bytes 19136512 | tf_op jit(solution)/shard_map/pallas_call | solution.py:127
  96.8 12.2 %shard_map.100 = (f32[640,1792]{1,0:T(8,128)}, f32[640,64]{1,0:T(8,128)S(1)}) custom-call(s32[8]{0:T(128)S(1)} %dynamic-slice_bitcast_fusion.where, bf16[640,512]{1,0:T(8,128)(2,1)S(1)} %collective-permute-done.2.refs_0_, bf16[640,512]{1,0:T(8,128)(2,1)S(1)} %collective-permute-done.10.refs_1_, ...), custom_call_target="tpu_custom_call", output_to_operand_aliasing={{0}: (9, {}), {1}: (10, {})} | custom-call | flops 5368709120 | bytes 19136512 | tf_op jit(solution)/shard_map/pallas_call | solution.py:127
  109.4 10.1 %shard_map.102 = f32[64,256]{1,0:T(8,128)S(1)} custom-call(s32[8]{0:T(128)S(1)} %dynamic-slice_bitcast_fusion.where, s32[1,4]{1,0:T(1,128)S(1)} %copy-done.4, bf16[640,512]{1,0:T(8,128)(2,1)S(1)} %collective-permute-done.3.refs_0_, bf16[640,512]{1,0:T(8,128)(2,1)S(1)} %collective-permute-done.7.refs_1_, bf16[8192,1792]{1,0:T(8,128)(2,1)} %refs_2_.3, ...), custom_call_target="tpu_custom_call" | custom-call | flops 3355443200 | bytes 11862016 | tf_op jit(solution)/shard_map/pallas_call | solution.py:184
  119.5 1.5 %collective-permute-start.14 = (f32[64,256]{1,0:T(8,128)S(1)}, f32[64,256]{1,0:T(8,128)S(1)}, u32[]{:S(2)}, u32[]{:S(2)}) collective-permute-start(f32[64,256]{1,0:T(8,128)S(1)} %shard_map.102), channel_id=1, source_target_pairs={{0,1},{1,0},{2,3},{3,2},{4,5},{5,4},{6,7},{7,6},{8,9},{9,8},{10,11... | collective-permute-start | bytes 196616 | tf_op jit(solution)/shard_map/ppermute | solution.py:255
  121.0 2.8 %collective-permute-done.14 = f32[64,256]{1,0:T(8,128)S(1)} collective-permute-done((f32[64,256]{1,0:T(8,128)S(1)}, f32[64,256]{1,0:T(8,128)S(1)}, u32[]{:S(2)}, u32[]{:S(2)}) %collective-permute-start.14) | collective-permute-done | bytes 65568 | tf_op jit(solution)/shard_map/ppermute | solution.py:255
  123.8 1.6 %collective-permute-start.15 = (f32[64,256]{1,0:T(8,128)S(1)}, f32[64,256]{1,0:T(8,128)S(1)}, u32[]{:S(2)}, u32[]{:S(2)}) collective-permute-start(f32[64,256]{1,0:T(8,128)S(1)} %add.16), channel_id=1, source_target_pairs={{0,2},{1,3},{2,0},{3,1},{4,6},{5,7},{6,4},{7,5},{8,10},{9,11},{10,... | collective-permute-start | bytes 196616 | tf_op jit(solution)/shard_map/ppermute | solution.py:255
  125.5 2.7 %collective-permute-done.15 = f32[64,256]{1,0:T(8,128)S(1)} collective-permute-done((f32[64,256]{1,0:T(8,128)S(1)}, f32[64,256]{1,0:T(8,128)S(1)}, u32[]{:S(2)}, u32[]{:S(2)}) %collective-permute-start.15) | collective-permute-done | bytes 65568 | tf_op jit(solution)/shard_map/ppermute | solution.py:255
  128.2 3.0 %collective-permute-start.16 = (f32[64,256]{1,0:T(8,128)S(1)}, f32[64,256]{1,0:T(8,128)S(1)}, u32[]{:S(2)}, u32[]{:S(2)}) collective-permute-start(f32[64,256]{1,0:T(8,128)S(1)} %add.17), channel_id=1, source_target_pairs={{0,4},{1,5},{2,6},{3,7},{4,0},{5,1},{6,2},{7,3},{8,12},{9,13},{10,... | collective-permute-start | bytes 196616 | tf_op jit(solution)/shard_map/ppermute | solution.py:255
  131.1 1.1 broadcast_select_fusion.1
  132.2 1.2 collective-permute-done.16
  134.3 1.0 fusion
  (36 shorter events, 2.7 us)
Async XLA Ops:
  0.6 40.8 %copy-start = (bf16[8192,64]{0,1:T(8,128)(2,1)S(1)}, bf16[8192,64]{0,1:T(8,128)(2,1)}, u32[]{:S(2)}) copy-start(bf16[8192,64]{0,1:T(8,128)(2,1)} %param.12) | copy-start | bytes 3145732
  0.6 1.7 %copy-start.1 = (bf16[4,256,1024]{2,1,0:T(8,128)(2,1)S(1)}, bf16[4,256,1024]{2,1,0:T(8,128)(2,1)}, u32[]{:S(2)}) copy-start(bf16[4,256,1024]{2,1,0:T(8,128)(2,1)} %param.8) | copy-start | bytes 6291460
  2.3 0.7 copy-start.3
  3.0 37.8 %copy-start.6 = (bf16[128,2048]{1,0:T(8,128)(2,1)S(1)}, bf16[128,2048]{1,0:T(8,128)(2,1)}, u32[]{:S(2)}) copy-start(bf16[128,2048]{1,0:T(8,128)(2,1)} %param.14) | copy-start | bytes 1572868
  4.4 18.7 %collective-permute-start = (bf16[640,512]{1,0:T(8,128)(2,1)S(1)}, bf16[640,512]{1,0:T(8,128)(2,1)}, u32[]{:S(2)}, u32[]{:S(2)}) collective-permute-start(bf16[640,512]{1,0:T(8,128)(2,1)S(1)} %shard_map.95.refs_0_), channel_id=1, source_target_pairs={{0,2},{2,4},{4,6},{6,7},{7,5},{5,3},{3,1},{1,0},{8,10},{10,12},{12... | collective-permute-start | bytes 1966088 | tf_op jit(solution)/shard_map/ppermute | solution.py:237
  8.9 17.8 %collective-permute-start.4 = (bf16[640,512]{1,0:T(8,128)(2,1)S(1)}, bf16[640,512]{1,0:T(8,128)(2,1)}, u32[]{:S(2)}, u32[]{:S(2)}) collective-permute-start(bf16[640,512]{1,0:T(8,128)(2,1)S(1)} %shard_map.96.refs_1_), channel_id=1, source_target_pairs={{2,0},{4,2},{6,4},{7,6},{5,7},{3,5},{1,3},{0,1},{10,8},{12,10},{14... | collective-permute-start | bytes 1966088 | tf_op jit(solution)/shard_map/ppermute | solution.py:239
  8.9 28.2 %collective-permute-start.8 = (bf16[640,512]{1,0:T(8,128)(2,1)S(1)}, bf16[640,512]{1,0:T(8,128)(2,1)}, u32[]{:S(2)}, u32[]{:S(2)}) collective-permute-start(bf16[640,512]{1,0:T(8,128)(2,1)S(1)} %shard_map.96.refs_1_), channel_id=1, source_target_pairs={{0,2},{2,4},{4,6},{6,7},{7,5},{5,3},{3,1},{1,0},{8,10},{10,12},{12... | collective-permute-start | bytes 1966088 | tf_op jit(solution)/shard_map/ppermute | solution.py:237
  11.0 29.8 %collective-permute-start.11 = (bf16[640,512]{1,0:T(8,128)(2,1)S(1)}, bf16[640,512]{1,0:T(8,128)(2,1)}, u32[]{:S(2)}, u32[]{:S(2)}) collective-permute-start(bf16[640,512]{1,0:T(8,128)(2,1)S(1)} %shard_map.95.refs_0_), channel_id=1, source_target_pairs={{2,0},{4,2},{6,4},{7,6},{5,7},{3,5},{1,3},{0,1},{10,8},{12,10},{14... | collective-permute-start | bytes 1966088 | tf_op jit(solution)/shard_map/ppermute | solution.py:239
  23.1 28.0 %collective-permute-start.1 = (bf16[640,512]{1,0:T(8,128)(2,1)}, bf16[640,512]{1,0:T(8,128)(2,1)S(1)}, u32[]{:S(2)}, u32[]{:S(2)}) collective-permute-start(bf16[640,512]{1,0:T(8,128)(2,1)} %collective-permute-done.refs_0_), channel_id=1, source_target_pairs={{0,2},{2,4},{4,6},{6,7},{7,5},{5,3},{3,1},{1,0},{8,10},{10,12},{12... | collective-permute-start | bytes 1966088 | tf_op jit(solution)/shard_map/ppermute | solution.py:237
  26.7 28.1 %collective-permute-start.5 = (bf16[640,512]{1,0:T(8,128)(2,1)}, bf16[640,512]{1,0:T(8,128)(2,1)}, u32[]{:S(2)}, u32[]{:S(2)}) collective-permute-start(bf16[640,512]{1,0:T(8,128)(2,1)} %collective-permute-done.4.refs_3_), channel_id=1, source_target_pairs={{2,0},{4,2},{6,4},{7,6},{5,7},{3,5},{1,3},{0,1},{10,8},{12,10},{14... | collective-permute-start | bytes 1966088 | tf_op jit(solution)/shard_map/ppermute | solution.py:239
  37.1 28.1 %collective-permute-start.9 = (bf16[640,512]{1,0:T(8,128)(2,1)}, bf16[640,512]{1,0:T(8,128)(2,1)}, u32[]{:S(2)}, u32[]{:S(2)}) collective-permute-start(bf16[640,512]{1,0:T(8,128)(2,1)} %collective-permute-done.8.refs_1_), channel_id=1, source_target_pairs={{0,2},{2,4},{4,6},{6,7},{7,5},{5,3},{3,1},{1,0},{8,10},{10,12},{12... | collective-permute-start | bytes 1966088 | tf_op jit(solution)/shard_map/ppermute | solution.py:237
  40.7 28.1 %collective-permute-start.12 = (bf16[640,512]{1,0:T(8,128)(2,1)}, bf16[640,512]{1,0:T(8,128)(2,1)}, u32[]{:S(2)}, u32[]{:S(2)}) collective-permute-start(bf16[640,512]{1,0:T(8,128)(2,1)} %collective-permute-done.11.refs_2_), channel_id=1, source_target_pairs={{2,0},{4,2},{6,4},{7,6},{5,7},{3,5},{1,3},{0,1},{10,8},{12,10},{14... | collective-permute-start | bytes 1966088 | tf_op jit(solution)/shard_map/ppermute | solution.py:239
  40.7 90.4 %collective-permute-start.17 = (bf16[128,2048]{1,0:T(8,128)(2,1)S(1)}, bf16[128,2048]{1,0:T(8,128)(2,1)}, u32[]{:S(2)}, u32[]{:S(2)}) collective-permute-start(bf16[128,2048]{1,0:T(8,128)(2,1)S(1)} %copy-done.6), channel_id=1, source_target_pairs={{0,8},{8,0},{1,9},{9,1},{2,10},{10,2},{3,11},{11,3},{4,12},{12,4},... | collective-permute-start | bytes 1572872 | tf_op jit(solution)/shard_map/ppermute | solution.py:243
  41.5 13.3 %copy-start.4 = (s32[1,4]{1,0:T(1,128)S(1)}, s32[1,4]{1,0:T(1,128)}, u32[]{:S(2)}) copy-start(s32[1,4]{1,0:T(1,128)} %lens.7) | copy-start | bytes 52
  41.5 13.3 %copy-start.5 = (bf16[4,256,1792]{2,1,0:T(8,128)(2,1)S(1)}, bf16[4,256,1792]{2,1,0:T(8,128)(2,1)}, u32[]{:S(2)}) copy-start(bf16[4,256,1792]{2,1,0:T(8,128)(2,1)} %param.11) | copy-start | bytes 11010052
  51.1 30.8 %collective-permute-start.2 = (bf16[640,512]{1,0:T(8,128)(2,1)S(1)}, bf16[640,512]{1,0:T(8,128)(2,1)S(1)}, u32[]{:S(2)}, u32[]{:S(2)}) collective-permute-start(bf16[640,512]{1,0:T(8,128)(2,1)S(1)} %collective-permute-done.1.refs_0_), channel_id=1, source_target_pairs={{0,2},{2,4},{4,6},{6,7},{7,5},{5,3},{3,1},{1,0},{8,10},{10,12},{12... | collective-permute-start | bytes 1966088 | tf_op jit(solution)/shard_map/ppermute | solution.py:237
  54.8 29.1 %collective-permute-start.6 = (bf16[640,512]{1,0:T(8,128)(2,1)}, bf16[640,512]{1,0:T(8,128)(2,1)S(1)}, u32[]{:S(2)}, u32[]{:S(2)}) collective-permute-start(bf16[640,512]{1,0:T(8,128)(2,1)} %collective-permute-done.5.refs_3_), channel_id=1, source_target_pairs={{2,0},{4,2},{6,4},{7,6},{5,7},{3,5},{1,3},{0,1},{10,8},{12,10},{14... | collective-permute-start | bytes 1966088 | tf_op jit(solution)/shard_map/ppermute | solution.py:239
  65.2 31.4 %collective-permute-start.10 = (bf16[640,512]{1,0:T(8,128)(2,1)}, bf16[640,512]{1,0:T(8,128)(2,1)S(1)}, u32[]{:S(2)}, u32[]{:S(2)}) collective-permute-start(bf16[640,512]{1,0:T(8,128)(2,1)} %collective-permute-done.9.refs_1_), channel_id=1, source_target_pairs={{0,2},{2,4},{4,6},{6,7},{7,5},{5,3},{3,1},{1,0},{8,10},{10,12},{12... | collective-permute-start | bytes 1966088 | tf_op jit(solution)/shard_map/ppermute | solution.py:237
  68.8 28.0 %collective-permute-start.13 = (bf16[640,512]{1,0:T(8,128)(2,1)}, bf16[640,512]{1,0:T(8,128)(2,1)S(1)}, u32[]{:S(2)}, u32[]{:S(2)}) collective-permute-start(bf16[640,512]{1,0:T(8,128)(2,1)} %collective-permute-done.12.refs_2_), channel_id=1, source_target_pairs={{2,0},{4,2},{6,4},{7,6},{5,7},{3,5},{1,3},{0,1},{10,8},{12,10},{14... | collective-permute-start | bytes 1966088 | tf_op jit(solution)/shard_map/ppermute | solution.py:239
  81.8 27.2 %collective-permute-start.3 = (bf16[640,512]{1,0:T(8,128)(2,1)S(1)}, bf16[640,512]{1,0:T(8,128)(2,1)S(1)}, u32[]{:S(2)}, u32[]{:S(2)}) collective-permute-start(bf16[640,512]{1,0:T(8,128)(2,1)S(1)} %collective-permute-done.2.refs_0_), channel_id=1, source_target_pairs={{0,2},{2,4},{4,6},{6,7},{7,5},{5,3},{3,1},{1,0},{8,10},{10,12},{12... | collective-permute-start | bytes 1966088 | tf_op jit(solution)/shard_map/ppermute | solution.py:237
  83.8 25.5 %collective-permute-start.7 = (bf16[640,512]{1,0:T(8,128)(2,1)S(1)}, bf16[640,512]{1,0:T(8,128)(2,1)S(1)}, u32[]{:S(2)}, u32[]{:S(2)}) collective-permute-start(bf16[640,512]{1,0:T(8,128)(2,1)S(1)} %collective-permute-done.6.refs_3_), channel_id=1, source_target_pairs={{2,0},{4,2},{6,4},{7,6},{5,7},{3,5},{1,3},{0,1},{10,8},{12,10},{14... | collective-permute-start | bytes 1966088 | tf_op jit(solution)/shard_map/ppermute | solution.py:239
  96.8 12.6 %copy-start.2 = (bf16[1792,64]{0,1:T(8,128)(2,1)S(1)}, bf16[1792,64]{0,1:T(8,128)(2,1)}, u32[]{:S(2)}) copy-start(bf16[1792,64]{0,1:T(8,128)(2,1)} %param.13) | copy-start | bytes 688132
  119.5 4.3 %collective-permute-start.14 = (f32[64,256]{1,0:T(8,128)S(1)}, f32[64,256]{1,0:T(8,128)S(1)}, u32[]{:S(2)}, u32[]{:S(2)}) collective-permute-start(f32[64,256]{1,0:T(8,128)S(1)} %shard_map.102), channel_id=1, source_target_pairs={{0,1},{1,0},{2,3},{3,2},{4,5},{5,4},{6,7},{7,6},{8,9},{9,8},{10,11... | collective-permute-start | bytes 196616 | tf_op jit(solution)/shard_map/ppermute | solution.py:255
  123.8 4.3 %collective-permute-start.15 = (f32[64,256]{1,0:T(8,128)S(1)}, f32[64,256]{1,0:T(8,128)S(1)}, u32[]{:S(2)}, u32[]{:S(2)}) collective-permute-start(f32[64,256]{1,0:T(8,128)S(1)} %add.16), channel_id=1, source_target_pairs={{0,2},{1,3},{2,0},{3,1},{4,6},{5,7},{6,4},{7,5},{8,10},{9,11},{10,... | collective-permute-start | bytes 196616 | tf_op jit(solution)/shard_map/ppermute | solution.py:255
  128.2 5.2 %collective-permute-start.16 = (f32[64,256]{1,0:T(8,128)S(1)}, f32[64,256]{1,0:T(8,128)S(1)}, u32[]{:S(2)}, u32[]{:S(2)}) collective-permute-start(f32[64,256]{1,0:T(8,128)S(1)} %add.17), channel_id=1, source_target_pairs={{0,4},{1,5},{2,6},{3,7},{4,0},{5,1},{6,2},{7,3},{8,12},{9,13},{10,... | collective-permute-start | bytes 196616 | tf_op jit(solution)/shard_map/ppermute | solution.py:255

commit v3 on v2

v3 whole, which is shorter than its diff:
```python
import functools
import math

import jax
import jax.numpy as jnp
from jax import lax
from jax.experimental import pallas as pl
from jax.experimental.pallas import tpu as pltpu
from jax.sharding import PartitionSpec as P

LIVE = 640
SMALL = 12 << 20
LARGE = 38 << 20
NT = (((1,), (1,)), ((), ()))
TN = (((0,), (0,)), ((), ()))


def ring_order(size, folded):
    if folded:
        return list(range(0, size, 2)) + list(range(size - 1, 0, -2))
    return list(range(size))


def dot(a, b):
    return jnp.dot(a, b, preferred_element_type=jnp.float32)


def row_sources(lens, examples, seq_len):
    row = lax.broadcasted_iota(jnp.int32, (LIVE, 1), 0)
    slot, owner, start = row, jnp.zeros_like(row), jnp.int32(0)
    for e in range(1, examples):
        start = start + lens[0, e - 1]
        slot = jnp.where(row >= start, row - start + e * seq_len, slot)
        owner = jnp.where(row >= start, e, owner)
    return slot, owner


def pack_kernel(examples, seq_len, lens, x_ref, out_ref, pick):
    @pl.when(pl.program_id(0) == 0)
    def _():
        slot, _ = row_sources(lens, examples, seq_len)
        columns = lax.broadcasted_iota(jnp.int32, (LIVE, examples * seq_len), 1)
        pick[...] = jnp.where(columns == slot, 1.0, 0.0).astype(pick.dtype)

    out_ref[...] = dot(pick[...], x_ref[...]).astype(out_ref.dtype)


def pack(lengths, rows, examples, seq_len, first, count, tile):
    slots = rows.shape[0]
    return pl.pallas_call(
        functools.partial(pack_kernel, examples, seq_len),
        out_shape=jax.ShapeDtypeStruct((LIVE, count), rows.dtype),
        grid=(count // tile,),
        in_specs=[
            pl.BlockSpec(memory_space=pltpu.SMEM),
            pl.BlockSpec((slots, tile), lambda j: (0, first // tile + j)),
        ],
        out_specs=pl.BlockSpec((LIVE, tile), lambda j: (0, j)),
        scratch_shapes=[pltpu.VMEM((LIVE, slots), rows.dtype)],
        compiler_params=pltpu.CompilerParams(vmem_limit_bytes=LARGE),
        cost_estimate=pl.CostEstimate(
            flops=2 * LIVE * slots * count, bytes_accessed=2 * (slots + LIVE) * count, transcendentals=0
        ),
    )(lengths, rows)


def project(x, proj_t):
    return lax.dot_general(x, proj_t, NT, preferred_element_type=jnp.float32)


def absorb_kernel(parts, first, final, tile, where, *refs):
    count = len(parts)
    xs, (weight, proj_t), refs = refs[:count], refs[count : count + 2], refs[count + 2 :]
    if not first:
        (gate_in, left_in), refs = refs[:2], refs[2:]
    gate, left, *handed, held, sems = refs
    depth = xs[0].shape[1]

    def start_of(step, h):
        return pl.multiple_of(where[step] * (2 * depth) + h * depth, depth)

    copies = []
    for i, (step, h) in enumerate(parts):
        copies.append(pltpu.make_async_copy(weight.at[pl.ds(start_of(step, h), depth), :], held.at[i], sems.at[i]))
    if handed:
        rows = pl.ds(start_of(final, 0), 2 * depth)
        copies.append(pltpu.make_async_copy(weight.at[rows, :], handed[0], sems.at[count]))
    for copy in copies:
        copy.start()
    total = None if first else left_in[...]
    for x, (step, h) in zip(xs, parts, strict=True):
        term = project(x[...], proj_t[:, pl.ds(start_of(step, h), depth)])
        total = term if total is None else total + term
    left[...] = total
    for copy in copies[:count]:
        copy.wait()

    def one(j, carry):
        columns = pl.ds(pl.multiple_of(j * tile, tile), tile)
        total = None if first else gate_in[:, columns]
        for i, x in enumerate(xs):
            term = dot(x[...], held[i, :, columns])
            total = term if total is None else total + term
        gate[:, columns] = total
        return carry

    lax.fori_loop(0, held.shape[2] // tile, one, 0)
    for copy in copies[count:]:
        copy.wait()


def in_vmem(count):
    return [pl.BlockSpec(memory_space=pltpu.VMEM)] * count


def absorb(where, parts, xs, weight, proj_t, state, tile, final=None):
    hidden, rank = weight.shape[1], proj_t.shape[0]
    args = [where, *xs, weight, proj_t, *(state or ())]
    aliases = {} if state is None else {len(args) - 2: 0, len(args) - 1: 1}
    depth, count = xs[0].shape[1], len(xs)
    handed = [] if final is None else [jax.ShapeDtypeStruct((2 * depth, hidden), weight.dtype)]
    return pl.pallas_call(
        functools.partial(absorb_kernel, parts, state is None, final, tile),
        out_shape=[
            jax.ShapeDtypeStruct((LIVE, hidden), jnp.float32),
            jax.ShapeDtypeStruct((LIVE, rank), jnp.float32),
        ]
        + handed,
        in_specs=[pl.BlockSpec(memory_space=pltpu.SMEM)]
        + in_vmem(count)
        + [pl.BlockSpec(memory_space=pltpu.HBM)]
        + in_vmem(len(args) - 2 - count),
        out_specs=in_vmem(2 + len(handed)),
        input_output_aliases=aliases,
        scratch_shapes=[
            pltpu.VMEM((count, depth, hidden), weight.dtype),
            pltpu.SemaphoreType.DMA((count + 1,)),
        ],
        compiler_params=pltpu.CompilerParams(vmem_limit_bytes=LARGE),
        cost_estimate=pl.CostEstimate(
            flops=2 * LIVE * depth * count * (hidden + 256),
            bytes_accessed=2 * depth * count * (hidden + LIVE) + 8 * LIVE * hidden,
            transcendentals=0,
        ),
    )(*args)


def finish_kernel(examples, seq_len, step, tile, where, lens, *refs):
    xs, refs = refs[:2], refs[2:]
    weight, proj_t, gate_in, left_in, grads, out_t, sketch, block, right = refs
    depth = xs[0].shape[1]
    row = pl.multiple_of(where[step] * (2 * depth), 2 * depth)
    block[:, :depth] = xs[0][...]
    block[:, depth:] = xs[1][...]
    right[...] = jnp.zeros_like(right)

    def one(j, carry):
        columns = pl.ds(pl.multiple_of(j * tile, tile), tile)
        gate = gate_in[:, columns] + dot(block[...], weight[:, columns])
        up_grad = (grads[:, columns].astype(jnp.float32) * jax.nn.silu(gate)).astype(jnp.bfloat16)
        right[...] += project(up_grad, out_t[:, columns])
        return carry

    lax.fori_loop(0, weight.shape[1] // tile, one, 0)
    left = left_in[...] + project(block[...], proj_t[:, pl.ds(row, 2 * depth)])
    _, owner = row_sources(lens, examples, seq_len)
    total = right[...]
    weighted = jnp.concatenate([jnp.where(owner == e, total, 0.0) for e in range(examples)], axis=1)
    sketch[...] = lax.dot_general(
        left * (1.0 / math.sqrt(seq_len)),
        weighted,
        TN,
        precision=lax.Precision.HIGHEST,
        preferred_element_type=jnp.float32,
    )


def finish(where, lengths, xs, weight, proj_t, state, grads, out_t, step, tile, examples, seq_len):
    hidden, rank_in, rank_out = weight.shape[1], proj_t.shape[0], out_t.shape[0]
    depth = xs[0].shape[1] * 2
    return pl.pallas_call(
        functools.partial(finish_kernel, examples, seq_len, step, tile),
        out_shape=jax.ShapeDtypeStruct((rank_in, examples * rank_out), jnp.float32),
        in_specs=[pl.BlockSpec(memory_space=pltpu.SMEM)] * 2 + in_vmem(8),
        out_specs=pl.BlockSpec(memory_space=pltpu.VMEM),
        scratch_shapes=[
            pltpu.VMEM((LIVE, depth), jnp.bfloat16),
            pltpu.VMEM((LIVE, rank_out), jnp.float32),
        ],
        compiler_params=pltpu.CompilerParams(vmem_limit_bytes=SMALL),
        cost_estimate=pl.CostEstimate(
            flops=2 * LIVE * (depth + 256) * (hidden + 256),
            bytes_accessed=2 * depth * (hidden + LIVE) + 6 * LIVE * hidden,
            transcendentals=LIVE * hidden,
        ),
    )(where, lengths, *xs, weight, proj_t, *state, grads, out_t)


def on_device(order, tokens, lengths, gate_weight, hidden_grad, in_proj, out_proj, query_sketch):
    examples, seq_len, width = tokens.shape
    hidden = hidden_grad.shape[2]
    rank_in, rank_out = in_proj.shape[1], out_proj.shape[1]
    size = len(order)
    half = size // 2
    right_way = [(order[i], order[(i + 1) % size]) for i in range(size)]
    left_way = [(d, s) for s, d in right_way]
    table = [[0] * size for _ in range(size)]
    for i, d in enumerate(order):
        table[d] = [order[(i - step) % size] for step in range(size)]
    where = jnp.asarray(table, jnp.int32)[lax.axis_index("fsdp")]
    tile = hidden
    halves = 2
    part = width // halves

    flat_rows = tokens.reshape(examples * seq_len, width)
    flat_grads = hidden_grad.reshape(examples * seq_len, hidden)
    own = [pack(lengths, flat_rows, examples, seq_len, h * part, part, part) for h in range(halves)]
    proj_t, out_t = in_proj.T, out_proj.T

    right, left = list(own), list(own)
    state = None
    for step in range(1, half + 1):
        for h in range(halves):
            if step == 2 and h == 0:
                right[h], left[h], state, grads = lax.optimization_barrier((right[h], left[h], state, grads))
            elif step > 1:
                right[h], left[h], state = lax.optimization_barrier((right[h], left[h], state))
            xs = [right[h], left[h]]
            if step < half or h == 0:
                right[h] = lax.ppermute(right[h], "fsdp", right_way)
            if step < half or h == 1:
                left[h] = lax.ppermute(left[h], "fsdp", left_way)
            if step > 1:
                parts = [(step - 1, h), (size - step + 1, h)]
                final = half if step == half and h == halves - 1 else None
                state = absorb(where, parts, xs, gate_weight, proj_t, state, tile, final)
        if step == 1:
            state = absorb(where, [(0, 0), (0, 1)], own, gate_weight, proj_t, None, tile)
            grads = pack(lengths, flat_grads, examples, seq_len, 0, hidden, tile)
            other = lax.ppermute(query_sketch, "dp", [(0, 1), (1, 0)])
    xs = [right[0], left[1]]
    *state, last_weight = state
    total = finish(
        where, lengths, xs, last_weight, proj_t, state, grads, out_t, half, tile, examples, seq_len
    )
    hop = 1
    while hop < size:
        total = total + lax.ppermute(total, "fsdp", [(i, i ^ hop) for i in range(size)])
        hop *= 2
    sketch = total.reshape(rank_in, examples, rank_out).transpose(1, 0, 2)
    sketch = sketch.reshape(examples, rank_in * rank_out)
    share = sketch.shape[1] // size
    own_cols = lax.dynamic_slice_in_dim(sketch, lax.axis_index("fsdp") * share, share, 1)
    first = lax.axis_index("dp") == 0
    queries = jnp.concatenate(
        [jnp.where(first, query_sketch, other), jnp.where(first, other, query_sketch)], axis=1
    )
    scores = jnp.einsum(
        "ek,qk->eq", sketch.astype(jnp.bfloat16), queries, preferred_element_type=jnp.float32
    )
    return (own_cols, scores)


def solution(mesh):
    order = ring_order(mesh.shape["fsdp"], folded=mesh.shape["parts"] == 2)

    def per_device(*args):
        return on_device(order, *args)

    return jax.shard_map(
        per_device,
        mesh=mesh,
        in_specs=(
            P(("parts", "dp"), None, "fsdp"),
            P(("parts", "dp"), None),
            P(None, "fsdp"),
            P(("parts", "dp"), None, "fsdp"),
            P(),
            P("fsdp", None),
            P("fsdp", "dp"),
        ),
        out_specs=(P(("parts", "dp"), "fsdp"), P(("parts", "dp"), "fsdp")),
        check_vma=False,
    )
```

time: 136 us -> 132 us (0.971)
  Pallas kernels: 64.9 us -> 56.4 us
  waiting for transfers between devices: 41.8 us -> 48.7 us
  starting transfers between devices: 21.8 us -> 19.7 us
    pallas_call x5 -> x8, Pallas kernels: 57.2 us -> 50.4 us  [the longest x7 45.3 us: absorb(): pl.pallas_call(functools.partial(absorb_kernel, parts, state is None, fin...]
    ppermute x3, waiting for transfers between devices: 6.67 us -> 10.8 us  [on_device(): lax.ppermute(total, 'fsdp', [(i, i ^ hop) for i in range(size)])]
    ppermute x14, waiting for transfers between devices: 35.2 us -> 37.9 us  [the longest x7 19.3 us: on_device(): left[h] = lax.ppermute(left[h], 'fsdp', left_way)]
    ppermute x3, starting transfers between devices: 6.11 us -> 4.4 us  [on_device(): lax.ppermute(total, 'fsdp', [(i, i ^ hop) for i in range(size)])]
    pallas_call x3, Pallas kernels: 7.68 us -> 6.02 us  [pack(): pl.pallas_call(functools.partial(pack_kernel, examples, seq_len), out_sha...]
    unnamed x14 -> x18, local copies, waits for them, and re-layouts: 2.35 us -> 3.66 us
  transfers between devices with their start and end apart: 18 -> 18, of which waited for: 13 -> 17; matrix products, arithmetic and copies ran while one was open for 1% -> 1% of each run, Pallas kernels for 47% -> 42%
where the time goes in v3:
time: 132 us
  Pallas kernels  56.4 us (43%)
  waiting for transfers between devices  48.7 us (37%)
  starting transfers between devices  19.7 us (15%)
  local copies, waits for them, and re-layouts  5.19 us (4%)
    pallas_call x7, Pallas kernels, absorb(): pl.pallas_call(functools.partial(absorb_kernel, parts, state is None, fin...  45.3 us
    ppermute x7, waiting for transfers between devices, on_device(): left[h] = lax.ppermute(left[h], 'fsdp', left_way)  19.3 us
    ppermute x7, waiting for transfers between devices, on_device(): right[h] = lax.ppermute(right[h], 'fsdp', right_way)  18.6 us
    ppermute x7, starting transfers between devices, on_device(): right[h] = lax.ppermute(right[h], 'fsdp', right_way)  13 us
    ppermute x3, waiting for transfers between devices, on_device(): lax.ppermute(total, 'fsdp', [(i, i ^ hop) for i in range(size)])  10.8 us
    pallas_call x3, Pallas kernels, pack(): pl.pallas_call(functools.partial(pack_kernel, examples, seq_len), out_sha...  6.02 us
    pallas_call x1, Pallas kernels, finish(): pl.pallas_call(functools.partial(finish_kernel, examples, seq_len, step,...  5.08 us
    ppermute x3, starting transfers between devices, on_device(): lax.ppermute(total, 'fsdp', [(i, i ^ hop) for i in range(size)])  4.4 us
  transfers between devices with their start and end apart: 18, of which 17 were waited for; matrix products, arithmetic and copies ran while one was open for 1% of the time, Pallas kernels for 42%

profile of v3, /device:TPU:0, one launch (start us, length us, event | category | flops | bytes accessed | tf_op | source)
XLA Modules:
  0.0 131.9 jit_solution(8321885782778007918)
XLA Ops:
  0.6 1.6 %copy-done.1 = bf16[4,256,1024]{2,1,0:T(8,128)(2,1)S(1)} copy-done((bf16[4,256,1024]{2,1,0:T(8,128)(2,1)S(1)}, bf16[4,256,1024]{2,1,0:T(8,128)(2,1)}, u32[]{:S(2)}) %copy-start.1) | copy-done | bytes 2097176
  4.3 3.1 %collective-permute-start = (bf16[640,512]{1,0:T(8,128)(2,1)S(1)}, bf16[640,512]{1,0:T(8,128)(2,1)}, u32[]{:S(2)}, u32[]{:S(2)}) collective-permute-start(bf16[640,512]{1,0:T(8,128)(2,1)S(1)} %shard_map.95.refs_0_), channel_id=1, source_target_pairs={{0,2},{2,4},{4,6},{6,7},{7,5},{5,3},{3,1},{1,0},{8,10},{10,12},{12... | collective-permute-start | bytes 1966088 | tf_op jit(solution)/shard_map/ppermute | solution.py:230
  8.8 2.1 %collective-permute-start.4 = (bf16[640,512]{1,0:T(8,128)(2,1)S(1)}, bf16[640,512]{1,0:T(8,128)(2,1)S(1)}, u32[]{:S(2)}, u32[]{:S(2)}) collective-permute-start(bf16[640,512]{1,0:T(8,128)(2,1)S(1)} %shard_map.96.refs_1_), channel_id=1, source_target_pairs={{0,2},{2,4},{4,6},{6,7},{7,5},{5,3},{3,1},{1,0},{8,10},{10,12},{12... | collective-permute-start | bytes 1966088 | tf_op jit(solution)/shard_map/ppermute | solution.py:230
  10.9 3.2 %shard_map.98.refs_6_ = bf16[640,1792]{1,0:T(8,128)(2,1)S(1)} custom-call(s32[1,4]{1,0:T(1,128)S(1)} %copy-done.5, bf16[1024,1792]{1,0:T(8,128)(2,1)S(1)} %bitcast.18), custom_call_target="tpu_custom_call" | custom-call | flops 2348810240 | bytes 5963776 | tf_op jit(solution)/shard_map/pallas_call | solution.py:50
  16.2 5.6 %shard_map.97 = (f32[640,1792]{1,0:T(8,128)S(1)}, f32[640,64]{1,0:T(8,128)S(1)}) custom-call(s32[8]{0:T(128)S(1)} %dynamic-slice_bitcast_fusion.where, bf16[640,512]{1,0:T(8,128)(2,1)S(1)} %shard_map.95.refs_0_, bf16[640,512]{1,0:T(8,128)(2,1)S(1)} %shard_map.96.refs_1_, bf16[8192,1792]{1,0:T(8,128)(2,1)} %refs_2_.13, bf16[64,8192]{1,0:T(8,128)(2,1)S(1)} %bitcast.7), custom_call_target="tpu_custom_call" | custom-call | flops 2684354560 | bytes 14155776 | tf_op jit(solution)/shard_map/pallas_call | solution.py:122
  23.0 2.2 %collective-permute-done.1.refs_1_ = bf16[640,512]{1,0:T(8,128)(2,1)} collective-permute-done((bf16[640,512]{1,0:T(8,128)(2,1)S(1)}, bf16[640,512]{1,0:T(8,128)(2,1)}, u32[]{:S(2)}, u32[]{:S(2)}) %collective-permute-start.1) | collective-permute-done | bytes 655392 | tf_op jit(solution)/shard_map/ppermute | solution.py:232
  25.1 1.6 %collective-permute-start.2 = (bf16[640,512]{1,0:T(8,128)(2,1)}, bf16[640,512]{1,0:T(8,128)(2,1)S(1)}, u32[]{:S(2)}, u32[]{:S(2)}) collective-permute-start(bf16[640,512]{1,0:T(8,128)(2,1)} %collective-permute-done.refs_0_), channel_id=1, source_target_pairs={{0,2},{2,4},{4,6},{6,7},{7,5},{5,3},{3,1},{1,0},{8,10},{10,12},{12... | collective-permute-start | bytes 1966088 | tf_op jit(solution)/shard_map/ppermute | solution.py:230
  27.2 7.0 %shard_map.99 = (f32[640,1792]{1,0:T(8,128)S(1)}, f32[640,64]{1,0:T(8,128)S(1)}) custom-call(s32[8]{0:T(128)S(1)} %dynamic-slice_bitcast_fusion.where, bf16[640,512]{1,0:T(8,128)(2,1)} %collective-permute-done.refs_0_, bf16[640,512]{1,0:T(8,128)(2,1)} %collective-permute-done.1.refs_1_, ...), custom_call_target="tpu_custom_call", output_to_operand_aliasing={{0}: (5, {}), {1}: (6, {})} | custom-call | flops 2684354560 | bytes 14155776 | tf_op jit(solution)/shard_map/pallas_call | solution.py:122
  34.2 2.7 %collective-permute-done.4.refs_0_ = bf16[640,512]{1,0:T(8,128)(2,1)S(1)} collective-permute-done((bf16[640,512]{1,0:T(8,128)(2,1)S(1)}, bf16[640,512]{1,0:T(8,128)(2,1)S(1)}, u32[]{:S(2)}, u32[]{:S(2)}) %collective-permute-start.4) | collective-permute-done | bytes 655392 | tf_op jit(solution)/shard_map/ppermute | solution.py:230
  36.9 2.3 %collective-permute-done.5.refs_1_ = bf16[640,512]{1,0:T(8,128)(2,1)} collective-permute-done((bf16[640,512]{1,0:T(8,128)(2,1)S(1)}, bf16[640,512]{1,0:T(8,128)(2,1)}, u32[]{:S(2)}, u32[]{:S(2)}) %collective-permute-start.5) | collective-permute-done | bytes 655392 | tf_op jit(solution)/shard_map/ppermute | solution.py:232
  39.2 1.6 %collective-permute-start.8 = (bf16[640,512]{1,0:T(8,128)(2,1)S(1)}, bf16[640,512]{1,0:T(8,128)(2,1)S(1)}, u32[]{:S(2)}, u32[]{:S(2)}) collective-permute-start(bf16[640,512]{1,0:T(8,128)(2,1)S(1)} %collective-permute-done.4.refs_0_), channel_id=1, source_target_pairs={{0,2},{2,4},{4,6},{6,7},{7,5},{5,3},{3,1},{1,0},{8,10},{10,12},{12... | collective-permute-start | bytes 1966088 | tf_op jit(solution)/shard_map/ppermute | solution.py:230
  41.2 6.8 %shard_map.100 = (f32[640,1792]{1,0:T(8,128)S(1)}, f32[640,64]{1,0:T(8,128)S(1)}) custom-call(s32[8]{0:T(128)S(1)} %dynamic-slice_bitcast_fusion.where, bf16[640,512]{1,0:T(8,128)(2,1)S(1)} %collective-permute-done.4.refs_0_, bf16[640,512]{1,0:T(8,128)(2,1)} %collective-permute-done.5.refs_1_, ...), custom_call_target="tpu_custom_call", output_to_operand_aliasing={{0}: (5, {}), {1}: (6, {})} | custom-call | flops 2684354560 | bytes 14155776 | tf_op jit(solution)/shard_map/pallas_call | solution.py:122
  48.0 2.9 %collective-permute-done.2.refs_0_ = bf16[640,512]{1,0:T(8,128)(2,1)S(1)} collective-permute-done((bf16[640,512]{1,0:T(8,128)(2,1)}, bf16[640,512]{1,0:T(8,128)(2,1)S(1)}, u32[]{:S(2)}, u32[]{:S(2)}) %collective-permute-start.2) | collective-permute-done | bytes 655392 | tf_op jit(solution)/shard_map/ppermute | solution.py:230
  51.0 2.2 %collective-permute-done.3.refs_1_ = bf16[640,512]{1,0:T(8,128)(2,1)S(1)} collective-permute-done((bf16[640,512]{1,0:T(8,128)(2,1)}, bf16[640,512]{1,0:T(8,128)(2,1)S(1)}, u32[]{:S(2)}, u32[]{:S(2)}) %collective-permute-start.3) | collective-permute-done | bytes 655392 | tf_op jit(solution)/shard_map/ppermute | solution.py:232
  53.1 1.6 %collective-permute-start.6 = (bf16[640,512]{1,0:T(8,128)(2,1)S(1)}, bf16[640,512]{1,0:T(8,128)(2,1)S(1)}, u32[]{:S(2)}, u32[]{:S(2)}) collective-permute-start(bf16[640,512]{1,0:T(8,128)(2,1)S(1)} %collective-permute-done.2.refs_0_), channel_id=1, source_target_pairs={{0,2},{2,4},{4,6},{6,7},{7,5},{5,3},{3,1},{1,0},{8,10},{10,12},{12... | collective-permute-start | bytes 1966088 | tf_op jit(solution)/shard_map/ppermute | solution.py:230
  55.1 6.5 %shard_map.101 = (f32[640,1792]{1,0:T(8,128)S(1)}, f32[640,64]{1,0:T(8,128)S(1)}) custom-call(s32[8]{0:T(128)S(1)} %dynamic-slice_bitcast_fusion.where, bf16[640,512]{1,0:T(8,128)(2,1)S(1)} %collective-permute-done.2.refs_0_, bf16[640,512]{1,0:T(8,128)(2,1)S(1)} %collective-permute-done.3.refs_1_, ...), custom_call_target="tpu_custom_call", output_to_operand_aliasing={{0}: (5, {}), {1}: (6, {})} | custom-call | flops 2684354560 | bytes 14155776 | tf_op jit(solution)/shard_map/pallas_call | solution.py:122
  61.7 3.3 %collective-permute-done.8.refs_0_ = bf16[640,512]{1,0:T(8,128)(2,1)S(1)} collective-permute-done((bf16[640,512]{1,0:T(8,128)(2,1)S(1)}, bf16[640,512]{1,0:T(8,128)(2,1)S(1)}, u32[]{:S(2)}, u32[]{:S(2)}) %collective-permute-start.8) | collective-permute-done | bytes 655392 | tf_op jit(solution)/shard_map/ppermute | solution.py:230
  65.0 2.2 %collective-permute-done.9.refs_1_ = bf16[640,512]{1,0:T(8,128)(2,1)S(1)} collective-permute-done((bf16[640,512]{1,0:T(8,128)(2,1)}, bf16[640,512]{1,0:T(8,128)(2,1)S(1)}, u32[]{:S(2)}, u32[]{:S(2)}) %collective-permute-start.9) | collective-permute-done | bytes 655392 | tf_op jit(solution)/shard_map/ppermute | solution.py:232
  67.2 1.6 %collective-permute-start.11 = (bf16[640,512]{1,0:T(8,128)(2,1)S(1)}, bf16[640,512]{1,0:T(8,128)(2,1)S(1)}, u32[]{:S(2)}, u32[]{:S(2)}) collective-permute-start(bf16[640,512]{1,0:T(8,128)(2,1)S(1)} %collective-permute-done.8.refs_0_), channel_id=1, source_target_pairs={{0,2},{2,4},{4,6},{6,7},{7,5},{5,3},{3,1},{1,0},{8,10},{10,12},{12... | collective-permute-start | bytes 1966088 | tf_op jit(solution)/shard_map/ppermute | solution.py:230
  69.2 6.5 %shard_map.102 = (f32[640,1792]{1,0:T(8,128)S(1)}, f32[640,64]{1,0:T(8,128)S(1)}) custom-call(s32[8]{0:T(128)S(1)} %dynamic-slice_bitcast_fusion.where, bf16[640,512]{1,0:T(8,128)(2,1)S(1)} %collective-permute-done.8.refs_0_, bf16[640,512]{1,0:T(8,128)(2,1)S(1)} %collective-permute-done.9.refs_1_, ...), custom_call_target="tpu_custom_call", output_to_operand_aliasing={{0}: (5, {}), {1}: (6, {})} | custom-call | flops 2684354560 | bytes 14155776 | tf_op jit(solution)/shard_map/pallas_call | solution.py:122
  75.7 3.3 %collective-permute-done.6.refs_0_ = bf16[640,512]{1,0:T(8,128)(2,1)S(1)} collective-permute-done((bf16[640,512]{1,0:T(8,128)(2,1)S(1)}, bf16[640,512]{1,0:T(8,128)(2,1)S(1)}, u32[]{:S(2)}, u32[]{:S(2)}) %collective-permute-start.6) | collective-permute-done | bytes 655392 | tf_op jit(solution)/shard_map/ppermute | solution.py:230
  79.0 2.2 %collective-permute-done.7.refs_1_ = bf16[640,512]{1,0:T(8,128)(2,1)S(1)} collective-permute-done((bf16[640,512]{1,0:T(8,128)(2,1)S(1)}, bf16[640,512]{1,0:T(8,128)(2,1)S(1)}, u32[]{:S(2)}, u32[]{:S(2)}) %collective-permute-start.7) | collective-permute-done | bytes 655392 | tf_op jit(solution)/shard_map/ppermute | solution.py:232
  81.2 6.5 %shard_map.103 = (f32[640,1792]{1,0:T(8,128)S(1)}, f32[640,64]{1,0:T(8,128)S(1)}) custom-call(s32[8]{0:T(128)S(1)} %dynamic-slice_bitcast_fusion.where, bf16[640,512]{1,0:T(8,128)(2,1)S(1)} %collective-permute-done.6.refs_0_, bf16[640,512]{1,0:T(8,128)(2,1)S(1)} %collective-permute-done.7.refs_1_, ...), custom_call_target="tpu_custom_call", output_to_operand_aliasing={{0}: (5, {}), {1}: (6, {})} | custom-call | flops 2684354560 | bytes 14155776 | tf_op jit(solution)/shard_map/pallas_call | solution.py:122
  87.8 4.5 %collective-permute-done.11.refs_0_ = bf16[640,512]{1,0:T(8,128)(2,1)S(1)} collective-permute-done((bf16[640,512]{1,0:T(8,128)(2,1)S(1)}, bf16[640,512]{1,0:T(8,128)(2,1)S(1)}, u32[]{:S(2)}, u32[]{:S(2)}) %collective-permute-start.11) | collective-permute-done | bytes 655392 | tf_op jit(solution)/shard_map/ppermute | solution.py:230
  95.8 6.3 %shard_map.104 = (f32[640,1792]{1,0:T(8,128)S(1)}, f32[640,64]{1,0:T(8,128)S(1)}, bf16[1024,1792]{1,0:T(8,128)(2,1)S(1)}) custom-call(s32[8]{0:T(128)S(1)} %dynamic-slice_bitcast_fusion.where, bf16[640,512]{1,0:T(8,128)(2,1)S(1)} %collective-permute-done.11.refs_0_, ...), custom_call_target="tpu_custom_call", output_to_operand_aliasing={{0}: (5, {}), {1}: (6, {})} | custom-call | flops 2684354560 | bytes 14155776 | tf_op jit(solution)/shard_map/pallas_call | solution.py:122
  102.1 6.9 %collective-permute-done.13.refs_1_ = bf16[640,512]{1,0:T(8,128)(2,1)S(1)} collective-permute-done((bf16[640,512]{1,0:T(8,128)(2,1)S(1)}, bf16[640,512]{1,0:T(8,128)(2,1)S(1)}, u32[]{:S(2)}, u32[]{:S(2)}) %collective-permute-start.13) | collective-permute-done | bytes 655392 | tf_op jit(solution)/shard_map/ppermute | solution.py:232
  109.6 5.1 %shard_map.105 = f32[64,256]{1,0:T(8,128)S(1)} custom-call(s32[8]{0:T(128)S(1)} %dynamic-slice_bitcast_fusion.where, s32[1,4]{1,0:T(1,128)S(1)} %copy-done.6, bf16[640,512]{1,0:T(8,128)(2,1)S(1)} %collective-permute-done.10.refs_0_, bf16[640,512]{1,0:T(8,128)(2,1)S(1)} %collective-permute-done.13.refs_1_, bf16[1024,1792]{1,0:T(8,128)(2,1)S(1)} %get-tuple-element.78.refs_2_, ...), custom_call_target="tpu_custom_call" | custom-call | flops 3355443200 | bytes 11862016 | tf_op jit(solution)/shard_map/pallas_call | solution.py:181
  114.7 1.6 %collective-permute-start.14 = (f32[64,256]{1,0:T(8,128)S(1)}, f32[64,256]{1,0:T(8,128)S(1)}, u32[]{:S(2)}, u32[]{:S(2)}) collective-permute-start(f32[64,256]{1,0:T(8,128)S(1)} %shard_map.105), channel_id=1, source_target_pairs={{0,1},{1,0},{2,3},{3,2},{4,5},{5,4},{6,7},{7,6},{8,9},{9,8},{10,11... | collective-permute-start | bytes 196616 | tf_op jit(solution)/shard_map/ppermute | solution.py:248
  116.4 2.7 %collective-permute-done.14 = f32[64,256]{1,0:T(8,128)S(1)} collective-permute-done((f32[64,256]{1,0:T(8,128)S(1)}, f32[64,256]{1,0:T(8,128)S(1)}, u32[]{:S(2)}, u32[]{:S(2)}) %collective-permute-start.14) | collective-permute-done | bytes 65568 | tf_op jit(solution)/shard_map/ppermute | solution.py:248
  120.3 3.8 %collective-permute-done.15 = f32[64,256]{1,0:T(8,128)S(1)} collective-permute-done((f32[64,256]{1,0:T(8,128)S(1)}, f32[64,256]{1,0:T(8,128)S(1)}, u32[]{:S(2)}, u32[]{:S(2)}) %collective-permute-start.15) | collective-permute-done | bytes 65568 | tf_op jit(solution)/shard_map/ppermute | solution.py:248
  124.1 1.5 %collective-permute-start.16 = (f32[64,256]{1,0:T(8,128)S(1)}, f32[64,256]{1,0:T(8,128)S(1)}, u32[]{:S(2)}, u32[]{:S(2)}) collective-permute-start(f32[64,256]{1,0:T(8,128)S(1)} %add.17), channel_id=1, source_target_pairs={{0,4},{1,5},{2,6},{3,7},{4,0},{5,1},{6,2},{7,3},{8,12},{9,13},{10,... | collective-permute-start | bytes 196616 | tf_op jit(solution)/shard_map/ppermute | solution.py:248
  125.8 4.3 %collective-permute-done.16 = f32[64,256]{1,0:T(8,128)S(1)} collective-permute-done((f32[64,256]{1,0:T(8,128)S(1)}, f32[64,256]{1,0:T(8,128)S(1)}, u32[]{:S(2)}, u32[]{:S(2)}) %collective-permute-start.16) | collective-permute-done | bytes 65568 | tf_op jit(solution)/shard_map/ppermute | solution.py:248
  (43 shorter events, 15.8 us)
Async XLA Ops:
  0.6 1.6 %copy-start.1 = (bf16[4,256,1024]{2,1,0:T(8,128)(2,1)S(1)}, bf16[4,256,1024]{2,1,0:T(8,128)(2,1)}, u32[]{:S(2)}) copy-start(bf16[4,256,1024]{2,1,0:T(8,128)(2,1)} %param.8) | copy-start | bytes 6291460
  2.2 0.7 copy-start.5
  2.9 8.0 %copy-start.7 = (bf16[4,256,1792]{2,1,0:T(8,128)(2,1)S(1)}, bf16[4,256,1792]{2,1,0:T(8,128)(2,1)}, u32[]{:S(2)}) copy-start(bf16[4,256,1792]{2,1,0:T(8,128)(2,1)} %param.11) | copy-start | bytes 11010052
  4.3 18.7 %collective-permute-start = (bf16[640,512]{1,0:T(8,128)(2,1)S(1)}, bf16[640,512]{1,0:T(8,128)(2,1)}, u32[]{:S(2)}, u32[]{:S(2)}) collective-permute-start(bf16[640,512]{1,0:T(8,128)(2,1)S(1)} %shard_map.95.refs_0_), channel_id=1, source_target_pairs={{0,2},{2,4},{4,6},{6,7},{7,5},{5,3},{3,1},{1,0},{8,10},{10,12},{12... | collective-permute-start | bytes 1966088 | tf_op jit(solution)/shard_map/ppermute | solution.py:230
  7.4 17.8 %collective-permute-start.1 = (bf16[640,512]{1,0:T(8,128)(2,1)S(1)}, bf16[640,512]{1,0:T(8,128)(2,1)}, u32[]{:S(2)}, u32[]{:S(2)}) collective-permute-start(bf16[640,512]{1,0:T(8,128)(2,1)S(1)} %shard_map.95.refs_0_), channel_id=1, source_target_pairs={{2,0},{4,2},{6,4},{7,6},{5,7},{3,5},{1,3},{0,1},{10,8},{12,10},{14... | collective-permute-start | bytes 1966088 | tf_op jit(solution)/shard_map/ppermute | solution.py:232
  8.8 7.4 %copy-start = (bf16[8192,64]{0,1:T(8,128)(2,1)S(1)}, bf16[8192,64]{0,1:T(8,128)(2,1)}, u32[]{:S(2)}) copy-start(bf16[8192,64]{0,1:T(8,128)(2,1)} %param.12) | copy-start | bytes 3145732
  8.8 28.1 %collective-permute-start.4 = (bf16[640,512]{1,0:T(8,128)(2,1)S(1)}, bf16[640,512]{1,0:T(8,128)(2,1)S(1)}, u32[]{:S(2)}, u32[]{:S(2)}) collective-permute-start(bf16[640,512]{1,0:T(8,128)(2,1)S(1)} %shard_map.96.refs_1_), channel_id=1, source_target_pairs={{0,2},{2,4},{4,6},{6,7},{7,5},{5,3},{3,1},{1,0},{8,10},{10,12},{12... | collective-permute-start | bytes 1966088 | tf_op jit(solution)/shard_map/ppermute | solution.py:230
  10.9 28.3 %collective-permute-start.5 = (bf16[640,512]{1,0:T(8,128)(2,1)S(1)}, bf16[640,512]{1,0:T(8,128)(2,1)}, u32[]{:S(2)}, u32[]{:S(2)}) collective-permute-start(bf16[640,512]{1,0:T(8,128)(2,1)S(1)} %shard_map.96.refs_1_), channel_id=1, source_target_pairs={{2,0},{4,2},{6,4},{7,6},{5,7},{3,5},{1,3},{0,1},{10,8},{12,10},{14... | collective-permute-start | bytes 1966088 | tf_op jit(solution)/shard_map/ppermute | solution.py:232
  14.1 1.4 %copy-start.2 = (bf16[640,1792]{1,0:T(8,128)(2,1)}, bf16[640,1792]{1,0:T(8,128)(2,1)S(1)}, u32[]{:S(2)}) copy-start(bf16[640,1792]{1,0:T(8,128)(2,1)S(1)} %shard_map.98.refs_6_) | copy-start | bytes 6881284
  25.1 25.8 %collective-permute-start.2 = (bf16[640,512]{1,0:T(8,128)(2,1)}, bf16[640,512]{1,0:T(8,128)(2,1)S(1)}, u32[]{:S(2)}, u32[]{:S(2)}) collective-permute-start(bf16[640,512]{1,0:T(8,128)(2,1)} %collective-permute-done.refs_0_), channel_id=1, source_target_pairs={{0,2},{2,4},{4,6},{6,7},{7,5},{5,3},{3,1},{1,0},{8,10},{10,12},{12... | collective-permute-start | bytes 1966088 | tf_op jit(solution)/shard_map/ppermute | solution.py:230
  26.7 26.4 %collective-permute-start.3 = (bf16[640,512]{1,0:T(8,128)(2,1)}, bf16[640,512]{1,0:T(8,128)(2,1)S(1)}, u32[]{:S(2)}, u32[]{:S(2)}) collective-permute-start(bf16[640,512]{1,0:T(8,128)(2,1)} %collective-permute-done.1.refs_1_), channel_id=1, source_target_pairs={{2,0},{4,2},{6,4},{7,6},{5,7},{3,5},{1,3},{0,1},{10,8},{12,10},{14... | collective-permute-start | bytes 1966088 | tf_op jit(solution)/shard_map/ppermute | solution.py:232
  39.2 25.8 %collective-permute-start.8 = (bf16[640,512]{1,0:T(8,128)(2,1)S(1)}, bf16[640,512]{1,0:T(8,128)(2,1)S(1)}, u32[]{:S(2)}, u32[]{:S(2)}) collective-permute-start(bf16[640,512]{1,0:T(8,128)(2,1)S(1)} %collective-permute-done.4.refs_0_), channel_id=1, source_target_pairs={{0,2},{2,4},{4,6},{6,7},{7,5},{5,3},{3,1},{1,0},{8,10},{10,12},{12... | collective-permute-start | bytes 1966088 | tf_op jit(solution)/shard_map/ppermute | solution.py:230
  40.8 26.4 %collective-permute-start.9 = (bf16[640,512]{1,0:T(8,128)(2,1)}, bf16[640,512]{1,0:T(8,128)(2,1)S(1)}, u32[]{:S(2)}, u32[]{:S(2)}) collective-permute-start(bf16[640,512]{1,0:T(8,128)(2,1)} %collective-permute-done.5.refs_1_), channel_id=1, source_target_pairs={{2,0},{4,2},{6,4},{7,6},{5,7},{3,5},{1,3},{0,1},{10,8},{12,10},{14... | collective-permute-start | bytes 1966088 | tf_op jit(solution)/shard_map/ppermute | solution.py:232
  53.1 25.9 %collective-permute-start.6 = (bf16[640,512]{1,0:T(8,128)(2,1)S(1)}, bf16[640,512]{1,0:T(8,128)(2,1)S(1)}, u32[]{:S(2)}, u32[]{:S(2)}) collective-permute-start(bf16[640,512]{1,0:T(8,128)(2,1)S(1)} %collective-permute-done.2.refs_0_), channel_id=1, source_target_pairs={{0,2},{2,4},{4,6},{6,7},{7,5},{5,3},{3,1},{1,0},{8,10},{10,12},{12... | collective-permute-start | bytes 1966088 | tf_op jit(solution)/shard_map/ppermute | solution.py:230
  54.7 26.5 %collective-permute-start.7 = (bf16[640,512]{1,0:T(8,128)(2,1)S(1)}, bf16[640,512]{1,0:T(8,128)(2,1)S(1)}, u32[]{:S(2)}, u32[]{:S(2)}) collective-permute-start(bf16[640,512]{1,0:T(8,128)(2,1)S(1)} %collective-permute-done.3.refs_1_), channel_id=1, source_target_pairs={{2,0},{4,2},{6,4},{7,6},{5,7},{3,5},{1,3},{0,1},{10,8},{12,10},{14... | collective-permute-start | bytes 1966088 | tf_op jit(solution)/shard_map/ppermute | solution.py:232
  67.2 25.1 %collective-permute-start.11 = (bf16[640,512]{1,0:T(8,128)(2,1)S(1)}, bf16[640,512]{1,0:T(8,128)(2,1)S(1)}, u32[]{:S(2)}, u32[]{:S(2)}) collective-permute-start(bf16[640,512]{1,0:T(8,128)(2,1)S(1)} %collective-permute-done.8.refs_0_), channel_id=1, source_target_pairs={{0,2},{2,4},{4,6},{6,7},{7,5},{5,3},{3,1},{1,0},{8,10},{10,12},{12... | collective-permute-start | bytes 1966088 | tf_op jit(solution)/shard_map/ppermute | solution.py:230
  68.7 25.0 %collective-permute-start.12 = (bf16[640,512]{1,0:T(8,128)(2,1)S(1)}, bf16[640,512]{1,0:T(8,128)(2,1)S(1)}, u32[]{:S(2)}, u32[]{:S(2)}) collective-permute-start(bf16[640,512]{1,0:T(8,128)(2,1)S(1)} %collective-permute-done.9.refs_1_), channel_id=1, source_target_pairs={{2,0},{4,2},{6,4},{7,6},{5,7},{3,5},{1,3},{0,1},{10,8},{12,10},{14... | collective-permute-start | bytes 1966088 | tf_op jit(solution)/shard_map/ppermute | solution.py:232
  81.2 14.6 %copy-start.8 = (bf16[128,2048]{1,0:T(8,128)(2,1)S(1)}, bf16[128,2048]{1,0:T(8,128)(2,1)}, u32[]{:S(2)}) copy-start(bf16[128,2048]{1,0:T(8,128)(2,1)} %param.14) | copy-start | bytes 1572868
  93.8 15.9 %copy-start.3 = (bf16[640,1792]{1,0:T(8,128)(2,1)S(1)}, bf16[640,1792]{1,0:T(8,128)(2,1)}, u32[]{:S(2)}) copy-start(bf16[640,1792]{1,0:T(8,128)(2,1)} %copy-done.2) | copy-start | bytes 6881284
  93.8 15.9 %copy-start.4 = (bf16[1792,64]{0,1:T(8,128)(2,1)S(1)}, bf16[1792,64]{0,1:T(8,128)(2,1)}, u32[]{:S(2)}) copy-start(bf16[1792,64]{0,1:T(8,128)(2,1)} %param.13) | copy-start | bytes 688132
  93.8 15.9 %copy-start.6 = (s32[1,4]{1,0:T(1,128)S(1)}, s32[1,4]{1,0:T(1,128)}, u32[]{:S(2)}) copy-start(s32[1,4]{1,0:T(1,128)} %lens.7) | copy-start | bytes 52
  93.8 15.3 %collective-permute-start.13 = (bf16[640,512]{1,0:T(8,128)(2,1)S(1)}, bf16[640,512]{1,0:T(8,128)(2,1)S(1)}, u32[]{:S(2)}, u32[]{:S(2)}) collective-permute-start(bf16[640,512]{1,0:T(8,128)(2,1)S(1)} %collective-permute-done.12.refs_1_), channel_id=1, source_target_pairs={{2,0},{4,2},{6,4},{7,6},{5,7},{3,5},{1,3},{0,1},{10,8},{12,10},{14... | collective-permute-start | bytes 1966088 | tf_op jit(solution)/shard_map/ppermute | solution.py:232
  94.3 15.3 %collective-permute-start.10 = (bf16[640,512]{1,0:T(8,128)(2,1)S(1)}, bf16[640,512]{1,0:T(8,128)(2,1)S(1)}, u32[]{:S(2)}, u32[]{:S(2)}) collective-permute-start(bf16[640,512]{1,0:T(8,128)(2,1)S(1)} %collective-permute-done.6.refs_0_), channel_id=1, source_target_pairs={{0,2},{2,4},{4,6},{6,7},{7,5},{5,3},{3,1},{1,0},{8,10},{10,12},{12... | collective-permute-start | bytes 1966088 | tf_op jit(solution)/shard_map/ppermute | solution.py:230
  95.8 29.9 %collective-permute-start.17 = (bf16[128,2048]{1,0:T(8,128)(2,1)S(1)}, bf16[128,2048]{1,0:T(8,128)(2,1)S(1)}, u32[]{:S(2)}, u32[]{:S(2)}) collective-permute-start(bf16[128,2048]{1,0:T(8,128)(2,1)S(1)} %copy-done.8), channel_id=1, source_target_pairs={{0,8},{8,0},{1,9},{9,1},{2,10},{10,2},{3,11},{11,3},{4,12},{12,4},... | collective-permute-start | bytes 1572872 | tf_op jit(solution)/shard_map/ppermute | solution.py:240
  114.7 4.3 %collective-permute-start.14 = (f32[64,256]{1,0:T(8,128)S(1)}, f32[64,256]{1,0:T(8,128)S(1)}, u32[]{:S(2)}, u32[]{:S(2)}) collective-permute-start(f32[64,256]{1,0:T(8,128)S(1)} %shard_map.105), channel_id=1, source_target_pairs={{0,1},{1,0},{2,3},{3,2},{4,5},{5,4},{6,7},{7,6},{8,9},{9,8},{10,11... | collective-permute-start | bytes 196616 | tf_op jit(solution)/shard_map/ppermute | solution.py:248
  119.1 5.0 %collective-permute-start.15 = (f32[64,256]{1,0:T(8,128)S(1)}, f32[64,256]{1,0:T(8,128)S(1)}, u32[]{:S(2)}, u32[]{:S(2)}) collective-permute-start(f32[64,256]{1,0:T(8,128)S(1)} %add.16), channel_id=1, source_target_pairs={{0,2},{1,3},{2,0},{3,1},{4,6},{5,7},{6,4},{7,5},{8,10},{9,11},{10,... | collective-permute-start | bytes 196616 | tf_op jit(solution)/shard_map/ppermute | solution.py:248
  124.1 5.9 %collective-permute-start.16 = (f32[64,256]{1,0:T(8,128)S(1)}, f32[64,256]{1,0:T(8,128)S(1)}, u32[]{:S(2)}, u32[]{:S(2)}) collective-permute-start(f32[64,256]{1,0:T(8,128)S(1)} %add.17), channel_id=1, source_target_pairs={{0,4},{1,5},{2,6},{3,7},{4,0},{5,1},{6,2},{7,3},{8,12},{9,13},{10,... | collective-permute-start | bytes 196616 | tf_op jit(solution)/shard_map/ppermute | solution.py:248

commit v4 on v3

--- a/solution.py
+++ b/solution.py
@@ -9,6 +9,8 @@
 from jax.sharding import PartitionSpec as P
 
 LIVE = 640
+CUT = 384
+WHOLE = 60 << 20
 SMALL = 12 << 20
 LARGE = 38 << 20
 NT = (((1,), (1,)), ((), ()))
@@ -19,6 +21,14 @@
     if folded:
         return list(range(0, size, 2)) + list(range(size - 1, 0, -2))
     return list(range(size))
+
+
+def reduce_hops(size):
+    rounds, hop = [], 1
+    while hop < size:
+        rounds.append((hop, 2 * hop, 3 * hop) if 2 * hop < size else (hop,))
+        hop *= 4
+    return rounds
 
 
 def dot(a, b):
@@ -66,6 +76,52 @@
 
 def project(x, proj_t):
     return lax.dot_general(x, proj_t, NT, preferred_element_type=jnp.float32)
+
+
+def open_kernel(examples, seq_len, reach, lens_in, x_in, *refs):
+    outs, (lens, x, pick, sem) = refs[:-4], refs[-4:]
+    count = len(outs)
+    slots, width = x.shape
+    depth, rows = width // count, LIVE // 2
+    lens_copy = pltpu.make_async_copy(lens_in, lens, sem.at[count])
+    lens_copy.start()
+    loads = []
+    for h in range(count):
+        columns = slice(h * depth, (h + 1) * depth)
+        loads.append(pltpu.make_async_copy(x_in.at[:, columns], x.at[:, columns], sem.at[h]))
+        loads[h].start()
+    lens_copy.wait()
+    slot, _ = row_sources(lens, examples, seq_len)
+    for m in range(2):
+        columns = lax.broadcasted_iota(jnp.int32, (rows, reach), 1) + m * (slots - reach)
+        pick[m] = jnp.where(columns == slot[m * rows : (m + 1) * rows], 1.0, 0.0).astype(pick.dtype)
+    for h, out in enumerate(outs):
+        loads[h].wait()
+        for m in range(2):
+            first = m * (slots - reach)
+            part = dot(pick[m], x[first : first + reach, h * depth : (h + 1) * depth])
+            out[m * rows : (m + 1) * rows, :] = part.astype(out.dtype)
+
+
+def open_pack(lengths, rows, examples, seq_len, halves):
+    slots, width = rows.shape
+    reach = -(-(slots - LIVE // 2) // 128) * 128
+    return pl.pallas_call(
+        functools.partial(open_kernel, examples, seq_len, reach),
+        out_shape=[jax.ShapeDtypeStruct((LIVE, width // halves), rows.dtype)] * halves,
+        in_specs=[pl.BlockSpec(memory_space=pl.ANY)] * 2,
+        out_specs=[pl.BlockSpec(memory_space=pltpu.VMEM)] * halves,
+        scratch_shapes=[
+            pltpu.SMEM(lengths.shape, lengths.dtype),
+            pltpu.VMEM(rows.shape, rows.dtype),
+            pltpu.VMEM((2, LIVE // 2, reach), rows.dtype),
+            pltpu.SemaphoreType.DMA((halves + 1,)),
+        ],
+        compiler_params=pltpu.CompilerParams(vmem_limit_bytes=WHOLE),
+        cost_estimate=pl.CostEstimate(
+            flops=2 * LIVE * slots * width, bytes_accessed=2 * (slots + LIVE) * width, transcendentals=0
+        ),
+    )(lengths, rows)
 
 
 def absorb_kernel(parts, first, final, tile, where, *refs):
@@ -145,55 +201,48 @@
     )(*args)
 
 
-def finish_kernel(examples, seq_len, step, tile, where, lens, *refs):
+def finish_kernel(examples, seq_len, step, first, where, lens, *refs):
     xs, refs = refs[:2], refs[2:]
-    weight, proj_t, gate_in, left_in, grads, out_t, sketch, block, right = refs
-    depth = xs[0].shape[1]
+    weight, proj_t, gate_in, left_in, grads, out_t, *before, sketch, block = refs
+    count, depth = xs[0].shape
+    rows = slice(first, first + count)
     row = pl.multiple_of(where[step] * (2 * depth), 2 * depth)
     block[:, :depth] = xs[0][...]
     block[:, depth:] = xs[1][...]
-    right[...] = jnp.zeros_like(right)
-
-    def one(j, carry):
-        columns = pl.ds(pl.multiple_of(j * tile, tile), tile)
-        gate = gate_in[:, columns] + dot(block[...], weight[:, columns])
-        up_grad = (grads[:, columns].astype(jnp.float32) * jax.nn.silu(gate)).astype(jnp.bfloat16)
-        right[...] += project(up_grad, out_t[:, columns])
-        return carry
-
-    lax.fori_loop(0, weight.shape[1] // tile, one, 0)
-    left = left_in[...] + project(block[...], proj_t[:, pl.ds(row, 2 * depth)])
+    gate = gate_in[rows, :] + dot(block[...], weight[...])
+    up_grad = (grads[rows, :].astype(jnp.float32) * jax.nn.silu(gate)).astype(jnp.bfloat16)
+    right = project(up_grad, out_t[...])
+    left = left_in[rows, :] + project(block[...], proj_t[:, pl.ds(row, 2 * depth)])
     _, owner = row_sources(lens, examples, seq_len)
-    total = right[...]
-    weighted = jnp.concatenate([jnp.where(owner == e, total, 0.0) for e in range(examples)], axis=1)
-    sketch[...] = lax.dot_general(
+    owner = owner[rows, :]
+    weighted = jnp.concatenate([jnp.where(owner == e, right, 0.0) for e in range(examples)], axis=1)
+    term = lax.dot_general(
         left * (1.0 / math.sqrt(seq_len)),
         weighted,
         TN,
         precision=lax.Precision.HIGHEST,
         preferred_element_type=jnp.float32,
     )
-
-
-def finish(where, lengths, xs, weight, proj_t, state, grads, out_t, step, tile, examples, seq_len):
+    sketch[...] = before[0][...] + term if before else term
+
+
+def finish(where, lengths, xs, weight, proj_t, state, grads, out_t, before, step, first, examples, seq_len):
     hidden, rank_in, rank_out = weight.shape[1], proj_t.shape[0], out_t.shape[0]
-    depth = xs[0].shape[1] * 2
+    count, depth = xs[0].shape[0], xs[0].shape[1] * 2
+    args = [*xs, weight, proj_t, *state, grads, out_t, *([] if before is None else [before])]
     return pl.pallas_call(
-        functools.partial(finish_kernel, examples, seq_len, step, tile),
+        functools.partial(finish_kernel, examples, seq_len, step, first),
         out_shape=jax.ShapeDtypeStruct((rank_in, examples * rank_out), jnp.float32),
-        in_specs=[pl.BlockSpec(memory_space=pltpu.SMEM)] * 2 + in_vmem(8),
+        in_specs=[pl.BlockSpec(memory_space=pltpu.SMEM)] * 2 + in_vmem(len(args)),
         out_specs=pl.BlockSpec(memory_space=pltpu.VMEM),
-        scratch_shapes=[
-            pltpu.VMEM((LIVE, depth), jnp.bfloat16),
-            pltpu.VMEM((LIVE, rank_out), jnp.float32),
-        ],
+        scratch_shapes=[pltpu.VMEM((count, depth), jnp.bfloat16)],
         compiler_params=pltpu.CompilerParams(vmem_limit_bytes=SMALL),
         cost_estimate=pl.CostEstimate(
-            flops=2 * LIVE * (depth + 256) * (hidden + 256),
-            bytes_accessed=2 * depth * (hidden + LIVE) + 6 * LIVE * hidden,
-            transcendentals=LIVE * hidden,
-        ),
-    )(where, lengths, *xs, weight, proj_t, *state, grads, out_t)
+            flops=2 * count * (depth + 256) * (hidden + 256),
+            bytes_accessed=2 * depth * (hidden + count) + 6 * count * hidden,
+            transcendentals=count * hidden,
+        ),
+    )(where, lengths, *args)
 
 
 def on_device(order, tokens, lengths, gate_weight, hidden_grad, in_proj, out_proj, query_sketch):
@@ -210,43 +259,51 @@
     where = jnp.asarray(table, jnp.int32)[lax.axis_index("fsdp")]
     tile = hidden
     halves = 2
-    part = width // halves
 
     flat_rows = tokens.reshape(examples * seq_len, width)
     flat_grads = hidden_grad.reshape(examples * seq_len, hidden)
-    own = [pack(lengths, flat_rows, examples, seq_len, h * part, part, part) for h in range(halves)]
+    own = open_pack(lengths, flat_rows, examples, seq_len, halves)
     proj_t, out_t = in_proj.T, out_proj.T
 
     right, left = list(own), list(own)
     state = None
-    for step in range(1, half + 1):
+    for step in range(1, half):
         for h in range(halves):
+            o = 1 - h
             if step == 2 and h == 0:
-                right[h], left[h], state, grads = lax.optimization_barrier((right[h], left[h], state, grads))
+                right[h], left[o], state, grads = lax.optimization_barrier((right[h], left[o], state, grads))
             elif step > 1:
-                right[h], left[h], state = lax.optimization_barrier((right[h], left[h], state))
-            xs = [right[h], left[h]]
-            if step < half or h == 0:
-                right[h] = lax.ppermute(right[h], "fsdp", right_way)
-            if step < half or h == 1:
-                left[h] = lax.ppermute(left[h], "fsdp", left_way)
+                right[h], left[o], state = lax.optimization_barrier((right[h], left[o], state))
+            xs = [right[h], left[o]]
+            right[h] = lax.ppermute(right[h], "fsdp", right_way)
+            left[o] = lax.ppermute(left[o], "fsdp", left_way)
             if step > 1:
-                parts = [(step - 1, h), (size - step + 1, h)]
-                final = half if step == half and h == halves - 1 else None
-                state = absorb(where, parts, xs, gate_weight, proj_t, state, tile, final)
+                parts = [(step - 1, h), (size - step + 1, o)]
+                state = absorb(where, parts, xs, gate_weight, proj_t, state, tile)
         if step == 1:
             state = absorb(where, [(0, 0), (0, 1)], own, gate_weight, proj_t, None, tile)
             grads = pack(lengths, flat_grads, examples, seq_len, 0, hidden, tile)
             other = lax.ppermute(query_sketch, "dp", [(0, 1), (1, 0)])
-    xs = [right[0], left[1]]
+    right[0], left[1], state = lax.optimization_barrier((right[0], left[1], state))
+    cuts = [(0, CUT), (CUT, LIVE)]
+    last = [
+        [lax.ppermute(right[0][a:b], "fsdp", right_way), lax.ppermute(left[1][a:b], "fsdp", left_way)]
+        for a, b in cuts
+    ]
+    for h in range(halves):
+        parts = [(half - 1, h), (size - half + 1, 1 - h)]
+        final = half if h == halves - 1 else None
+        state = absorb(where, parts, [right[h], left[1 - h]], gate_weight, proj_t, state, tile, final)
     *state, last_weight = state
-    total = finish(
-        where, lengths, xs, last_weight, proj_t, state, grads, out_t, half, tile, examples, seq_len
-    )
-    hop = 1
-    while hop < size:
-        total = total + lax.ppermute(total, "fsdp", [(i, i ^ hop) for i in range(size)])
-        hop *= 2
+    total = None
+    for xs, (a, _) in zip(last, cuts, strict=True):
+        total = finish(
+            where, lengths, xs, last_weight, proj_t, state, grads, out_t, total, half, a, examples, seq_len
+        )
+    for hops in reduce_hops(size):
+        low = total.astype(jnp.bfloat16)
+        for hop in hops:
+            total = total + lax.ppermute(low, "fsdp", [(i, i ^ hop) for i in range(size)]).astype(jnp.float32)
     sketch = total.reshape(rank_in, examples, rank_out).transpose(1, 0, 2)
     sketch = sketch.reshape(examples, rank_in * rank_out)
     share = sketch.shape[1] // size

time: 132 us -> 125 us (0.947)
  waiting for transfers between devices: 48.7 us -> 33.3 us
  starting transfers between devices: 19.7 us -> 23.9 us
  Pallas kernels: 56.4 us -> 58.2 us
    ppermute x10 -> x14, waiting for transfers between devices: 30.1 us -> 18 us  [the longest x6 10.8 us: on_device(): left[o] = lax.ppermute(left[o], 'fsdp', left_way)]
    ppermute x10 -> x14, starting transfers between devices: 6.71 us -> 12.5 us  [the longest x4 6.44 us: on_device(): lax.ppermute(low, 'fsdp', [(i, i ^ hop) for i in range(size)])]
    pallas_call x0 -> x1, Pallas kernels: none -> 3.48 us  [open_pack(): pl.pallas_call(functools.partial(open_kernel, examples, seq_len, reach),...]
    ppermute x7 -> x6, waiting for transfers between devices: 18.6 us -> 15.3 us  [on_device(): right[h] = lax.ppermute(right[h], 'fsdp', right_way)]
    pallas_call x3 -> x1, Pallas kernels: 6.02 us -> 3.2 us  [pack(): pl.pallas_call(functools.partial(pack_kernel, examples, seq_len), out_sha...]
    ppermute x7 -> x6, starting transfers between devices: 13 us -> 11.4 us  [on_device(): right[h] = lax.ppermute(right[h], 'fsdp', right_way)]
    pallas_call x1 -> x2, Pallas kernels: 5.08 us -> 5.94 us  [finish(): pl.pallas_call(functools.partial(finish_kernel, examples, seq_len, step,...]
    unnamed x18 -> x12, local copies, waits for them, and re-layouts: 3.66 us -> 4.23 us
  transfers between devices with their start and end apart: 18 -> 21, of which waited for: 17 -> 17; matrix products, arithmetic and copies ran while one was open for 1% -> 2% of each run, Pallas kernels for 42% -> 44%
where the time goes in v4:
time: 125 us; the launch traced here: 124 us
  Pallas kernels  58.2 us (47%)
  waiting for transfers between devices  33.3 us (27%)
  starting transfers between devices  23.9 us (19%)
  local copies, waits for them, and re-layouts  5.85 us (5%)
  other arithmetic  1.32 us (1%)
    pallas_call x7, Pallas kernels, absorb(): pl.pallas_call(functools.partial(absorb_kernel, parts, state is None, fin...  45.6 us
    ppermute x6, waiting for transfers between devices, on_device(): right[h] = lax.ppermute(right[h], 'fsdp', right_way)  15.3 us
    ppermute x6, starting transfers between devices, on_device(): right[h] = lax.ppermute(right[h], 'fsdp', right_way)  11.4 us
    ppermute x6, waiting for transfers between devices, on_device(): left[o] = lax.ppermute(left[o], 'fsdp', left_way)  10.8 us
    ppermute x4, starting transfers between devices, on_device(): lax.ppermute(low, 'fsdp', [(i, i ^ hop) for i in range(size)])  6.44 us
    pallas_call x2, Pallas kernels, finish(): pl.pallas_call(functools.partial(finish_kernel, examples, seq_len, step,...  5.94 us
    ppermute x4, waiting for transfers between devices, on_device(): lax.ppermute(low, 'fsdp', [(i, i ^ hop) for i in range(size)])  4.31 us
    unnamed x12, local copies, waits for them, and re-layouts  4.23 us
  transfers between devices with their start and end apart: 21, of which 17 were waited for; matrix products, arithmetic and copies ran while one was open for 2% of the time, Pallas kernels for 44%

profile of v4, /device:TPU:0, one launch (start us, length us, event | category | flops | bytes accessed | tf_op | source)
XLA Modules:
  0.0 124.4 jit_solution(9222880333379010279)
XLA Ops:
  0.6 3.5 %shard_map.95 = (bf16[640,512]{1,0:T(8,128)(2,1)}, bf16[640,512]{1,0:T(8,128)(2,1)}) custom-call(s32[1,4]{1,0:T(1,128)} %lens.5, bf16[1024,1024]{1,0:T(8,128)(2,1)} %bitcast.20), custom_call_target="tpu_custom_call" | custom-call | flops 1342177280 | bytes 3407872 | tf_op jit(solution)/shard_map/pallas_call | solution.py:109
  4.1 3.1 %collective-permute-start = (bf16[640,512]{1,0:T(8,128)(2,1)}, bf16[640,512]{1,0:T(8,128)(2,1)}, u32[]{:S(2)}, u32[]{:S(2)}) collective-permute-start(bf16[640,512]{1,0:T(8,128)(2,1)} %get-tuple-element.40.refs_0_), channel_id=1, source_target_pairs={{0,2},{2,4},{4,6},{6,7},{7,5},{5,3},{3,1},{1,0},{8,10},{10,12},{12... | collective-permute-start | bytes 1966088 | tf_op jit(solution)/shard_map/ppermute | solution.py:278
  7.2 2.0 %collective-permute-start.4 = (bf16[640,512]{1,0:T(8,128)(2,1)}, bf16[640,512]{1,0:T(8,128)(2,1)}, u32[]{:S(2)}, u32[]{:S(2)}) collective-permute-start(bf16[640,512]{1,0:T(8,128)(2,1)} %get-tuple-element.41.refs_1_), channel_id=1, source_target_pairs={{0,2},{2,4},{4,6},{6,7},{7,5},{5,3},{3,1},{1,0},{8,10},{10,12},{12... | collective-permute-start | bytes 1966088 | tf_op jit(solution)/shard_map/ppermute | solution.py:278
  9.3 2.0 %copy-done.5 = bf16[4,256,1792]{2,1,0:T(8,128)(2,1)S(1)} copy-done((bf16[4,256,1792]{2,1,0:T(8,128)(2,1)S(1)}, bf16[4,256,1792]{2,1,0:T(8,128)(2,1)}, u32[]{:S(2)}) %copy-start.5) | copy-done | bytes 3670040
  11.3 3.2 %shard_map.97.refs_6_ = bf16[640,1792]{1,0:T(8,128)(2,1)S(1)} custom-call(s32[1,4]{1,0:T(1,128)S(1)} %copy-done.4, bf16[1024,1792]{1,0:T(8,128)(2,1)S(1)} %bitcast.18), custom_call_target="tpu_custom_call" | custom-call | flops 2348810240 | bytes 5963776 | tf_op jit(solution)/shard_map/pallas_call | solution.py:60
  17.4 5.6 %shard_map.96 = (f32[640,1792]{1,0:T(8,128)S(1)}, f32[640,64]{1,0:T(8,128)S(1)}) custom-call(s32[8]{0:T(128)S(1)} %dynamic-slice_bitcast_fusion.where, bf16[640,512]{1,0:T(8,128)(2,1)S(1)} %copy-done.2, bf16[640,512]{1,0:T(8,128)(2,1)S(1)} %copy-done.3, bf16[8192,1792]{1,0:T(8,128)(2,1)} %refs_2_.13, bf16[64,8192]{1,0:T(8,128)(2,1)S(1)} %bitcast.7), custom_call_target="tpu_custom_call" | custom-call | flops 2684354560 | bytes 14155776 | tf_op jit(solution)/shard_map/pallas_call | solution.py:178
  23.0 2.2 %collective-permute-done.1.refs_1_ = bf16[640,512]{1,0:T(8,128)(2,1)} collective-permute-done((bf16[640,512]{1,0:T(8,128)(2,1)}, bf16[640,512]{1,0:T(8,128)(2,1)}, u32[]{:S(2)}, u32[]{:S(2)}) %collective-permute-start.1) | collective-permute-done | bytes 655392 | tf_op jit(solution)/shard_map/ppermute | solution.py:279
  25.2 1.6 %collective-permute-start.2 = (bf16[640,512]{1,0:T(8,128)(2,1)}, bf16[640,512]{1,0:T(8,128)(2,1)S(1)}, u32[]{:S(2)}, u32[]{:S(2)}) collective-permute-start(bf16[640,512]{1,0:T(8,128)(2,1)} %collective-permute-done.refs_0_), channel_id=1, source_target_pairs={{0,2},{2,4},{4,6},{6,7},{7,5},{5,3},{3,1},{1,0},{8,10},{10,12},{12... | collective-permute-start | bytes 1966088 | tf_op jit(solution)/shard_map/ppermute | solution.py:278
  27.2 7.0 %shard_map.98 = (f32[640,1792]{1,0:T(8,128)S(1)}, f32[640,64]{1,0:T(8,128)S(1)}) custom-call(s32[8]{0:T(128)S(1)} %dynamic-slice_bitcast_fusion.where, bf16[640,512]{1,0:T(8,128)(2,1)} %collective-permute-done.refs_0_, bf16[640,512]{1,0:T(8,128)(2,1)} %collective-permute-done.1.refs_1_, ...), custom_call_target="tpu_custom_call", output_to_operand_aliasing={{0}: (5, {}), {1}: (6, {})} | custom-call | flops 2684354560 | bytes 14155776 | tf_op jit(solution)/shard_map/pallas_call | solution.py:178
  34.3 2.8 %collective-permute-done.4.refs_0_ = bf16[640,512]{1,0:T(8,128)(2,1)} collective-permute-done((bf16[640,512]{1,0:T(8,128)(2,1)}, bf16[640,512]{1,0:T(8,128)(2,1)}, u32[]{:S(2)}, u32[]{:S(2)}) %collective-permute-start.4) | collective-permute-done | bytes 655392 | tf_op jit(solution)/shard_map/ppermute | solution.py:278
  37.1 2.2 %collective-permute-done.5.refs_1_ = bf16[640,512]{1,0:T(8,128)(2,1)} collective-permute-done((bf16[640,512]{1,0:T(8,128)(2,1)}, bf16[640,512]{1,0:T(8,128)(2,1)}, u32[]{:S(2)}, u32[]{:S(2)}) %collective-permute-start.5) | collective-permute-done | bytes 655392 | tf_op jit(solution)/shard_map/ppermute | solution.py:279
  39.2 1.6 %collective-permute-start.8 = (bf16[640,512]{1,0:T(8,128)(2,1)}, bf16[640,512]{1,0:T(8,128)(2,1)S(1)}, u32[]{:S(2)}, u32[]{:S(2)}) collective-permute-start(bf16[640,512]{1,0:T(8,128)(2,1)} %collective-permute-done.4.refs_0_), channel_id=1, source_target_pairs={{0,2},{2,4},{4,6},{6,7},{7,5},{5,3},{3,1},{1,0},{8,10},{10,12},{12... | collective-permute-start | bytes 1966088 | tf_op jit(solution)/shard_map/ppermute | solution.py:278
  41.3 7.0 %shard_map.99 = (f32[640,1792]{1,0:T(8,128)S(1)}, f32[640,64]{1,0:T(8,128)S(1)}) custom-call(s32[8]{0:T(128)S(1)} %dynamic-slice_bitcast_fusion.where, bf16[640,512]{1,0:T(8,128)(2,1)} %collective-permute-done.4.refs_0_, bf16[640,512]{1,0:T(8,128)(2,1)} %collective-permute-done.5.refs_1_, ...), custom_call_target="tpu_custom_call", output_to_operand_aliasing={{0}: (5, {}), {1}: (6, {})} | custom-call | flops 2684354560 | bytes 14155776 | tf_op jit(solution)/shard_map/pallas_call | solution.py:178
  48.3 2.7 %collective-permute-done.2.refs_0_ = bf16[640,512]{1,0:T(8,128)(2,1)S(1)} collective-permute-done((bf16[640,512]{1,0:T(8,128)(2,1)}, bf16[640,512]{1,0:T(8,128)(2,1)S(1)}, u32[]{:S(2)}, u32[]{:S(2)}) %collective-permute-start.2) | collective-permute-done | bytes 655392 | tf_op jit(solution)/shard_map/ppermute | solution.py:278
  51.0 2.2 %collective-permute-done.3.refs_1_ = bf16[640,512]{1,0:T(8,128)(2,1)S(1)} collective-permute-done((bf16[640,512]{1,0:T(8,128)(2,1)}, bf16[640,512]{1,0:T(8,128)(2,1)S(1)}, u32[]{:S(2)}, u32[]{:S(2)}) %collective-permute-start.3) | collective-permute-done | bytes 655392 | tf_op jit(solution)/shard_map/ppermute | solution.py:279
  55.2 6.5 %shard_map.100 = (f32[640,1792]{1,0:T(8,128)S(1)}, f32[640,64]{1,0:T(8,128)S(1)}) custom-call(s32[8]{0:T(128)S(1)} %dynamic-slice_bitcast_fusion.where, bf16[640,512]{1,0:T(8,128)(2,1)S(1)} %collective-permute-done.2.refs_0_, bf16[640,512]{1,0:T(8,128)(2,1)S(1)} %collective-permute-done.3.refs_1_, ...), custom_call_target="tpu_custom_call", output_to_operand_aliasing={{0}: (5, {}), {1}: (6, {})} | custom-call | flops 2684354560 | bytes 14155776 | tf_op jit(solution)/shard_map/pallas_call | solution.py:178
  61.7 3.3 %collective-permute-done.8.refs_0_ = bf16[640,512]{1,0:T(8,128)(2,1)S(1)} collective-permute-done((bf16[640,512]{1,0:T(8,128)(2,1)}, bf16[640,512]{1,0:T(8,128)(2,1)S(1)}, u32[]{:S(2)}, u32[]{:S(2)}) %collective-permute-start.8) | collective-permute-done | bytes 655392 | tf_op jit(solution)/shard_map/ppermute | solution.py:278
  65.1 2.2 %collective-permute-done.9.refs_1_ = bf16[640,512]{1,0:T(8,128)(2,1)S(1)} collective-permute-done((bf16[640,512]{1,0:T(8,128)(2,1)}, bf16[640,512]{1,0:T(8,128)(2,1)S(1)}, u32[]{:S(2)}, u32[]{:S(2)}) %collective-permute-start.9) | collective-permute-done | bytes 655392 | tf_op jit(solution)/shard_map/ppermute | solution.py:279
  69.3 6.5 %shard_map.101 = (f32[640,1792]{1,0:T(8,128)S(1)}, f32[640,64]{1,0:T(8,128)S(1)}) custom-call(s32[8]{0:T(128)S(1)} %dynamic-slice_bitcast_fusion.where, bf16[640,512]{1,0:T(8,128)(2,1)S(1)} %collective-permute-done.8.refs_0_, bf16[640,512]{1,0:T(8,128)(2,1)S(1)} %collective-permute-done.9.refs_1_, ...), custom_call_target="tpu_custom_call", output_to_operand_aliasing={{0}: (5, {}), {1}: (6, {})} | custom-call | flops 2684354560 | bytes 14155776 | tf_op jit(solution)/shard_map/pallas_call | solution.py:178
  75.8 3.3 %collective-permute-done.6.refs_0_ = bf16[640,512]{1,0:T(8,128)(2,1)S(1)} collective-permute-done((bf16[640,512]{1,0:T(8,128)(2,1)S(1)}, bf16[640,512]{1,0:T(8,128)(2,1)S(1)}, u32[]{:S(2)}, u32[]{:S(2)}) %collective-permute-start.6) | collective-permute-done | bytes 655392 | tf_op jit(solution)/shard_map/ppermute | solution.py:278
  79.1 2.2 %collective-permute-done.7.refs_1_ = bf16[640,512]{1,0:T(8,128)(2,1)S(1)} collective-permute-done((bf16[640,512]{1,0:T(8,128)(2,1)S(1)}, bf16[640,512]{1,0:T(8,128)(2,1)S(1)}, u32[]{:S(2)}, u32[]{:S(2)}) %collective-permute-start.7) | collective-permute-done | bytes 655392 | tf_op jit(solution)/shard_map/ppermute | solution.py:279
  81.4 1.6 %collective-permute-start.14 = (bf16[384,512]{1,0:T(8,128)(2,1)S(1)}, bf16[384,512]{1,0:T(8,128)(2,1)S(1)}, u32[]{:S(2)}, u32[]{:S(2)}) collective-permute-start(bf16[384,512]{1,0:T(8,128)(2,1)S(1)} %slice.14), channel_id=1, source_target_pairs={{0,2},{2,4},{4,6},{6,7},{7,5},{5,3},{3,1},{1,0},{8,10},{10,12},{12... | collective-permute-start | bytes 1179656 | tf_op jit(solution)/shard_map/ppermute | solution.py:290
  83.5 6.5 %shard_map.102 = (f32[640,1792]{1,0:T(8,128)S(1)}, f32[640,64]{1,0:T(8,128)S(1)}) custom-call(s32[8]{0:T(128)S(1)} %dynamic-slice_bitcast_fusion.where, bf16[640,512]{1,0:T(8,128)(2,1)S(1)} %collective-permute-done.6.refs_0_, bf16[640,512]{1,0:T(8,128)(2,1)S(1)} %collective-permute-done.7.refs_1_, ...), custom_call_target="tpu_custom_call", output_to_operand_aliasing={{0}: (5, {}), {1}: (6, {})} | custom-call | flops 2684354560 | bytes 14155776 | tf_op jit(solution)/shard_map/pallas_call | solution.py:178
  90.0 3.1 %collective-permute-done.12.refs_0_ = bf16[640,512]{1,0:T(8,128)(2,1)S(1)} collective-permute-done((bf16[640,512]{1,0:T(8,128)(2,1)S(1)}, bf16[640,512]{1,0:T(8,128)(2,1)S(1)}, u32[]{:S(2)}, u32[]{:S(2)}) %collective-permute-start.12) | collective-permute-done | bytes 655392 | tf_op jit(solution)/shard_map/ppermute | solution.py:278
  93.2 2.1 %collective-permute-start.10 = (bf16[256,512]{1,0:T(8,128)(2,1)S(1)}, bf16[256,512]{1,0:T(8,128)(2,1)S(1)}, u32[]{:S(2)}, u32[]{:S(2)}) collective-permute-start(bf16[256,512]{1,0:T(8,128)(2,1)S(1)} %slice.12), channel_id=1, source_target_pairs={{0,2},{2,4},{4,6},{6,7},{7,5},{5,3},{3,1},{1,0},{8,10},{10,12},{12... | collective-permute-start | bytes 786440 | tf_op jit(solution)/shard_map/ppermute | solution.py:290
  95.3 6.3 %shard_map.103 = (f32[640,1792]{1,0:T(8,128)S(1)}, f32[640,64]{1,0:T(8,128)S(1)}, bf16[1024,1792]{1,0:T(8,128)(2,1)S(1)}) custom-call(s32[8]{0:T(128)S(1)} %dynamic-slice_bitcast_fusion.where, bf16[640,512]{1,0:T(8,128)(2,1)S(1)} %collective-permute-done.12.refs_0_, ...), custom_call_target="tpu_custom_call", output_to_operand_aliasing={{0}: (5, {}), {1}: (6, {})} | custom-call | flops 2684354560 | bytes 14155776 | tf_op jit(solution)/shard_map/pallas_call | solution.py:178
  101.6 2.1 %collective-permute-done.15.refs_1_ = bf16[384,512]{1,0:T(8,128)(2,1)S(1)} collective-permute-done((bf16[384,512]{1,0:T(8,128)(2,1)S(1)}, bf16[384,512]{1,0:T(8,128)(2,1)S(1)}, u32[]{:S(2)}, u32[]{:S(2)}) %collective-permute-start.15) | collective-permute-done | bytes 393248 | tf_op jit(solution)/shard_map/ppermute | solution.py:290
  103.7 3.4 %shard_map.104.refs_8_ = f32[64,256]{1,0:T(8,128)S(1)} custom-call(s32[8]{0:T(128)S(1)} %dynamic-slice_bitcast_fusion.where, s32[1,4]{1,0:T(1,128)S(1)} %copy-done.4, bf16[384,512]{1,0:T(8,128)(2,1)S(1)} %collective-permute-done.14.refs_0_, bf16[384,512]{1,0:T(8,128)(2,1)S(1)} %collective-permute-done.15.refs_1_, ...), custom_call_target="tpu_custom_call" | custom-call | flops 2013265920 | bytes 8585216 | tf_op jit(solution)/shard_map/pallas_call | solution.py:233
  107.9 2.6 %shard_map.105 = f32[64,256]{1,0:T(8,128)S(1)} custom-call(s32[8]{0:T(128)S(1)} %dynamic-slice_bitcast_fusion.where, s32[1,4]{1,0:T(1,128)S(1)} %copy-done.4, bf16[256,512]{1,0:T(8,128)(2,1)S(1)} %collective-permute-done.10.refs_0_, bf16[256,512]{1,0:T(8,128)(2,1)S(1)} %collective-permute-done.11.refs_1_, bf16[1024,1792]{1,0:T(8,128)(2,1)S(1)} %get-tuple-element.74.refs_2_, ...), custom_call_target="tpu_custom_call" | custom-call | flops 1342177280 | bytes 6946816 | tf_op jit(solution)/shard_map/pallas_call | solution.py:233
  110.8 1.7 %collective-permute-start.17 = (bf16[64,256]{1,0:T(8,128)(2,1)S(1)}, bf16[64,256]{1,0:T(8,128)(2,1)S(1)}, u32[]{:S(2)}, u32[]{:S(2)}) collective-permute-start(bf16[64,256]{1,0:T(8,128)(2,1)S(1)} %convert_element_type.21), channel_id=1, source_target_pairs={{0,2},{1,3},{2,0},{3,1},{4,6},{5,7},{6,4},{7,5},{8,10},{9,11},{10,... | collective-permute-start | bytes 98312 | tf_op jit(solution)/shard_map/ppermute | solution.py:306
  114.9 2.4 %collective-permute-done.18 = bf16[64,256]{1,0:T(8,128)(2,1)S(1)} collective-permute-done((bf16[64,256]{1,0:T(8,128)(2,1)S(1)}, bf16[64,256]{1,0:T(8,128)(2,1)S(1)}, u32[]{:S(2)}, u32[]{:S(2)}) %collective-permute-start.18) | collective-permute-done | bytes 32800 | tf_op jit(solution)/shard_map/ppermute | solution.py:306
  117.3 2.9 %collective-permute-start.19 = (bf16[64,256]{1,0:T(8,128)(2,1)S(1)}, bf16[64,256]{1,0:T(8,128)(2,1)S(1)}, u32[]{:S(2)}, u32[]{:S(2)}) collective-permute-start(bf16[64,256]{1,0:T(8,128)(2,1)S(1)} %fusion.5), channel_id=1, source_target_pairs={{0,4},{1,5},{2,6},{3,7},{4,0},{5,1},{6,2},{7,3},{8,12},{9,13},{10,... | collective-permute-start | bytes 98312 | tf_op jit(solution)/shard_map/ppermute | solution.py:306
  (47 shorter events, 16.2 us)
Async XLA Ops:
  0.6 8.6 %copy-start.4 = (s32[1,4]{1,0:T(1,128)S(1)}, s32[1,4]{1,0:T(1,128)}, u32[]{:S(2)}) copy-start(s32[1,4]{1,0:T(1,128)} %lens.5) | copy-start | bytes 52
  4.1 11.1 %copy-start = (bf16[8192,64]{0,1:T(8,128)(2,1)S(1)}, bf16[8192,64]{0,1:T(8,128)(2,1)}, u32[]{:S(2)}) copy-start(bf16[8192,64]{0,1:T(8,128)(2,1)} %param.12) | copy-start | bytes 3145732
  4.1 18.9 %collective-permute-start = (bf16[640,512]{1,0:T(8,128)(2,1)}, bf16[640,512]{1,0:T(8,128)(2,1)}, u32[]{:S(2)}, u32[]{:S(2)}) collective-permute-start(bf16[640,512]{1,0:T(8,128)(2,1)} %get-tuple-element.40.refs_0_), channel_id=1, source_target_pairs={{0,2},{2,4},{4,6},{6,7},{7,5},{5,3},{3,1},{1,0},{8,10},{10,12},{12... | collective-permute-start | bytes 1966088 | tf_op jit(solution)/shard_map/ppermute | solution.py:278
  7.2 18.0 %collective-permute-start.1 = (bf16[640,512]{1,0:T(8,128)(2,1)}, bf16[640,512]{1,0:T(8,128)(2,1)}, u32[]{:S(2)}, u32[]{:S(2)}) collective-permute-start(bf16[640,512]{1,0:T(8,128)(2,1)} %get-tuple-element.41.refs_1_), channel_id=1, source_target_pairs={{2,0},{4,2},{6,4},{7,6},{5,7},{3,5},{1,3},{0,1},{10,8},{12,10},{14... | collective-permute-start | bytes 1966088 | tf_op jit(solution)/shard_map/ppermute | solution.py:279
  7.2 29.9 %collective-permute-start.4 = (bf16[640,512]{1,0:T(8,128)(2,1)}, bf16[640,512]{1,0:T(8,128)(2,1)}, u32[]{:S(2)}, u32[]{:S(2)}) collective-permute-start(bf16[640,512]{1,0:T(8,128)(2,1)} %get-tuple-element.41.refs_1_), channel_id=1, source_target_pairs={{0,2},{2,4},{4,6},{6,7},{7,5},{5,3},{3,1},{1,0},{8,10},{10,12},{12... | collective-permute-start | bytes 1966088 | tf_op jit(solution)/shard_map/ppermute | solution.py:278
  9.2 30.0 %collective-permute-start.5 = (bf16[640,512]{1,0:T(8,128)(2,1)}, bf16[640,512]{1,0:T(8,128)(2,1)}, u32[]{:S(2)}, u32[]{:S(2)}) collective-permute-start(bf16[640,512]{1,0:T(8,128)(2,1)} %get-tuple-element.40.refs_0_), channel_id=1, source_target_pairs={{2,0},{4,2},{6,4},{7,6},{5,7},{3,5},{1,3},{0,1},{10,8},{12,10},{14... | collective-permute-start | bytes 1966088 | tf_op jit(solution)/shard_map/ppermute | solution.py:279
  9.3 2.0 %copy-start.5 = (bf16[4,256,1792]{2,1,0:T(8,128)(2,1)S(1)}, bf16[4,256,1792]{2,1,0:T(8,128)(2,1)}, u32[]{:S(2)}) copy-start(bf16[4,256,1792]{2,1,0:T(8,128)(2,1)} %param.11) | copy-start | bytes 11010052
  15.2 1.1 copy-start.2
  16.3 1.1 copy-start.3
  25.2 25.8 %collective-permute-start.2 = (bf16[640,512]{1,0:T(8,128)(2,1)}, bf16[640,512]{1,0:T(8,128)(2,1)S(1)}, u32[]{:S(2)}, u32[]{:S(2)}) collective-permute-start(bf16[640,512]{1,0:T(8,128)(2,1)} %collective-permute-done.refs_0_), channel_id=1, source_target_pairs={{0,2},{2,4},{4,6},{6,7},{7,5},{5,3},{3,1},{1,0},{8,10},{10,12},{12... | collective-permute-start | bytes 1966088 | tf_op jit(solution)/shard_map/ppermute | solution.py:278
  26.8 26.4 %collective-permute-start.3 = (bf16[640,512]{1,0:T(8,128)(2,1)}, bf16[640,512]{1,0:T(8,128)(2,1)S(1)}, u32[]{:S(2)}, u32[]{:S(2)}) collective-permute-start(bf16[640,512]{1,0:T(8,128)(2,1)} %collective-permute-done.1.refs_1_), channel_id=1, source_target_pairs={{2,0},{4,2},{6,4},{7,6},{5,7},{3,5},{1,3},{0,1},{10,8},{12,10},{14... | collective-permute-start | bytes 1966088 | tf_op jit(solution)/shard_map/ppermute | solution.py:279
  39.2 25.8 %collective-permute-start.8 = (bf16[640,512]{1,0:T(8,128)(2,1)}, bf16[640,512]{1,0:T(8,128)(2,1)S(1)}, u32[]{:S(2)}, u32[]{:S(2)}) collective-permute-start(bf16[640,512]{1,0:T(8,128)(2,1)} %collective-permute-done.4.refs_0_), channel_id=1, source_target_pairs={{0,2},{2,4},{4,6},{6,7},{7,5},{5,3},{3,1},{1,0},{8,10},{10,12},{12... | collective-permute-start | bytes 1966088 | tf_op jit(solution)/shard_map/ppermute | solution.py:278
  40.8 26.4 %collective-permute-start.9 = (bf16[640,512]{1,0:T(8,128)(2,1)}, bf16[640,512]{1,0:T(8,128)(2,1)S(1)}, u32[]{:S(2)}, u32[]{:S(2)}) collective-permute-start(bf16[640,512]{1,0:T(8,128)(2,1)} %collective-permute-done.5.refs_1_), channel_id=1, source_target_pairs={{2,0},{4,2},{6,4},{7,6},{5,7},{3,5},{1,3},{0,1},{10,8},{12,10},{14... | collective-permute-start | bytes 1966088 | tf_op jit(solution)/shard_map/ppermute | solution.py:279
  53.2 25.9 %collective-permute-start.6 = (bf16[640,512]{1,0:T(8,128)(2,1)S(1)}, bf16[640,512]{1,0:T(8,128)(2,1)S(1)}, u32[]{:S(2)}, u32[]{:S(2)}) collective-permute-start(bf16[640,512]{1,0:T(8,128)(2,1)S(1)} %collective-permute-done.2.refs_0_), channel_id=1, source_target_pairs={{0,2},{2,4},{4,6},{6,7},{7,5},{5,3},{3,1},{1,0},{8,10},{10,12},{12... | collective-permute-start | bytes 1966088 | tf_op jit(solution)/shard_map/ppermute | solution.py:278
  54.7 26.5 %collective-permute-start.7 = (bf16[640,512]{1,0:T(8,128)(2,1)S(1)}, bf16[640,512]{1,0:T(8,128)(2,1)S(1)}, u32[]{:S(2)}, u32[]{:S(2)}) collective-permute-start(bf16[640,512]{1,0:T(8,128)(2,1)S(1)} %collective-permute-done.3.refs_1_), channel_id=1, source_target_pairs={{2,0},{4,2},{6,4},{7,6},{5,7},{3,5},{1,3},{0,1},{10,8},{12,10},{14... | collective-permute-start | bytes 1966088 | tf_op jit(solution)/shard_map/ppermute | solution.py:279
  67.2 25.9 %collective-permute-start.12 = (bf16[640,512]{1,0:T(8,128)(2,1)S(1)}, bf16[640,512]{1,0:T(8,128)(2,1)S(1)}, u32[]{:S(2)}, u32[]{:S(2)}) collective-permute-start(bf16[640,512]{1,0:T(8,128)(2,1)S(1)} %collective-permute-done.8.refs_0_), channel_id=1, source_target_pairs={{0,2},{2,4},{4,6},{6,7},{7,5},{5,3},{3,1},{1,0},{8,10},{10,12},{12... | collective-permute-start | bytes 1966088 | tf_op jit(solution)/shard_map/ppermute | solution.py:278
  68.8 26.5 %collective-permute-start.13 = (bf16[640,512]{1,0:T(8,128)(2,1)S(1)}, bf16[640,512]{1,0:T(8,128)(2,1)S(1)}, u32[]{:S(2)}, u32[]{:S(2)}) collective-permute-start(bf16[640,512]{1,0:T(8,128)(2,1)S(1)} %collective-permute-done.9.refs_1_), channel_id=1, source_target_pairs={{2,0},{4,2},{6,4},{7,6},{5,7},{3,5},{1,3},{0,1},{10,8},{12,10},{14... | collective-permute-start | bytes 1966088 | tf_op jit(solution)/shard_map/ppermute | solution.py:279
  69.3 51.0 %collective-permute-start.20 = (bf16[128,2048]{1,0:T(8,128)(2,1)}, bf16[128,2048]{1,0:T(8,128)(2,1)}, u32[]{:S(2)}, u32[]{:S(2)}) collective-permute-start(bf16[128,2048]{1,0:T(8,128)(2,1)} %param.14), channel_id=1, source_target_pairs={{0,8},{8,0},{1,9},{9,1},{2,10},{10,2},{3,11},{11,3},{4,12},{12,4},... | collective-permute-start | bytes 1572872 | tf_op jit(solution)/shard_map/ppermute | solution.py:286
  81.4 20.2 %collective-permute-start.14 = (bf16[384,512]{1,0:T(8,128)(2,1)S(1)}, bf16[384,512]{1,0:T(8,128)(2,1)S(1)}, u32[]{:S(2)}, u32[]{:S(2)}) collective-permute-start(bf16[384,512]{1,0:T(8,128)(2,1)S(1)} %slice.14), channel_id=1, source_target_pairs={{0,2},{2,4},{4,6},{6,7},{7,5},{5,3},{3,1},{1,0},{8,10},{10,12},{12... | collective-permute-start | bytes 1179656 | tf_op jit(solution)/shard_map/ppermute | solution.py:290
  83.0 20.7 %collective-permute-start.15 = (bf16[384,512]{1,0:T(8,128)(2,1)S(1)}, bf16[384,512]{1,0:T(8,128)(2,1)S(1)}, u32[]{:S(2)}, u32[]{:S(2)}) collective-permute-start(bf16[384,512]{1,0:T(8,128)(2,1)S(1)} %slice.15), channel_id=1, source_target_pairs={{2,0},{4,2},{6,4},{7,6},{5,7},{3,5},{1,3},{0,1},{10,8},{12,10},{14... | collective-permute-start | bytes 1179656 | tf_op jit(solution)/shard_map/ppermute | solution.py:290
  93.2 14.0 %collective-permute-start.10 = (bf16[256,512]{1,0:T(8,128)(2,1)S(1)}, bf16[256,512]{1,0:T(8,128)(2,1)S(1)}, u32[]{:S(2)}, u32[]{:S(2)}) collective-permute-start(bf16[256,512]{1,0:T(8,128)(2,1)S(1)} %slice.12), channel_id=1, source_target_pairs={{0,2},{2,4},{4,6},{6,7},{7,5},{5,3},{3,1},{1,0},{8,10},{10,12},{12... | collective-permute-start | bytes 786440 | tf_op jit(solution)/shard_map/ppermute | solution.py:290
  95.3 12.6 %collective-permute-start.11 = (bf16[256,512]{1,0:T(8,128)(2,1)S(1)}, bf16[256,512]{1,0:T(8,128)(2,1)S(1)}, u32[]{:S(2)}, u32[]{:S(2)}) collective-permute-start(bf16[256,512]{1,0:T(8,128)(2,1)S(1)} %slice.13), channel_id=1, source_target_pairs={{2,0},{4,2},{6,4},{7,6},{5,7},{3,5},{1,3},{0,1},{10,8},{12,10},{14... | collective-permute-start | bytes 786440 | tf_op jit(solution)/shard_map/ppermute | solution.py:290
  95.3 8.4 %copy-start.1 = (bf16[1792,64]{0,1:T(8,128)(2,1)S(1)}, bf16[1792,64]{0,1:T(8,128)(2,1)}, u32[]{:S(2)}) copy-start(bf16[1792,64]{0,1:T(8,128)(2,1)} %param.13) | copy-start | bytes 688132
  110.5 4.3 %collective-permute-start.16 = (bf16[64,256]{1,0:T(8,128)(2,1)S(1)}, bf16[64,256]{1,0:T(8,128)(2,1)S(1)}, u32[]{:S(2)}, u32[]{:S(2)}) collective-permute-start(bf16[64,256]{1,0:T(8,128)(2,1)S(1)} %convert_element_type.21), channel_id=1, source_target_pairs={{0,1},{1,0},{2,3},{3,2},{4,5},{5,4},{6,7},{7,6},{8,9},{9,8},{10,11... | collective-permute-start | bytes 98312 | tf_op jit(solution)/shard_map/ppermute | solution.py:306
  110.8 4.1 %collective-permute-start.17 = (bf16[64,256]{1,0:T(8,128)(2,1)S(1)}, bf16[64,256]{1,0:T(8,128)(2,1)S(1)}, u32[]{:S(2)}, u32[]{:S(2)}) collective-permute-start(bf16[64,256]{1,0:T(8,128)(2,1)S(1)} %convert_element_type.21), channel_id=1, source_target_pairs={{0,2},{1,3},{2,0},{3,1},{4,6},{5,7},{6,4},{7,5},{8,10},{9,11},{10,... | collective-permute-start | bytes 98312 | tf_op jit(solution)/shard_map/ppermute | solution.py:306
  112.5 4.8 %collective-permute-start.18 = (bf16[64,256]{1,0:T(8,128)(2,1)S(1)}, bf16[64,256]{1,0:T(8,128)(2,1)S(1)}, u32[]{:S(2)}, u32[]{:S(2)}) collective-permute-start(bf16[64,256]{1,0:T(8,128)(2,1)S(1)} %convert_element_type.21), channel_id=1, source_target_pairs={{0,3},{1,2},{2,1},{3,0},{4,7},{5,6},{6,5},{7,4},{8,11},{9,10},{10,... | collective-permute-start | bytes 98312 | tf_op jit(solution)/shard_map/ppermute | solution.py:306
  117.3 5.2 %collective-permute-start.19 = (bf16[64,256]{1,0:T(8,128)(2,1)S(1)}, bf16[64,256]{1,0:T(8,128)(2,1)S(1)}, u32[]{:S(2)}, u32[]{:S(2)}) collective-permute-start(bf16[64,256]{1,0:T(8,128)(2,1)S(1)} %fusion.5), channel_id=1, source_target_pairs={{0,4},{1,5},{2,6},{3,7},{4,0},{5,1},{6,2},{7,3},{8,12},{9,13},{10,... | collective-permute-start | bytes 98312 | tf_op jit(solution)/shard_map/ppermute | solution.py:306

commit v5 on v4

--- a/solution.py
+++ b/solution.py
@@ -271,7 +271,7 @@
         for h in range(halves):
             o = 1 - h
             if step == 2 and h == 0:
-                right[h], left[o], state, grads = lax.optimization_barrier((right[h], left[o], state, grads))
+                right[h], left[o], state, grads, other = lax.optimization_barrier((right[h], left[o], state, grads, other))
             elif step > 1:
                 right[h], left[o], state = lax.optimization_barrier((right[h], left[o], state))
             xs = [right[h], left[o]]
@@ -301,9 +301,9 @@
             where, lengths, xs, last_weight, proj_t, state, grads, out_t, total, half, a, examples, seq_len
         )
     for hops in reduce_hops(size):
-        low = total.astype(jnp.bfloat16)
+        held = total
         for hop in hops:
-            total = total + lax.ppermute(low, "fsdp", [(i, i ^ hop) for i in range(size)]).astype(jnp.float32)
+            total = total + lax.ppermute(held, "fsdp", [(i, i ^ hop) for i in range(size)])
     sketch = total.reshape(rank_in, examples, rank_out).transpose(1, 0, 2)
     sketch = sketch.reshape(examples, rank_in * rank_out)
     share = sketch.shape[1] // size

time: 125 us -> 126 us (level)
  starting transfers between devices: 23.9 us -> 25.6 us
    ppermute x6, waiting for transfers between devices: 15.3 us -> 10.5 us  [on_device(): right[h] = lax.ppermute(right[h], 'fsdp', right_way)]
    ppermute x6, waiting for transfers between devices: 10.8 us -> 14.2 us  [on_device(): left[o] = lax.ppermute(left[o], 'fsdp', left_way)]
    ppermute x2, starting transfers between devices: 0.46 us -> 2.52 us  [on_device(): lax.ppermute(left[1][a:b], 'fsdp', left_way)]
  transfers between devices with their start and end apart: 21 -> 21, of which waited for: 17 -> 16; matrix products, arithmetic and copies ran while one was open for 2% -> 2% of each run, Pallas kernels for 44% -> 42%
where the time goes in v5:
time: 126 us
  Pallas kernels  58.1 us (46%)
  waiting for transfers between devices  32.9 us (26%)
  starting transfers between devices  25.6 us (20%)
  local copies, waits for them, and re-layouts  5.85 us (5%)
  other arithmetic  1.3 us (1%)
    pallas_call x7, Pallas kernels, absorb(): pl.pallas_call(functools.partial(absorb_kernel, parts, state is None, fin...  45.6 us
    ppermute x6, waiting for transfers between devices, on_device(): left[o] = lax.ppermute(left[o], 'fsdp', left_way)  14.2 us
    ppermute x6, starting transfers between devices, on_device(): right[h] = lax.ppermute(right[h], 'fsdp', right_way)  11.8 us
    ppermute x6, waiting for transfers between devices, on_device(): right[h] = lax.ppermute(right[h], 'fsdp', right_way)  10.5 us
    ppermute x4, starting transfers between devices, on_device(): lax.ppermute(held, 'fsdp', [(i, i ^ hop) for i in range(size)])  6.65 us
    pallas_call x2, Pallas kernels, finish(): pl.pallas_call(functools.partial(finish_kernel, examples, seq_len, step,...  5.94 us
    ppermute x4, waiting for transfers between devices, on_device(): lax.ppermute(held, 'fsdp', [(i, i ^ hop) for i in range(size)])  5.33 us
    unnamed x12, local copies, waits for them, and re-layouts  4.22 us
  transfers between devices with their start and end apart: 21, of which 16 were waited for; matrix products, arithmetic and copies ran while one was open for 2% of the time, Pallas kernels for 42%

profile of v5, /device:TPU:0, one launch (start us, length us, event | category | flops | bytes accessed | tf_op | source)
XLA Modules:
  0.0 125.5 jit_solution(676800275382671362)
XLA Ops:
  0.6 3.4 %shard_map.95 = (bf16[640,512]{1,0:T(8,128)(2,1)}, bf16[640,512]{1,0:T(8,128)(2,1)}) custom-call(s32[1,4]{1,0:T(1,128)} %lens.5, bf16[1024,1024]{1,0:T(8,128)(2,1)} %bitcast.20), custom_call_target="tpu_custom_call" | custom-call | flops 1342177280 | bytes 3407872 | tf_op jit(solution)/shard_map/pallas_call | solution.py:109
  4.1 3.1 %collective-permute-start = (bf16[640,512]{1,0:T(8,128)(2,1)}, bf16[640,512]{1,0:T(8,128)(2,1)}, u32[]{:S(2)}, u32[]{:S(2)}) collective-permute-start(bf16[640,512]{1,0:T(8,128)(2,1)} %get-tuple-element.41.refs_0_), channel_id=1, source_target_pairs={{0,2},{2,4},{4,6},{6,7},{7,5},{5,3},{3,1},{1,0},{8,10},{10,12},{12... | collective-permute-start | bytes 1966088 | tf_op jit(solution)/shard_map/ppermute | solution.py:278
  7.2 2.0 %collective-permute-start.5 = (bf16[640,512]{1,0:T(8,128)(2,1)}, bf16[640,512]{1,0:T(8,128)(2,1)}, u32[]{:S(2)}, u32[]{:S(2)}) collective-permute-start(bf16[640,512]{1,0:T(8,128)(2,1)} %get-tuple-element.42.refs_1_), channel_id=1, source_target_pairs={{0,2},{2,4},{4,6},{6,7},{7,5},{5,3},{3,1},{1,0},{8,10},{10,12},{12... | collective-permute-start | bytes 1966088 | tf_op jit(solution)/shard_map/ppermute | solution.py:278
  9.2 2.0 %copy-done.5 = bf16[4,256,1792]{2,1,0:T(8,128)(2,1)S(1)} copy-done((bf16[4,256,1792]{2,1,0:T(8,128)(2,1)S(1)}, bf16[4,256,1792]{2,1,0:T(8,128)(2,1)}, u32[]{:S(2)}) %copy-start.5) | copy-done | bytes 3670040
  11.3 3.2 %shard_map.97.refs_6_ = bf16[640,1792]{1,0:T(8,128)(2,1)S(1)} custom-call(s32[1,4]{1,0:T(1,128)S(1)} %copy-done.4, bf16[1024,1792]{1,0:T(8,128)(2,1)S(1)} %bitcast.18), custom_call_target="tpu_custom_call" | custom-call | flops 2348810240 | bytes 5963776 | tf_op jit(solution)/shard_map/pallas_call | solution.py:60
  17.4 5.6 %shard_map.96 = (f32[640,1792]{1,0:T(8,128)S(1)}, f32[640,64]{1,0:T(8,128)S(1)}) custom-call(s32[8]{0:T(128)S(1)} %dynamic-slice_bitcast_fusion.where, bf16[640,512]{1,0:T(8,128)(2,1)S(1)} %copy-done.2, bf16[640,512]{1,0:T(8,128)(2,1)S(1)} %copy-done.3, bf16[8192,1792]{1,0:T(8,128)(2,1)} %refs_2_.13, bf16[64,8192]{1,0:T(8,128)(2,1)S(1)} %bitcast.7), custom_call_target="tpu_custom_call" | custom-call | flops 2684354560 | bytes 14155776 | tf_op jit(solution)/shard_map/pallas_call | solution.py:178
  23.0 2.2 %collective-permute-done.1.refs_1_ = bf16[640,512]{1,0:T(8,128)(2,1)} collective-permute-done((bf16[640,512]{1,0:T(8,128)(2,1)}, bf16[640,512]{1,0:T(8,128)(2,1)}, u32[]{:S(2)}, u32[]{:S(2)}) %collective-permute-start.1) | collective-permute-done | bytes 655392 | tf_op jit(solution)/shard_map/ppermute | solution.py:279
  27.2 7.0 %shard_map.98 = (f32[640,1792]{1,0:T(8,128)S(1)}, f32[640,64]{1,0:T(8,128)S(1)}) custom-call(s32[8]{0:T(128)S(1)} %dynamic-slice_bitcast_fusion.where, bf16[640,512]{1,0:T(8,128)(2,1)} %collective-permute-done.refs_0_, bf16[640,512]{1,0:T(8,128)(2,1)} %collective-permute-done.1.refs_1_, ...), custom_call_target="tpu_custom_call", output_to_operand_aliasing={{0}: (5, {}), {1}: (6, {})} | custom-call | flops 2684354560 | bytes 14155776 | tf_op jit(solution)/shard_map/pallas_call | solution.py:178
  34.2 2.8 %collective-permute-done.5.refs_0_ = bf16[640,512]{1,0:T(8,128)(2,1)} collective-permute-done((bf16[640,512]{1,0:T(8,128)(2,1)}, bf16[640,512]{1,0:T(8,128)(2,1)}, u32[]{:S(2)}, u32[]{:S(2)}) %collective-permute-start.5) | collective-permute-done | bytes 655392 | tf_op jit(solution)/shard_map/ppermute | solution.py:278
  37.0 2.2 %collective-permute-done.6.refs_1_ = bf16[640,512]{1,0:T(8,128)(2,1)} collective-permute-done((bf16[640,512]{1,0:T(8,128)(2,1)}, bf16[640,512]{1,0:T(8,128)(2,1)}, u32[]{:S(2)}, u32[]{:S(2)}) %collective-permute-start.6) | collective-permute-done | bytes 655392 | tf_op jit(solution)/shard_map/ppermute | solution.py:279
  39.2 2.0 %collective-permute-start.9 = (bf16[640,512]{1,0:T(8,128)(2,1)}, bf16[640,512]{1,0:T(8,128)(2,1)S(1)}, u32[]{:S(2)}, u32[]{:S(2)}) collective-permute-start(bf16[640,512]{1,0:T(8,128)(2,1)} %collective-permute-done.5.refs_0_), channel_id=1, source_target_pairs={{0,2},{2,4},{4,6},{6,7},{7,5},{5,3},{3,1},{1,0},{8,10},{10,12},{12... | collective-permute-start | bytes 1966088 | tf_op jit(solution)/shard_map/ppermute | solution.py:278
  41.2 7.0 %shard_map.99 = (f32[640,1792]{1,0:T(8,128)S(1)}, f32[640,64]{1,0:T(8,128)S(1)}) custom-call(s32[8]{0:T(128)S(1)} %dynamic-slice_bitcast_fusion.where, bf16[640,512]{1,0:T(8,128)(2,1)} %collective-permute-done.5.refs_0_, bf16[640,512]{1,0:T(8,128)(2,1)} %collective-permute-done.6.refs_1_, ...), custom_call_target="tpu_custom_call", output_to_operand_aliasing={{0}: (5, {}), {1}: (6, {})} | custom-call | flops 2684354560 | bytes 14155776 | tf_op jit(solution)/shard_map/pallas_call | solution.py:178
  48.3 2.7 %collective-permute-done.3.refs_0_ = bf16[640,512]{1,0:T(8,128)(2,1)S(1)} collective-permute-done((bf16[640,512]{1,0:T(8,128)(2,1)}, bf16[640,512]{1,0:T(8,128)(2,1)S(1)}, u32[]{:S(2)}, u32[]{:S(2)}) %collective-permute-start.3) | collective-permute-done | bytes 655392 | tf_op jit(solution)/shard_map/ppermute | solution.py:278
  51.0 2.2 %collective-permute-done.4.refs_1_ = bf16[640,512]{1,0:T(8,128)(2,1)S(1)} collective-permute-done((bf16[640,512]{1,0:T(8,128)(2,1)}, bf16[640,512]{1,0:T(8,128)(2,1)S(1)}, u32[]{:S(2)}, u32[]{:S(2)}) %collective-permute-start.4) | collective-permute-done | bytes 655392 | tf_op jit(solution)/shard_map/ppermute | solution.py:279
  55.2 6.5 %shard_map.100 = (f32[640,1792]{1,0:T(8,128)S(1)}, f32[640,64]{1,0:T(8,128)S(1)}) custom-call(s32[8]{0:T(128)S(1)} %dynamic-slice_bitcast_fusion.where, bf16[640,512]{1,0:T(8,128)(2,1)S(1)} %collective-permute-done.3.refs_0_, bf16[640,512]{1,0:T(8,128)(2,1)S(1)} %collective-permute-done.4.refs_1_, ...), custom_call_target="tpu_custom_call", output_to_operand_aliasing={{0}: (5, {}), {1}: (6, {})} | custom-call | flops 2684354560 | bytes 14155776 | tf_op jit(solution)/shard_map/pallas_call | solution.py:178
  61.7 5.5 %collective-permute-done.10.refs_1_ = bf16[640,512]{1,0:T(8,128)(2,1)S(1)} collective-permute-done((bf16[640,512]{1,0:T(8,128)(2,1)}, bf16[640,512]{1,0:T(8,128)(2,1)S(1)}, u32[]{:S(2)}, u32[]{:S(2)}) %collective-permute-start.10) | collective-permute-done | bytes 655392 | tf_op jit(solution)/shard_map/ppermute | solution.py:279
  67.2 1.6 %collective-permute-start.13 = (bf16[640,512]{1,0:T(8,128)(2,1)S(1)}, bf16[640,512]{1,0:T(8,128)(2,1)S(1)}, u32[]{:S(2)}, u32[]{:S(2)}) collective-permute-start(bf16[640,512]{1,0:T(8,128)(2,1)S(1)} %collective-permute-done.9.refs_0_), channel_id=1, source_target_pairs={{0,2},{2,4},{4,6},{6,7},{7,5},{5,3},{3,1},{1,0},{8,10},{10,12},{12... | collective-permute-start | bytes 1966088 | tf_op jit(solution)/shard_map/ppermute | solution.py:278
  69.2 6.5 %shard_map.101 = (f32[640,1792]{1,0:T(8,128)S(1)}, f32[640,64]{1,0:T(8,128)S(1)}) custom-call(s32[8]{0:T(128)S(1)} %dynamic-slice_bitcast_fusion.where, bf16[640,512]{1,0:T(8,128)(2,1)S(1)} %collective-permute-done.9.refs_0_, bf16[640,512]{1,0:T(8,128)(2,1)S(1)} %collective-permute-done.10.refs_1_, ...), custom_call_target="tpu_custom_call", output_to_operand_aliasing={{0}: (5, {}), {1}: (6, {})} | custom-call | flops 2684354560 | bytes 14155776 | tf_op jit(solution)/shard_map/pallas_call | solution.py:178
  75.8 3.3 %collective-permute-done.7.refs_0_ = bf16[640,512]{1,0:T(8,128)(2,1)S(1)} collective-permute-done((bf16[640,512]{1,0:T(8,128)(2,1)S(1)}, bf16[640,512]{1,0:T(8,128)(2,1)S(1)}, u32[]{:S(2)}, u32[]{:S(2)}) %collective-permute-start.7) | collective-permute-done | bytes 655392 | tf_op jit(solution)/shard_map/ppermute | solution.py:278
  79.1 2.2 %collective-permute-done.8.refs_1_ = bf16[640,512]{1,0:T(8,128)(2,1)S(1)} collective-permute-done((bf16[640,512]{1,0:T(8,128)(2,1)S(1)}, bf16[640,512]{1,0:T(8,128)(2,1)S(1)}, u32[]{:S(2)}, u32[]{:S(2)}) %collective-permute-start.8) | collective-permute-done | bytes 655392 | tf_op jit(solution)/shard_map/ppermute | solution.py:279
  81.4 1.6 %collective-permute-start.15 = (bf16[384,512]{1,0:T(8,128)(2,1)S(1)}, bf16[384,512]{1,0:T(8,128)(2,1)S(1)}, u32[]{:S(2)}, u32[]{:S(2)}) collective-permute-start(bf16[384,512]{1,0:T(8,128)(2,1)S(1)} %slice.14), channel_id=1, source_target_pairs={{0,2},{2,4},{4,6},{6,7},{7,5},{5,3},{3,1},{1,0},{8,10},{10,12},{12... | collective-permute-start | bytes 1179656 | tf_op jit(solution)/shard_map/ppermute | solution.py:290
  85.0 6.5 %shard_map.102 = (f32[640,1792]{1,0:T(8,128)S(1)}, f32[640,64]{1,0:T(8,128)S(1)}) custom-call(s32[8]{0:T(128)S(1)} %dynamic-slice_bitcast_fusion.where, bf16[640,512]{1,0:T(8,128)(2,1)S(1)} %collective-permute-done.7.refs_0_, bf16[640,512]{1,0:T(8,128)(2,1)S(1)} %collective-permute-done.8.refs_1_, ...), custom_call_target="tpu_custom_call", output_to_operand_aliasing={{0}: (5, {}), {1}: (6, {})} | custom-call | flops 2684354560 | bytes 14155776 | tf_op jit(solution)/shard_map/pallas_call | solution.py:178
  91.5 1.6 %collective-permute-done.13.refs_0_ = bf16[640,512]{1,0:T(8,128)(2,1)S(1)} collective-permute-done((bf16[640,512]{1,0:T(8,128)(2,1)S(1)}, bf16[640,512]{1,0:T(8,128)(2,1)S(1)}, u32[]{:S(2)}, u32[]{:S(2)}) %collective-permute-start.13) | collective-permute-done | bytes 655392 | tf_op jit(solution)/shard_map/ppermute | solution.py:278
  93.1 2.1 %collective-permute-start.12 = (bf16[256,512]{1,0:T(8,128)(2,1)S(1)}, bf16[256,512]{1,0:T(8,128)(2,1)S(1)}, u32[]{:S(2)}, u32[]{:S(2)}) collective-permute-start(bf16[256,512]{1,0:T(8,128)(2,1)S(1)} %slice.13), channel_id=1, source_target_pairs={{2,0},{4,2},{6,4},{7,6},{5,7},{3,5},{1,3},{0,1},{10,8},{12,10},{14... | collective-permute-start | bytes 786440 | tf_op jit(solution)/shard_map/ppermute | solution.py:290
  95.3 6.3 %shard_map.103 = (f32[640,1792]{1,0:T(8,128)S(1)}, f32[640,64]{1,0:T(8,128)S(1)}, bf16[1024,1792]{1,0:T(8,128)(2,1)S(1)}) custom-call(s32[8]{0:T(128)S(1)} %dynamic-slice_bitcast_fusion.where, bf16[640,512]{1,0:T(8,128)(2,1)S(1)} %collective-permute-done.13.refs_0_, ...), custom_call_target="tpu_custom_call", output_to_operand_aliasing={{0}: (5, {}), {1}: (6, {})} | custom-call | flops 2684354560 | bytes 14155776 | tf_op jit(solution)/shard_map/pallas_call | solution.py:178
  101.6 2.1 %collective-permute-done.16.refs_1_ = bf16[384,512]{1,0:T(8,128)(2,1)S(1)} collective-permute-done((bf16[384,512]{1,0:T(8,128)(2,1)S(1)}, bf16[384,512]{1,0:T(8,128)(2,1)S(1)}, u32[]{:S(2)}, u32[]{:S(2)}) %collective-permute-start.16) | collective-permute-done | bytes 393248 | tf_op jit(solution)/shard_map/ppermute | solution.py:290
  103.7 3.4 %shard_map.104.refs_8_ = f32[64,256]{1,0:T(8,128)S(1)} custom-call(s32[8]{0:T(128)S(1)} %dynamic-slice_bitcast_fusion.where, s32[1,4]{1,0:T(1,128)S(1)} %copy-done.4, bf16[384,512]{1,0:T(8,128)(2,1)S(1)} %collective-permute-done.15.refs_0_, bf16[384,512]{1,0:T(8,128)(2,1)S(1)} %collective-permute-done.16.refs_1_, ...), custom_call_target="tpu_custom_call" | custom-call | flops 2013265920 | bytes 8585216 | tf_op jit(solution)/shard_map/pallas_call | solution.py:233
  107.8 2.6 %shard_map.105 = f32[64,256]{1,0:T(8,128)S(1)} custom-call(s32[8]{0:T(128)S(1)} %dynamic-slice_bitcast_fusion.where, s32[1,4]{1,0:T(1,128)S(1)} %copy-done.4, bf16[256,512]{1,0:T(8,128)(2,1)S(1)} %collective-permute-done.11.refs_0_, bf16[256,512]{1,0:T(8,128)(2,1)S(1)} %collective-permute-done.12.refs_1_, bf16[1024,1792]{1,0:T(8,128)(2,1)S(1)} %get-tuple-element.75.refs_2_, ...), custom_call_target="tpu_custom_call" | custom-call | flops 1342177280 | bytes 6946816 | tf_op jit(solution)/shard_map/pallas_call | solution.py:233
  110.8 1.7 %collective-permute-start.18 = (f32[64,256]{1,0:T(8,128)S(1)}, f32[64,256]{1,0:T(8,128)S(1)}, u32[]{:S(2)}, u32[]{:S(2)}) collective-permute-start(f32[64,256]{1,0:T(8,128)S(1)} %shard_map.105), channel_id=1, source_target_pairs={{0,2},{1,3},{2,0},{3,1},{4,6},{5,7},{6,4},{7,5},{8,10},{9,11},{10,... | collective-permute-start | bytes 196616 | tf_op jit(solution)/shard_map/ppermute | solution.py:306
  115.6 2.0 %collective-permute-done.19 = f32[64,256]{1,0:T(8,128)S(1)} collective-permute-done((f32[64,256]{1,0:T(8,128)S(1)}, f32[64,256]{1,0:T(8,128)S(1)}, u32[]{:S(2)}, u32[]{:S(2)}) %collective-permute-start.19) | collective-permute-done | bytes 65568 | tf_op jit(solution)/shard_map/ppermute | solution.py:306
  117.6 3.1 %collective-permute-start.20 = (f32[64,256]{1,0:T(8,128)S(1)}, f32[64,256]{1,0:T(8,128)S(1)}, u32[]{:S(2)}, u32[]{:S(2)}) collective-permute-start(f32[64,256]{1,0:T(8,128)S(1)} %add_add_fusion), channel_id=1, source_target_pairs={{0,4},{1,5},{2,6},{3,7},{4,0},{5,1},{6,2},{7,3},{8,12},{9,13},{10,... | collective-permute-start | bytes 196616 | tf_op jit(solution)/shard_map/ppermute | solution.py:306
  122.0 1.7 %collective-permute-done.20 = f32[64,256]{1,0:T(8,128)S(1)} collective-permute-done((f32[64,256]{1,0:T(8,128)S(1)}, f32[64,256]{1,0:T(8,128)S(1)}, u32[]{:S(2)}, u32[]{:S(2)}) %collective-permute-start.20) | collective-permute-done | bytes 65568 | tf_op jit(solution)/shard_map/ppermute | solution.py:306
  (46 shorter events, 17.0 us)
Async XLA Ops:
  0.6 8.6 %copy-start.4 = (s32[1,4]{1,0:T(1,128)S(1)}, s32[1,4]{1,0:T(1,128)}, u32[]{:S(2)}) copy-start(s32[1,4]{1,0:T(1,128)} %lens.5) | copy-start | bytes 52
  4.1 11.1 %copy-start = (bf16[8192,64]{0,1:T(8,128)(2,1)S(1)}, bf16[8192,64]{0,1:T(8,128)(2,1)}, u32[]{:S(2)}) copy-start(bf16[8192,64]{0,1:T(8,128)(2,1)} %param.12) | copy-start | bytes 3145732
  4.1 18.9 %collective-permute-start = (bf16[640,512]{1,0:T(8,128)(2,1)}, bf16[640,512]{1,0:T(8,128)(2,1)}, u32[]{:S(2)}, u32[]{:S(2)}) collective-permute-start(bf16[640,512]{1,0:T(8,128)(2,1)} %get-tuple-element.41.refs_0_), channel_id=1, source_target_pairs={{0,2},{2,4},{4,6},{6,7},{7,5},{5,3},{3,1},{1,0},{8,10},{10,12},{12... | collective-permute-start | bytes 1966088 | tf_op jit(solution)/shard_map/ppermute | solution.py:278
  7.2 18.0 %collective-permute-start.1 = (bf16[640,512]{1,0:T(8,128)(2,1)}, bf16[640,512]{1,0:T(8,128)(2,1)}, u32[]{:S(2)}, u32[]{:S(2)}) collective-permute-start(bf16[640,512]{1,0:T(8,128)(2,1)} %get-tuple-element.42.refs_1_), channel_id=1, source_target_pairs={{2,0},{4,2},{6,4},{7,6},{5,7},{3,5},{1,3},{0,1},{10,8},{12,10},{14... | collective-permute-start | bytes 1966088 | tf_op jit(solution)/shard_map/ppermute | solution.py:279
  7.2 29.9 %collective-permute-start.5 = (bf16[640,512]{1,0:T(8,128)(2,1)}, bf16[640,512]{1,0:T(8,128)(2,1)}, u32[]{:S(2)}, u32[]{:S(2)}) collective-permute-start(bf16[640,512]{1,0:T(8,128)(2,1)} %get-tuple-element.42.refs_1_), channel_id=1, source_target_pairs={{0,2},{2,4},{4,6},{6,7},{7,5},{5,3},{3,1},{1,0},{8,10},{10,12},{12... | collective-permute-start | bytes 1966088 | tf_op jit(solution)/shard_map/ppermute | solution.py:278
  9.2 30.0 %collective-permute-start.6 = (bf16[640,512]{1,0:T(8,128)(2,1)}, bf16[640,512]{1,0:T(8,128)(2,1)}, u32[]{:S(2)}, u32[]{:S(2)}) collective-permute-start(bf16[640,512]{1,0:T(8,128)(2,1)} %get-tuple-element.41.refs_0_), channel_id=1, source_target_pairs={{2,0},{4,2},{6,4},{7,6},{5,7},{3,5},{1,3},{0,1},{10,8},{12,10},{14... | collective-permute-start | bytes 1966088 | tf_op jit(solution)/shard_map/ppermute | solution.py:279
  9.2 13.7 %collective-permute-start.2 = (bf16[128,2048]{1,0:T(8,128)(2,1)}, bf16[128,2048]{1,0:T(8,128)(2,1)}, u32[]{:S(2)}, u32[]{:S(2)}) collective-permute-start(bf16[128,2048]{1,0:T(8,128)(2,1)} %param.14), channel_id=1, source_target_pairs={{0,8},{8,0},{1,9},{9,1},{2,10},{10,2},{3,11},{11,3},{4,12},{12,4},... | collective-permute-start | bytes 1572872 | tf_op jit(solution)/shard_map/ppermute | solution.py:286
  9.2 2.0 %copy-start.5 = (bf16[4,256,1792]{2,1,0:T(8,128)(2,1)S(1)}, bf16[4,256,1792]{2,1,0:T(8,128)(2,1)}, u32[]{:S(2)}) copy-start(bf16[4,256,1792]{2,1,0:T(8,128)(2,1)} %param.11) | copy-start | bytes 11010052
  15.2 1.1 copy-start.2
  16.3 1.1 copy-start.3
  25.2 25.8 %collective-permute-start.3 = (bf16[640,512]{1,0:T(8,128)(2,1)}, bf16[640,512]{1,0:T(8,128)(2,1)S(1)}, u32[]{:S(2)}, u32[]{:S(2)}) collective-permute-start(bf16[640,512]{1,0:T(8,128)(2,1)} %collective-permute-done.refs_0_), channel_id=1, source_target_pairs={{0,2},{2,4},{4,6},{6,7},{7,5},{5,3},{3,1},{1,0},{8,10},{10,12},{12... | collective-permute-start | bytes 1966088 | tf_op jit(solution)/shard_map/ppermute | solution.py:278
  26.7 26.4 %collective-permute-start.4 = (bf16[640,512]{1,0:T(8,128)(2,1)}, bf16[640,512]{1,0:T(8,128)(2,1)S(1)}, u32[]{:S(2)}, u32[]{:S(2)}) collective-permute-start(bf16[640,512]{1,0:T(8,128)(2,1)} %collective-permute-done.1.refs_1_), channel_id=1, source_target_pairs={{2,0},{4,2},{6,4},{7,6},{5,7},{3,5},{1,3},{0,1},{10,8},{12,10},{14... | collective-permute-start | bytes 1966088 | tf_op jit(solution)/shard_map/ppermute | solution.py:279
  39.2 28.0 %collective-permute-start.10 = (bf16[640,512]{1,0:T(8,128)(2,1)}, bf16[640,512]{1,0:T(8,128)(2,1)S(1)}, u32[]{:S(2)}, u32[]{:S(2)}) collective-permute-start(bf16[640,512]{1,0:T(8,128)(2,1)} %collective-permute-done.6.refs_1_), channel_id=1, source_target_pairs={{2,0},{4,2},{6,4},{7,6},{5,7},{3,5},{1,3},{0,1},{10,8},{12,10},{14... | collective-permute-start | bytes 1966088 | tf_op jit(solution)/shard_map/ppermute | solution.py:279
  39.2 28.0 %collective-permute-start.9 = (bf16[640,512]{1,0:T(8,128)(2,1)}, bf16[640,512]{1,0:T(8,128)(2,1)S(1)}, u32[]{:S(2)}, u32[]{:S(2)}) collective-permute-start(bf16[640,512]{1,0:T(8,128)(2,1)} %collective-permute-done.5.refs_0_), channel_id=1, source_target_pairs={{0,2},{2,4},{4,6},{6,7},{7,5},{5,3},{3,1},{1,0},{8,10},{10,12},{12... | collective-permute-start | bytes 1966088 | tf_op jit(solution)/shard_map/ppermute | solution.py:278
  53.1 25.9 %collective-permute-start.7 = (bf16[640,512]{1,0:T(8,128)(2,1)S(1)}, bf16[640,512]{1,0:T(8,128)(2,1)S(1)}, u32[]{:S(2)}, u32[]{:S(2)}) collective-permute-start(bf16[640,512]{1,0:T(8,128)(2,1)S(1)} %collective-permute-done.3.refs_0_), channel_id=1, source_target_pairs={{0,2},{2,4},{4,6},{6,7},{7,5},{5,3},{3,1},{1,0},{8,10},{10,12},{12... | collective-permute-start | bytes 1966088 | tf_op jit(solution)/shard_map/ppermute | solution.py:278
  54.7 26.5 %collective-permute-start.8 = (bf16[640,512]{1,0:T(8,128)(2,1)S(1)}, bf16[640,512]{1,0:T(8,128)(2,1)S(1)}, u32[]{:S(2)}, u32[]{:S(2)}) collective-permute-start(bf16[640,512]{1,0:T(8,128)(2,1)S(1)} %collective-permute-done.4.refs_1_), channel_id=1, source_target_pairs={{2,0},{4,2},{6,4},{7,6},{5,7},{3,5},{1,3},{0,1},{10,8},{12,10},{14... | collective-permute-start | bytes 1966088 | tf_op jit(solution)/shard_map/ppermute | solution.py:279
  67.2 25.9 %collective-permute-start.13 = (bf16[640,512]{1,0:T(8,128)(2,1)S(1)}, bf16[640,512]{1,0:T(8,128)(2,1)S(1)}, u32[]{:S(2)}, u32[]{:S(2)}) collective-permute-start(bf16[640,512]{1,0:T(8,128)(2,1)S(1)} %collective-permute-done.9.refs_0_), channel_id=1, source_target_pairs={{0,2},{2,4},{4,6},{6,7},{7,5},{5,3},{3,1},{1,0},{8,10},{10,12},{12... | collective-permute-start | bytes 1966088 | tf_op jit(solution)/shard_map/ppermute | solution.py:278
  68.8 26.5 %collective-permute-start.14 = (bf16[640,512]{1,0:T(8,128)(2,1)S(1)}, bf16[640,512]{1,0:T(8,128)(2,1)S(1)}, u32[]{:S(2)}, u32[]{:S(2)}) collective-permute-start(bf16[640,512]{1,0:T(8,128)(2,1)S(1)} %collective-permute-done.10.refs_1_), channel_id=1, source_target_pairs={{2,0},{4,2},{6,4},{7,6},{5,7},{3,5},{1,3},{0,1},{10,8},{12,10},{14... | collective-permute-start | bytes 1966088 | tf_op jit(solution)/shard_map/ppermute | solution.py:279
  81.4 20.2 %collective-permute-start.15 = (bf16[384,512]{1,0:T(8,128)(2,1)S(1)}, bf16[384,512]{1,0:T(8,128)(2,1)S(1)}, u32[]{:S(2)}, u32[]{:S(2)}) collective-permute-start(bf16[384,512]{1,0:T(8,128)(2,1)S(1)} %slice.14), channel_id=1, source_target_pairs={{0,2},{2,4},{4,6},{6,7},{7,5},{5,3},{3,1},{1,0},{8,10},{10,12},{12... | collective-permute-start | bytes 1179656 | tf_op jit(solution)/shard_map/ppermute | solution.py:290
  83.0 20.7 %collective-permute-start.16 = (bf16[384,512]{1,0:T(8,128)(2,1)S(1)}, bf16[384,512]{1,0:T(8,128)(2,1)S(1)}, u32[]{:S(2)}, u32[]{:S(2)}) collective-permute-start(bf16[384,512]{1,0:T(8,128)(2,1)S(1)} %slice.15), channel_id=1, source_target_pairs={{2,0},{4,2},{6,4},{7,6},{5,7},{3,5},{1,3},{0,1},{10,8},{12,10},{14... | collective-permute-start | bytes 1179656 | tf_op jit(solution)/shard_map/ppermute | solution.py:290
  83.4 23.7 %collective-permute-start.11 = (bf16[256,512]{1,0:T(8,128)(2,1)S(1)}, bf16[256,512]{1,0:T(8,128)(2,1)S(1)}, u32[]{:S(2)}, u32[]{:S(2)}) collective-permute-start(bf16[256,512]{1,0:T(8,128)(2,1)S(1)} %slice.12), channel_id=1, source_target_pairs={{0,2},{2,4},{4,6},{6,7},{7,5},{5,3},{3,1},{1,0},{8,10},{10,12},{12... | collective-permute-start | bytes 786440 | tf_op jit(solution)/shard_map/ppermute | solution.py:290
  93.1 14.7 %collective-permute-start.12 = (bf16[256,512]{1,0:T(8,128)(2,1)S(1)}, bf16[256,512]{1,0:T(8,128)(2,1)S(1)}, u32[]{:S(2)}, u32[]{:S(2)}) collective-permute-start(bf16[256,512]{1,0:T(8,128)(2,1)S(1)} %slice.13), channel_id=1, source_target_pairs={{2,0},{4,2},{6,4},{7,6},{5,7},{3,5},{1,3},{0,1},{10,8},{12,10},{14... | collective-permute-start | bytes 786440 | tf_op jit(solution)/shard_map/ppermute | solution.py:290
  95.3 8.4 %copy-start.1 = (bf16[1792,64]{0,1:T(8,128)(2,1)S(1)}, bf16[1792,64]{0,1:T(8,128)(2,1)}, u32[]{:S(2)}) copy-start(bf16[1792,64]{0,1:T(8,128)(2,1)} %param.13) | copy-start | bytes 688132
  110.4 5.0 %collective-permute-start.17 = (f32[64,256]{1,0:T(8,128)S(1)}, f32[64,256]{1,0:T(8,128)S(1)}, u32[]{:S(2)}, u32[]{:S(2)}) collective-permute-start(f32[64,256]{1,0:T(8,128)S(1)} %shard_map.105), channel_id=1, source_target_pairs={{0,1},{1,0},{2,3},{3,2},{4,5},{5,4},{6,7},{7,6},{8,9},{9,8},{10,11... | collective-permute-start | bytes 196616 | tf_op jit(solution)/shard_map/ppermute | solution.py:306
  110.8 4.8 %collective-permute-start.18 = (f32[64,256]{1,0:T(8,128)S(1)}, f32[64,256]{1,0:T(8,128)S(1)}, u32[]{:S(2)}, u32[]{:S(2)}) collective-permute-start(f32[64,256]{1,0:T(8,128)S(1)} %shard_map.105), channel_id=1, source_target_pairs={{0,2},{1,3},{2,0},{3,1},{4,6},{5,7},{6,4},{7,5},{8,10},{9,11},{10,... | collective-permute-start | bytes 196616 | tf_op jit(solution)/shard_map/ppermute | solution.py:306
  112.5 5.2 %collective-permute-start.19 = (f32[64,256]{1,0:T(8,128)S(1)}, f32[64,256]{1,0:T(8,128)S(1)}, u32[]{:S(2)}, u32[]{:S(2)}) collective-permute-start(f32[64,256]{1,0:T(8,128)S(1)} %shard_map.105), channel_id=1, source_target_pairs={{0,3},{1,2},{2,1},{3,0},{4,7},{5,6},{6,5},{7,4},{8,11},{9,10},{10,... | collective-permute-start | bytes 196616 | tf_op jit(solution)/shard_map/ppermute | solution.py:306
  117.6 6.0 %collective-permute-start.20 = (f32[64,256]{1,0:T(8,128)S(1)}, f32[64,256]{1,0:T(8,128)S(1)}, u32[]{:S(2)}, u32[]{:S(2)}) collective-permute-start(f32[64,256]{1,0:T(8,128)S(1)} %add_add_fusion), channel_id=1, source_target_pairs={{0,4},{1,5},{2,6},{3,7},{4,0},{5,1},{6,2},{7,3},{8,12},{9,13},{10,... | collective-permute-start | bytes 196616 | tf_op jit(solution)/shard_map/ppermute | solution.py:306

commit v6 on v4

--- a/solution.py
+++ b/solution.py
@@ -245,6 +245,30 @@
     )(where, lengths, *args)
 
 
+def score_kernel(share, sketch, queries_t, own_cols, scores):
+    place = lax.axis_index("fsdp")
+    own_cols[...] = sketch[:, pl.ds(pl.multiple_of(place * share, share), share)]
+    scores[...] = dot(sketch[...].astype(jnp.bfloat16), queries_t[...])
+
+
+def score(sketch, queries_t, size):
+    examples, entries = sketch.shape
+    share, count = entries // size, queries_t.shape[1]
+    return pl.pallas_call(
+        functools.partial(score_kernel, share),
+        out_shape=[
+            jax.ShapeDtypeStruct((examples, share), jnp.float32),
+            jax.ShapeDtypeStruct((examples, count), jnp.float32),
+        ],
+        in_specs=in_vmem(2),
+        out_specs=in_vmem(2),
+        compiler_params=pltpu.CompilerParams(vmem_limit_bytes=SMALL),
+        cost_estimate=pl.CostEstimate(
+            flops=2 * examples * entries * count, bytes_accessed=2 * entries * count, transcendentals=0
+        ),
+    )(sketch, queries_t)
+
+
 def on_device(order, tokens, lengths, gate_weight, hidden_grad, in_proj, out_proj, query_sketch):
     examples, seq_len, width = tokens.shape
     hidden = hidden_grad.shape[2]
@@ -272,6 +296,10 @@
             o = 1 - h
             if step == 2 and h == 0:
                 right[h], left[o], state, grads = lax.optimization_barrier((right[h], left[o], state, grads))
+            elif step == 3 and h == 0:
+                right[h], left[o], state, query_sketch = lax.optimization_barrier(
+                    (right[h], left[o], state, query_sketch)
+                )
             elif step > 1:
                 right[h], left[o], state = lax.optimization_barrier((right[h], left[o], state))
             xs = [right[h], left[o]]
@@ -283,17 +311,24 @@
         if step == 1:
             state = absorb(where, [(0, 0), (0, 1)], own, gate_weight, proj_t, None, tile)
             grads = pack(lengths, flat_grads, examples, seq_len, 0, hidden, tile)
+        if step == 3:
             other = lax.ppermute(query_sketch, "dp", [(0, 1), (1, 0)])
-    right[0], left[1], state = lax.optimization_barrier((right[0], left[1], state))
+            mine_t, other_t = query_sketch.T, other.T
+            first = lax.axis_index("dp") == 0
+            queries_t = jnp.concatenate(
+                [jnp.where(first, mine_t, other_t), jnp.where(first, other_t, mine_t)], axis=0
+            )
+    right[0], left[1], state, queries_t = lax.optimization_barrier((right[0], left[1], state, queries_t))
     cuts = [(0, CUT), (CUT, LIVE)]
-    last = [
-        [lax.ppermute(right[0][a:b], "fsdp", right_way), lax.ppermute(left[1][a:b], "fsdp", left_way)]
-        for a, b in cuts
-    ]
+    ends = [right[0], left[1]]
+    last = [[lax.ppermute(ends[0][:CUT], "fsdp", right_way), lax.ppermute(ends[1][:CUT], "fsdp", left_way)]]
     for h in range(halves):
         parts = [(half - 1, h), (size - half + 1, 1 - h)]
         final = half if h == halves - 1 else None
         state = absorb(where, parts, [right[h], left[1 - h]], gate_weight, proj_t, state, tile, final)
+        if h == 0:
+            *ends, state = lax.optimization_barrier((ends[0][CUT:], ends[1][CUT:], state))
+            last.append([lax.ppermute(ends[0], "fsdp", right_way), lax.ppermute(ends[1], "fsdp", left_way)])
     *state, last_weight = state
     total = None
     for xs, (a, _) in zip(last, cuts, strict=True):
@@ -306,16 +341,7 @@
             total = total + lax.ppermute(low, "fsdp", [(i, i ^ hop) for i in range(size)]).astype(jnp.float32)
     sketch = total.reshape(rank_in, examples, rank_out).transpose(1, 0, 2)
     sketch = sketch.reshape(examples, rank_in * rank_out)
-    share = sketch.shape[1] // size
-    own_cols = lax.dynamic_slice_in_dim(sketch, lax.axis_index("fsdp") * share, share, 1)
-    first = lax.axis_index("dp") == 0
-    queries = jnp.concatenate(
-        [jnp.where(first, query_sketch, other), jnp.where(first, other, query_sketch)], axis=1
-    )
-    scores = jnp.einsum(
-        "ek,qk->eq", sketch.astype(jnp.bfloat16), queries, preferred_element_type=jnp.float32
-    )
-    return (own_cols, scores)
+    return score(sketch, queries_t, size)
 
 
 def solution(mesh):

time: 125 us -> 123 us (0.984)
  waiting for transfers between devices: 33.3 us -> 24.5 us
  local copies, waits for them, and re-layouts: 5.85 us -> 11 us
  starting transfers between devices: 23.9 us -> 25.3 us
    ppermute x6, waiting for transfers between devices: 15.3 us -> 5.28 us  [on_device(): right[h] = lax.ppermute(right[h], 'fsdp', right_way)]
    unnamed x12 -> x22, local copies, waits for them, and re-layouts: 4.23 us -> 7.9 us
    optimization_barrier x0 -> x1, local copies, waits for them, and re-layouts: none -> 2.05 us  [on_device(): lax.optimization_barrier((right[h], left[o], state, query_sketch))]
    ppermute x6, starting transfers between devices: 1.85 us -> 3.8 us  [on_device(): left[o] = lax.ppermute(left[o], 'fsdp', left_way)]
    ppermute x6, starting transfers between devices: 11.4 us -> 9.44 us  [on_device(): right[h] = lax.ppermute(right[h], 'fsdp', right_way)]
    ppermute x4, starting transfers between devices: 4.2 us -> 5.75 us  [the longest x1 2.06 us: on_device(): lax.ppermute(ends[1], 'fsdp', left_way)]
  transfers between devices with their start and end apart: 21 -> 21, of which waited for: 17 -> 16; matrix products, arithmetic and copies ran while one was open for 2% -> 3% of each run, Pallas kernels for 44% -> 43%
where the time goes in v6:
time: 123 us; the launch traced here: 122 us
  Pallas kernels  59.2 us (48%)
  starting transfers between devices  25.3 us (21%)
  waiting for transfers between devices  24.5 us (20%)
  local copies, waits for them, and re-layouts  11 us (9%)
  other arithmetic  1.24 us (1%)
    pallas_call x7, Pallas kernels, absorb(): pl.pallas_call(functools.partial(absorb_kernel, parts, state is None, fin...  45.9 us
    ppermute x6, waiting for transfers between devices, on_device(): left[o] = lax.ppermute(left[o], 'fsdp', left_way)  12 us
    ppermute x6, starting transfers between devices, on_device(): right[h] = lax.ppermute(right[h], 'fsdp', right_way)  9.44 us
    unnamed x22, local copies, waits for them, and re-layouts  7.9 us
    ppermute x4, starting transfers between devices, on_device(): lax.ppermute(low, 'fsdp', [(i, i ^ hop) for i in range(size)])  6.3 us
    pallas_call x2, Pallas kernels, finish(): pl.pallas_call(functools.partial(finish_kernel, examples, seq_len, step,...  5.84 us
    ppermute x6, waiting for transfers between devices, on_device(): right[h] = lax.ppermute(right[h], 'fsdp', right_way)  5.28 us
    ppermute x4, waiting for transfers between devices, on_device(): lax.ppermute(low, 'fsdp', [(i, i ^ hop) for i in range(size)])  4.31 us
  transfers between devices with their start and end apart: 21, of which 16 were waited for; matrix products, arithmetic and copies ran while one was open for 3% of the time, Pallas kernels for 43%

profile of v6, /device:TPU:0, one launch (start us, length us, event | category | flops | bytes accessed | tf_op | source)
XLA Modules:
  0.0 122.2 jit_solution(8067700162952821614)
XLA Ops:
  0.6 3.5 %shard_map.95 = (bf16[640,512]{1,0:T(8,128)(2,1)}, bf16[640,512]{1,0:T(8,128)(2,1)}) custom-call(s32[1,4]{1,0:T(1,128)} %lens.5, bf16[1024,1024]{1,0:T(8,128)(2,1)} %bitcast.26), custom_call_target="tpu_custom_call" | custom-call | flops 1342177280 | bytes 3407872 | tf_op jit(solution)/shard_map/pallas_call | solution.py:109
  4.1 3.1 %collective-permute-start = (bf16[640,512]{1,0:T(8,128)(2,1)}, bf16[640,512]{1,0:T(8,128)(2,1)}, u32[]{:S(2)}, u32[]{:S(2)}) collective-permute-start(bf16[640,512]{1,0:T(8,128)(2,1)} %get-tuple-element.46.refs_0_), channel_id=1, source_target_pairs={{0,2},{2,4},{4,6},{6,7},{7,5},{5,3},{3,1},{1,0},{8,10},{10,12},{12... | collective-permute-start | bytes 1966088 | tf_op jit(solution)/shard_map/ppermute | solution.py:306
  7.2 2.0 %collective-permute-start.5 = (bf16[640,512]{1,0:T(8,128)(2,1)}, bf16[640,512]{1,0:T(8,128)(2,1)S(1)}, u32[]{:S(2)}, u32[]{:S(2)}) collective-permute-start(bf16[640,512]{1,0:T(8,128)(2,1)} %get-tuple-element.46.refs_0_), channel_id=1, source_target_pairs={{2,0},{4,2},{6,4},{7,6},{5,7},{3,5},{1,3},{0,1},{10,8},{12,10},{14... | collective-permute-start | bytes 1966088 | tf_op jit(solution)/shard_map/ppermute | solution.py:307
  9.3 2.0 %copy-done.9 = bf16[4,256,1792]{2,1,0:T(8,128)(2,1)S(1)} copy-done((bf16[4,256,1792]{2,1,0:T(8,128)(2,1)S(1)}, bf16[4,256,1792]{2,1,0:T(8,128)(2,1)}, u32[]{:S(2)}) %copy-start.9) | copy-done | bytes 3670040
  11.3 3.2 %shard_map.97.refs_6_ = bf16[640,1792]{1,0:T(8,128)(2,1)S(1)} custom-call(s32[1,4]{1,0:T(1,128)S(1)} %copy-done.8, bf16[1024,1792]{1,0:T(8,128)(2,1)S(1)} %bitcast.24), custom_call_target="tpu_custom_call" | custom-call | flops 2348810240 | bytes 5963776 | tf_op jit(solution)/shard_map/pallas_call | solution.py:60
  16.7 5.6 %shard_map.96 = (f32[640,1792]{1,0:T(8,128)S(1)}, f32[640,64]{1,0:T(8,128)S(1)}) custom-call(s32[8]{0:T(128)S(1)} %dynamic-slice_bitcast_fusion.where, bf16[640,512]{1,0:T(8,128)(2,1)S(1)} %copy-done.7, bf16[640,512]{1,0:T(8,128)(2,1)S(1)} %copy-done.6, bf16[8192,1792]{1,0:T(8,128)(2,1)} %refs_2_.13, bf16[64,8192]{1,0:T(8,128)(2,1)S(1)} %bitcast.13), custom_call_target="tpu_custom_call" | custom-call | flops 2684354560 | bytes 14155776 | tf_op jit(solution)/shard_map/pallas_call | solution.py:178
  23.0 2.2 %collective-permute-done.1.refs_1_ = bf16[640,512]{1,0:T(8,128)(2,1)} collective-permute-done((bf16[640,512]{1,0:T(8,128)(2,1)}, bf16[640,512]{1,0:T(8,128)(2,1)}, u32[]{:S(2)}, u32[]{:S(2)}) %collective-permute-start.1) | collective-permute-done | bytes 655392 | tf_op jit(solution)/shard_map/ppermute | solution.py:307
  25.2 1.6 %collective-permute-start.2 = (bf16[640,512]{1,0:T(8,128)(2,1)}, bf16[640,512]{1,0:T(8,128)(2,1)}, u32[]{:S(2)}, u32[]{:S(2)}) collective-permute-start(bf16[640,512]{1,0:T(8,128)(2,1)} %collective-permute-done.refs_0_), channel_id=1, source_target_pairs={{0,2},{2,4},{4,6},{6,7},{7,5},{5,3},{3,1},{1,0},{8,10},{10,12},{12... | collective-permute-start | bytes 1966088 | tf_op jit(solution)/shard_map/ppermute | solution.py:306
  27.2 7.0 %shard_map.98 = (f32[640,1792]{1,0:T(8,128)S(1)}, f32[640,64]{1,0:T(8,128)S(1)}) custom-call(s32[8]{0:T(128)S(1)} %dynamic-slice_bitcast_fusion.where, bf16[640,512]{1,0:T(8,128)(2,1)} %collective-permute-done.refs_0_, bf16[640,512]{1,0:T(8,128)(2,1)} %collective-permute-done.1.refs_1_, ...), custom_call_target="tpu_custom_call", output_to_operand_aliasing={{0}: (5, {}), {1}: (6, {})} | custom-call | flops 2684354560 | bytes 14155776 | tf_op jit(solution)/shard_map/pallas_call | solution.py:178
  34.3 4.9 %collective-permute-done.5.refs_1_ = bf16[640,512]{1,0:T(8,128)(2,1)S(1)} collective-permute-done((bf16[640,512]{1,0:T(8,128)(2,1)}, bf16[640,512]{1,0:T(8,128)(2,1)S(1)}, u32[]{:S(2)}, u32[]{:S(2)}) %collective-permute-start.5) | collective-permute-done | bytes 655392 | tf_op jit(solution)/shard_map/ppermute | solution.py:307
  39.1 1.6 %collective-permute-start.8 = (bf16[640,512]{1,0:T(8,128)(2,1)}, bf16[640,512]{1,0:T(8,128)(2,1)}, u32[]{:S(2)}, u32[]{:S(2)}) collective-permute-start(bf16[640,512]{1,0:T(8,128)(2,1)} %collective-permute-done.4.refs_0_), channel_id=1, source_target_pairs={{0,2},{2,4},{4,6},{6,7},{7,5},{5,3},{3,1},{1,0},{8,10},{10,12},{12... | collective-permute-start | bytes 1966088 | tf_op jit(solution)/shard_map/ppermute | solution.py:306
  41.2 6.7 %shard_map.99 = (f32[640,1792]{1,0:T(8,128)S(1)}, f32[640,64]{1,0:T(8,128)S(1)}) custom-call(s32[8]{0:T(128)S(1)} %dynamic-slice_bitcast_fusion.where, bf16[640,512]{1,0:T(8,128)(2,1)} %collective-permute-done.4.refs_0_, bf16[640,512]{1,0:T(8,128)(2,1)S(1)} %collective-permute-done.5.refs_1_, ...), custom_call_target="tpu_custom_call", output_to_operand_aliasing={{0}: (5, {}), {1}: (6, {})} | custom-call | flops 2684354560 | bytes 14155776 | tf_op jit(solution)/shard_map/pallas_call | solution.py:178
  47.9 2.1 %copy-done = f32[640,1792]{1,0:T(8,128)} copy-done((f32[640,1792]{1,0:T(8,128)}, f32[640,1792]{1,0:T(8,128)S(1)}, u32[]{:S(2)}) %copy-start) | copy-done | bytes 4587544
  51.1 2.2 %collective-permute-done.3.refs_1_ = bf16[640,512]{1,0:T(8,128)(2,1)} collective-permute-done((bf16[640,512]{1,0:T(8,128)(2,1)}, bf16[640,512]{1,0:T(8,128)(2,1)}, u32[]{:S(2)}, u32[]{:S(2)}) %collective-permute-start.3) | collective-permute-done | bytes 655392 | tf_op jit(solution)/shard_map/ppermute | solution.py:307
  53.3 2.1 %copy.23 = bf16[128,2048]{0,1:T(8,128)(2,1)} copy(bf16[128,2048]{1,0:T(8,128)(2,1)} %param.14) | data formatting | bytes 1048576 | tf_op jit(solution)/shard_map/optimization_barrier | solution.py:300
  55.4 1.6 %collective-permute-start.6 = (bf16[640,512]{1,0:T(8,128)(2,1)}, bf16[640,512]{1,0:T(8,128)(2,1)S(1)}, u32[]{:S(2)}, u32[]{:S(2)}) collective-permute-start(bf16[640,512]{1,0:T(8,128)(2,1)} %collective-permute-done.2.refs_0_), channel_id=1, source_target_pairs={{0,2},{2,4},{4,6},{6,7},{7,5},{5,3},{3,1},{1,0},{8,10},{10,12},{12... | collective-permute-start | bytes 1966088 | tf_op jit(solution)/shard_map/ppermute | solution.py:306
  57.4 2.3 %copy-done.1 = f32[640,1792]{1,0:T(8,128)S(1)} copy-done((f32[640,1792]{1,0:T(8,128)S(1)}, f32[640,1792]{1,0:T(8,128)}, u32[]{:S(2)}) %copy-start.1) | copy-done | bytes 4587544
  59.7 7.0 %shard_map.100 = (f32[640,1792]{1,0:T(8,128)S(1)}, f32[640,64]{1,0:T(8,128)S(1)}) custom-call(s32[8]{0:T(128)S(1)} %dynamic-slice_bitcast_fusion.where, bf16[640,512]{1,0:T(8,128)(2,1)} %collective-permute-done.2.refs_0_, bf16[640,512]{1,0:T(8,128)(2,1)} %collective-permute-done.3.refs_1_, ...), custom_call_target="tpu_custom_call", output_to_operand_aliasing={{0}: (5, {}), {1}: (6, {})} | custom-call | flops 2684354560 | bytes 14155776 | tf_op jit(solution)/shard_map/pallas_call | solution.py:178
  69.3 6.7 %shard_map.101 = (f32[640,1792]{1,0:T(8,128)S(1)}, f32[640,64]{1,0:T(8,128)S(1)}) custom-call(s32[8]{0:T(128)S(1)} %dynamic-slice_bitcast_fusion.where, bf16[640,512]{1,0:T(8,128)(2,1)} %collective-permute-done.8.refs_0_, bf16[640,512]{1,0:T(8,128)(2,1)S(1)} %collective-permute-done.9.refs_1_, ...), custom_call_target="tpu_custom_call", output_to_operand_aliasing={{0}: (5, {}), {1}: (6, {})} | custom-call | flops 2684354560 | bytes 14155776 | tf_op jit(solution)/shard_map/pallas_call | solution.py:178
  77.2 1.9 %collective-permute-done.6.refs_0_ = bf16[640,512]{1,0:T(8,128)(2,1)S(1)} collective-permute-done((bf16[640,512]{1,0:T(8,128)(2,1)}, bf16[640,512]{1,0:T(8,128)(2,1)S(1)}, u32[]{:S(2)}, u32[]{:S(2)}) %collective-permute-start.6) | collective-permute-done | bytes 655392 | tf_op jit(solution)/shard_map/ppermute | solution.py:306
  79.1 2.2 %collective-permute-done.7.refs_1_ = bf16[640,512]{1,0:T(8,128)(2,1)S(1)} collective-permute-done((bf16[640,512]{1,0:T(8,128)(2,1)}, bf16[640,512]{1,0:T(8,128)(2,1)S(1)}, u32[]{:S(2)}, u32[]{:S(2)}) %collective-permute-start.7) | collective-permute-done | bytes 655392 | tf_op jit(solution)/shard_map/ppermute | solution.py:307
  81.5 2.0 %collective-permute-start.15 = (bf16[384,512]{1,0:T(8,128)(2,1)S(1)}, bf16[384,512]{1,0:T(8,128)(2,1)S(1)}, u32[]{:S(2)}, u32[]{:S(2)}) collective-permute-start(bf16[384,512]{1,0:T(8,128)(2,1)S(1)} %slice.14), channel_id=1, source_target_pairs={{0,2},{2,4},{4,6},{6,7},{7,5},{5,3},{3,1},{1,0},{8,10},{10,12},{12... | collective-permute-start | bytes 1179656 | tf_op jit(solution)/shard_map/ppermute | solution.py:324
  83.5 6.5 %shard_map.102 = (f32[640,1792]{1,0:T(8,128)S(1)}, f32[640,64]{1,0:T(8,128)S(1)}) custom-call(s32[8]{0:T(128)S(1)} %dynamic-slice_bitcast_fusion.where, bf16[640,512]{1,0:T(8,128)(2,1)S(1)} %collective-permute-done.6.refs_0_, bf16[640,512]{1,0:T(8,128)(2,1)S(1)} %collective-permute-done.7.refs_1_, ...), custom_call_target="tpu_custom_call", output_to_operand_aliasing={{0}: (5, {}), {1}: (6, {})} | custom-call | flops 2684354560 | bytes 14155776 | tf_op jit(solution)/shard_map/pallas_call | solution.py:178
  90.0 1.6 %collective-permute-start.11 = (bf16[256,512]{1,0:T(8,128)(2,1)S(1)}, bf16[256,512]{1,0:T(8,128)(2,1)S(1)}, u32[]{:S(2)}, u32[]{:S(2)}) collective-permute-start(bf16[256,512]{1,0:T(8,128)(2,1)S(1)} %slice.12), channel_id=1, source_target_pairs={{0,2},{2,4},{4,6},{6,7},{7,5},{5,3},{3,1},{1,0},{8,10},{10,12},{12... | collective-permute-start | bytes 786440 | tf_op jit(solution)/shard_map/ppermute | solution.py:331
  93.2 2.1 %collective-permute-start.12 = (bf16[256,512]{1,0:T(8,128)(2,1)S(1)}, bf16[256,512]{1,0:T(8,128)(2,1)S(1)}, u32[]{:S(2)}, u32[]{:S(2)}) collective-permute-start(bf16[256,512]{1,0:T(8,128)(2,1)S(1)} %slice.13), channel_id=1, source_target_pairs={{2,0},{4,2},{6,4},{7,6},{5,7},{3,5},{1,3},{0,1},{10,8},{12,10},{14... | collective-permute-start | bytes 786440 | tf_op jit(solution)/shard_map/ppermute | solution.py:331
  95.3 6.3 %shard_map.103 = (f32[640,1792]{1,0:T(8,128)S(1)}, f32[640,64]{1,0:T(8,128)S(1)}, bf16[1024,1792]{1,0:T(8,128)(2,1)S(1)}) custom-call(s32[8]{0:T(128)S(1)} %dynamic-slice_bitcast_fusion.where, bf16[640,512]{1,0:T(8,128)(2,1)S(1)} %collective-permute-done.13.refs_0_, ...), custom_call_target="tpu_custom_call", output_to_operand_aliasing={{0}: (5, {}), {1}: (6, {})} | custom-call | flops 2684354560 | bytes 14155776 | tf_op jit(solution)/shard_map/pallas_call | solution.py:178
  101.6 2.2 %collective-permute-done.16.refs_1_ = bf16[384,512]{1,0:T(8,128)(2,1)S(1)} collective-permute-done((bf16[384,512]{1,0:T(8,128)(2,1)S(1)}, bf16[384,512]{1,0:T(8,128)(2,1)S(1)}, u32[]{:S(2)}, u32[]{:S(2)}) %collective-permute-start.16) | collective-permute-done | bytes 393248 | tf_op jit(solution)/shard_map/ppermute | solution.py:324
  103.8 3.3 %shard_map.104.refs_8_ = f32[64,256]{1,0:T(8,128)S(1)} custom-call(s32[8]{0:T(128)S(1)} %dynamic-slice_bitcast_fusion.where, s32[1,4]{1,0:T(1,128)S(1)} %copy-done.8, bf16[384,512]{1,0:T(8,128)(2,1)S(1)} %collective-permute-done.15.refs_0_, bf16[384,512]{1,0:T(8,128)(2,1)S(1)} %collective-permute-done.16.refs_1_, ...), custom_call_target="tpu_custom_call" | custom-call | flops 2013265920 | bytes 8585216 | tf_op jit(solution)/shard_map/pallas_call | solution.py:233
  107.9 2.5 %shard_map.105 = f32[64,256]{1,0:T(8,128)S(1)} custom-call(s32[8]{0:T(128)S(1)} %dynamic-slice_bitcast_fusion.where, s32[1,4]{1,0:T(1,128)S(1)} %copy-done.8, bf16[256,512]{1,0:T(8,128)(2,1)S(1)} %collective-permute-done.11.refs_0_, bf16[256,512]{1,0:T(8,128)(2,1)S(1)} %collective-permute-done.12.refs_1_, bf16[1024,1792]{1,0:T(8,128)(2,1)S(1)} %get-tuple-element.85.refs_2_, ...), custom_call_target="tpu_custom_call" | custom-call | flops 1342177280 | bytes 6946816 | tf_op jit(solution)/shard_map/pallas_call | solution.py:233
  112.3 1.7 %collective-permute-start.17 = (bf16[64,256]{1,0:T(8,128)(2,1)S(1)}, bf16[64,256]{1,0:T(8,128)(2,1)S(1)}, u32[]{:S(2)}, u32[]{:S(2)}) collective-permute-start(bf16[64,256]{1,0:T(8,128)(2,1)S(1)} %convert_element_type.18), channel_id=1, source_target_pairs={{0,1},{1,0},{2,3},{3,2},{4,5},{5,4},{6,7},{7,6},{8,9},{9,8},{10,11... | collective-permute-start | bytes 98312 | tf_op jit(solution)/shard_map/ppermute | solution.py:341
  116.2 2.8 %collective-permute-start.20 = (bf16[64,256]{1,0:T(8,128)(2,1)S(1)}, bf16[64,256]{1,0:T(8,128)(2,1)S(1)}, u32[]{:S(2)}, u32[]{:S(2)}) collective-permute-start(bf16[64,256]{1,0:T(8,128)(2,1)S(1)} %fusion), channel_id=1, source_target_pairs={{0,4},{1,5},{2,6},{3,7},{4,0},{5,1},{6,2},{7,3},{8,12},{9,13},{10,... | collective-permute-start | bytes 98312 | tf_op jit(solution)/shard_map/ppermute | solution.py:341
  119.0 2.1 %collective-permute-done.20 = bf16[64,256]{1,0:T(8,128)(2,1)S(1)} collective-permute-done((bf16[64,256]{1,0:T(8,128)(2,1)S(1)}, bf16[64,256]{1,0:T(8,128)(2,1)S(1)}, u32[]{:S(2)}, u32[]{:S(2)}) %collective-permute-start.20) | collective-permute-done | bytes 32800 | tf_op jit(solution)/shard_map/ppermute | solution.py:341
  (58 shorter events, 16.9 us)
Async XLA Ops:
  0.6 8.7 %copy-start.8 = (s32[1,4]{1,0:T(1,128)S(1)}, s32[1,4]{1,0:T(1,128)}, u32[]{:S(2)}) copy-start(s32[1,4]{1,0:T(1,128)} %lens.5) | copy-start | bytes 52
  4.1 12.6 %copy-start.2 = (bf16[8192,64]{0,1:T(8,128)(2,1)S(1)}, bf16[8192,64]{0,1:T(8,128)(2,1)}, u32[]{:S(2)}) copy-start(bf16[8192,64]{0,1:T(8,128)(2,1)} %param.12) | copy-start | bytes 3145732
  4.1 12.6 %copy-start.6 = (bf16[640,512]{1,0:T(8,128)(2,1)S(1)}, bf16[640,512]{1,0:T(8,128)(2,1)}, u32[]{:S(2)}) copy-start(bf16[640,512]{1,0:T(8,128)(2,1)} %get-tuple-element.47.refs_1_) | copy-start | bytes 1966084
  4.1 12.6 %copy-start.7 = (bf16[640,512]{1,0:T(8,128)(2,1)S(1)}, bf16[640,512]{1,0:T(8,128)(2,1)}, u32[]{:S(2)}) copy-start(bf16[640,512]{1,0:T(8,128)(2,1)} %get-tuple-element.46.refs_0_) | copy-start | bytes 1966084
  4.1 18.9 %collective-permute-start = (bf16[640,512]{1,0:T(8,128)(2,1)}, bf16[640,512]{1,0:T(8,128)(2,1)}, u32[]{:S(2)}, u32[]{:S(2)}) collective-permute-start(bf16[640,512]{1,0:T(8,128)(2,1)} %get-tuple-element.46.refs_0_), channel_id=1, source_target_pairs={{0,2},{2,4},{4,6},{6,7},{7,5},{5,3},{3,1},{1,0},{8,10},{10,12},{12... | collective-permute-start | bytes 1966088 | tf_op jit(solution)/shard_map/ppermute | solution.py:306
  7.2 18.0 %collective-permute-start.1 = (bf16[640,512]{1,0:T(8,128)(2,1)}, bf16[640,512]{1,0:T(8,128)(2,1)}, u32[]{:S(2)}, u32[]{:S(2)}) collective-permute-start(bf16[640,512]{1,0:T(8,128)(2,1)} %get-tuple-element.47.refs_1_), channel_id=1, source_target_pairs={{2,0},{4,2},{6,4},{7,6},{5,7},{3,5},{1,3},{0,1},{10,8},{12,10},{14... | collective-permute-start | bytes 1966088 | tf_op jit(solution)/shard_map/ppermute | solution.py:307
  7.2 31.9 %collective-permute-start.5 = (bf16[640,512]{1,0:T(8,128)(2,1)}, bf16[640,512]{1,0:T(8,128)(2,1)S(1)}, u32[]{:S(2)}, u32[]{:S(2)}) collective-permute-start(bf16[640,512]{1,0:T(8,128)(2,1)} %get-tuple-element.46.refs_0_), channel_id=1, source_target_pairs={{2,0},{4,2},{6,4},{7,6},{5,7},{3,5},{1,3},{0,1},{10,8},{12,10},{14... | collective-permute-start | bytes 1966088 | tf_op jit(solution)/shard_map/ppermute | solution.py:307
  9.2 30.0 %collective-permute-start.4 = (bf16[640,512]{1,0:T(8,128)(2,1)}, bf16[640,512]{1,0:T(8,128)(2,1)}, u32[]{:S(2)}, u32[]{:S(2)}) collective-permute-start(bf16[640,512]{1,0:T(8,128)(2,1)} %get-tuple-element.47.refs_1_), channel_id=1, source_target_pairs={{0,2},{2,4},{4,6},{6,7},{7,5},{5,3},{3,1},{1,0},{8,10},{10,12},{12... | collective-permute-start | bytes 1966088 | tf_op jit(solution)/shard_map/ppermute | solution.py:306
  9.3 2.0 %copy-start.9 = (bf16[4,256,1792]{2,1,0:T(8,128)(2,1)S(1)}, bf16[4,256,1792]{2,1,0:T(8,128)(2,1)}, u32[]{:S(2)}) copy-start(bf16[4,256,1792]{2,1,0:T(8,128)(2,1)} %param.11) | copy-start | bytes 11010052
  14.6 1.4 %copy-start.3 = (bf16[640,1792]{1,0:T(8,128)(2,1)}, bf16[640,1792]{1,0:T(8,128)(2,1)S(1)}, u32[]{:S(2)}) copy-start(bf16[640,1792]{1,0:T(8,128)(2,1)S(1)} %shard_map.97.refs_6_) | copy-start | bytes 6881284
  25.2 25.9 %collective-permute-start.2 = (bf16[640,512]{1,0:T(8,128)(2,1)}, bf16[640,512]{1,0:T(8,128)(2,1)}, u32[]{:S(2)}, u32[]{:S(2)}) collective-permute-start(bf16[640,512]{1,0:T(8,128)(2,1)} %collective-permute-done.refs_0_), channel_id=1, source_target_pairs={{0,2},{2,4},{4,6},{6,7},{7,5},{5,3},{3,1},{1,0},{8,10},{10,12},{12... | collective-permute-start | bytes 1966088 | tf_op jit(solution)/shard_map/ppermute | solution.py:306
  26.8 26.5 %collective-permute-start.3 = (bf16[640,512]{1,0:T(8,128)(2,1)}, bf16[640,512]{1,0:T(8,128)(2,1)}, u32[]{:S(2)}, u32[]{:S(2)}) collective-permute-start(bf16[640,512]{1,0:T(8,128)(2,1)} %collective-permute-done.1.refs_1_), channel_id=1, source_target_pairs={{2,0},{4,2},{6,4},{7,6},{5,7},{3,5},{1,3},{0,1},{10,8},{12,10},{14... | collective-permute-start | bytes 1966088 | tf_op jit(solution)/shard_map/ppermute | solution.py:307
  39.1 27.6 %collective-permute-start.8 = (bf16[640,512]{1,0:T(8,128)(2,1)}, bf16[640,512]{1,0:T(8,128)(2,1)}, u32[]{:S(2)}, u32[]{:S(2)}) collective-permute-start(bf16[640,512]{1,0:T(8,128)(2,1)} %collective-permute-done.4.refs_0_), channel_id=1, source_target_pairs={{0,2},{2,4},{4,6},{6,7},{7,5},{5,3},{3,1},{1,0},{8,10},{10,12},{12... | collective-permute-start | bytes 1966088 | tf_op jit(solution)/shard_map/ppermute | solution.py:306
  40.7 26.5 %collective-permute-start.9 = (bf16[640,512]{1,0:T(8,128)(2,1)S(1)}, bf16[640,512]{1,0:T(8,128)(2,1)S(1)}, u32[]{:S(2)}, u32[]{:S(2)}) collective-permute-start(bf16[640,512]{1,0:T(8,128)(2,1)S(1)} %collective-permute-done.5.refs_1_), channel_id=1, source_target_pairs={{2,0},{4,2},{6,4},{7,6},{5,7},{3,5},{1,3},{0,1},{10,8},{12,10},{14... | collective-permute-start | bytes 1966088 | tf_op jit(solution)/shard_map/ppermute | solution.py:307
  47.9 2.1 %copy-start = (f32[640,1792]{1,0:T(8,128)}, f32[640,1792]{1,0:T(8,128)S(1)}, u32[]{:S(2)}) copy-start(f32[640,1792]{1,0:T(8,128)S(1)} %get-tuple-element.64.refs_4_) | copy-start | bytes 13762564
  55.4 20.7 %collective-permute-start.10 = (bf16[128,2048]{0,1:T(8,128)(2,1)}, bf16[128,2048]{0,1:T(8,128)(2,1)}, u32[]{:S(2)}, u32[]{:S(2)}) collective-permute-start(bf16[128,2048]{0,1:T(8,128)(2,1)} %copy.23), channel_id=1, source_target_pairs={{0,8},{8,0},{1,9},{9,1},{2,10},{10,2},{3,11},{11,3},{4,12},{12,4},... | collective-permute-start | bytes 1572872 | tf_op jit(solution)/shard_map/ppermute | solution.py:315
  55.4 23.8 %collective-permute-start.6 = (bf16[640,512]{1,0:T(8,128)(2,1)}, bf16[640,512]{1,0:T(8,128)(2,1)S(1)}, u32[]{:S(2)}, u32[]{:S(2)}) collective-permute-start(bf16[640,512]{1,0:T(8,128)(2,1)} %collective-permute-done.2.refs_0_), channel_id=1, source_target_pairs={{0,2},{2,4},{4,6},{6,7},{7,5},{5,3},{3,1},{1,0},{8,10},{10,12},{12... | collective-permute-start | bytes 1966088 | tf_op jit(solution)/shard_map/ppermute | solution.py:306
  56.9 24.4 %collective-permute-start.7 = (bf16[640,512]{1,0:T(8,128)(2,1)}, bf16[640,512]{1,0:T(8,128)(2,1)S(1)}, u32[]{:S(2)}, u32[]{:S(2)}) collective-permute-start(bf16[640,512]{1,0:T(8,128)(2,1)} %collective-permute-done.3.refs_1_), channel_id=1, source_target_pairs={{2,0},{4,2},{6,4},{7,6},{5,7},{3,5},{1,3},{0,1},{10,8},{12,10},{14... | collective-permute-start | bytes 1966088 | tf_op jit(solution)/shard_map/ppermute | solution.py:307
  57.4 2.3 %copy-start.1 = (f32[640,1792]{1,0:T(8,128)S(1)}, f32[640,1792]{1,0:T(8,128)}, u32[]{:S(2)}) copy-start(f32[640,1792]{1,0:T(8,128)} %copy-done) | copy-start | bytes 13762564
  67.2 8.8 %copy-start.10 = (bf16[128,2048]{0,1:T(8,128)(2,1)S(1)}, bf16[128,2048]{0,1:T(8,128)(2,1)}, u32[]{:S(2)}) copy-start(bf16[128,2048]{0,1:T(8,128)(2,1)} %copy.23) | copy-start | bytes 1572868
  67.2 25.9 %collective-permute-start.13 = (bf16[640,512]{1,0:T(8,128)(2,1)}, bf16[640,512]{1,0:T(8,128)(2,1)S(1)}, u32[]{:S(2)}, u32[]{:S(2)}) collective-permute-start(bf16[640,512]{1,0:T(8,128)(2,1)} %collective-permute-done.8.refs_0_), channel_id=1, source_target_pairs={{0,2},{2,4},{4,6},{6,7},{7,5},{5,3},{3,1},{1,0},{8,10},{10,12},{12... | collective-permute-start | bytes 1966088 | tf_op jit(solution)/shard_map/ppermute | solution.py:306
  68.8 26.5 %collective-permute-start.14 = (bf16[640,512]{1,0:T(8,128)(2,1)S(1)}, bf16[640,512]{1,0:T(8,128)(2,1)S(1)}, u32[]{:S(2)}, u32[]{:S(2)}) collective-permute-start(bf16[640,512]{1,0:T(8,128)(2,1)S(1)} %collective-permute-done.9.refs_1_), channel_id=1, source_target_pairs={{2,0},{4,2},{6,4},{7,6},{5,7},{3,5},{1,3},{0,1},{10,8},{12,10},{14... | collective-permute-start | bytes 1966088 | tf_op jit(solution)/shard_map/ppermute | solution.py:307
  81.4 22.4 %collective-permute-start.16 = (bf16[384,512]{1,0:T(8,128)(2,1)S(1)}, bf16[384,512]{1,0:T(8,128)(2,1)S(1)}, u32[]{:S(2)}, u32[]{:S(2)}) collective-permute-start(bf16[384,512]{1,0:T(8,128)(2,1)S(1)} %slice.15), channel_id=1, source_target_pairs={{2,0},{4,2},{6,4},{7,6},{5,7},{3,5},{1,3},{0,1},{10,8},{12,10},{14... | collective-permute-start | bytes 1179656 | tf_op jit(solution)/shard_map/ppermute | solution.py:324
  81.5 22.3 %collective-permute-start.15 = (bf16[384,512]{1,0:T(8,128)(2,1)S(1)}, bf16[384,512]{1,0:T(8,128)(2,1)S(1)}, u32[]{:S(2)}, u32[]{:S(2)}) collective-permute-start(bf16[384,512]{1,0:T(8,128)(2,1)S(1)} %slice.14), channel_id=1, source_target_pairs={{0,2},{2,4},{4,6},{6,7},{7,5},{5,3},{3,1},{1,0},{8,10},{10,12},{12... | collective-permute-start | bytes 1179656 | tf_op jit(solution)/shard_map/ppermute | solution.py:324
  90.0 13.8 %copy-start.4 = (bf16[640,1792]{1,0:T(8,128)(2,1)S(1)}, bf16[640,1792]{1,0:T(8,128)(2,1)}, u32[]{:S(2)}) copy-start(bf16[640,1792]{1,0:T(8,128)(2,1)} %copy-done.3) | copy-start | bytes 6881284
  90.0 13.8 %copy-start.5 = (bf16[1792,64]{0,1:T(8,128)(2,1)S(1)}, bf16[1792,64]{0,1:T(8,128)(2,1)}, u32[]{:S(2)}) copy-start(bf16[1792,64]{0,1:T(8,128)(2,1)} %param.13) | copy-start | bytes 688132
  90.0 17.1 %collective-permute-start.11 = (bf16[256,512]{1,0:T(8,128)(2,1)S(1)}, bf16[256,512]{1,0:T(8,128)(2,1)S(1)}, u32[]{:S(2)}, u32[]{:S(2)}) collective-permute-start(bf16[256,512]{1,0:T(8,128)(2,1)S(1)} %slice.12), channel_id=1, source_target_pairs={{0,2},{2,4},{4,6},{6,7},{7,5},{5,3},{3,1},{1,0},{8,10},{10,12},{12... | collective-permute-start | bytes 786440 | tf_op jit(solution)/shard_map/ppermute | solution.py:331
  93.2 14.7 %collective-permute-start.12 = (bf16[256,512]{1,0:T(8,128)(2,1)S(1)}, bf16[256,512]{1,0:T(8,128)(2,1)S(1)}, u32[]{:S(2)}, u32[]{:S(2)}) collective-permute-start(bf16[256,512]{1,0:T(8,128)(2,1)S(1)} %slice.13), channel_id=1, source_target_pairs={{2,0},{4,2},{6,4},{7,6},{5,7},{3,5},{1,3},{0,1},{10,8},{12,10},{14... | collective-permute-start | bytes 786440 | tf_op jit(solution)/shard_map/ppermute | solution.py:331
  110.4 4.9 %collective-permute-start.19 = (bf16[64,256]{1,0:T(8,128)(2,1)S(1)}, bf16[64,256]{1,0:T(8,128)(2,1)S(1)}, u32[]{:S(2)}, u32[]{:S(2)}) collective-permute-start(bf16[64,256]{1,0:T(8,128)(2,1)S(1)} %convert_element_type.18), channel_id=1, source_target_pairs={{0,3},{1,2},{2,1},{3,0},{4,7},{5,6},{6,5},{7,4},{8,11},{9,10},{10,... | collective-permute-start | bytes 98312 | tf_op jit(solution)/shard_map/ppermute | solution.py:341
  111.9 3.9 %collective-permute-start.18 = (bf16[64,256]{1,0:T(8,128)(2,1)S(1)}, bf16[64,256]{1,0:T(8,128)(2,1)S(1)}, u32[]{:S(2)}, u32[]{:S(2)}) collective-permute-start(bf16[64,256]{1,0:T(8,128)(2,1)S(1)} %convert_element_type.18), channel_id=1, source_target_pairs={{0,2},{1,3},{2,0},{3,1},{4,6},{5,7},{6,4},{7,5},{8,10},{9,11},{10,... | collective-permute-start | bytes 98312 | tf_op jit(solution)/shard_map/ppermute | solution.py:341
  112.3 3.9 %collective-permute-start.17 = (bf16[64,256]{1,0:T(8,128)(2,1)S(1)}, bf16[64,256]{1,0:T(8,128)(2,1)S(1)}, u32[]{:S(2)}, u32[]{:S(2)}) collective-permute-start(bf16[64,256]{1,0:T(8,128)(2,1)S(1)} %convert_element_type.18), channel_id=1, source_target_pairs={{0,1},{1,0},{2,3},{3,2},{4,5},{5,4},{6,7},{7,6},{8,9},{9,8},{10,11... | collective-permute-start | bytes 98312 | tf_op jit(solution)/shard_map/ppermute | solution.py:341
  116.2 4.9 %collective-permute-start.20 = (bf16[64,256]{1,0:T(8,128)(2,1)S(1)}, bf16[64,256]{1,0:T(8,128)(2,1)S(1)}, u32[]{:S(2)}, u32[]{:S(2)}) collective-permute-start(bf16[64,256]{1,0:T(8,128)(2,1)S(1)} %fusion), channel_id=1, source_target_pairs={{0,4},{1,5},{2,6},{3,7},{4,0},{5,1},{6,2},{7,3},{8,12},{9,13},{10,... | collective-permute-start | bytes 98312 | tf_op jit(solution)/shard_map/ppermute | solution.py:341

commit v7 on v6

--- a/solution.py
+++ b/solution.py
@@ -336,9 +336,9 @@
             where, lengths, xs, last_weight, proj_t, state, grads, out_t, total, half, a, examples, seq_len
         )
     for hops in reduce_hops(size):
-        low = total.astype(jnp.bfloat16)
+        held = total
         for hop in hops:
-            total = total + lax.ppermute(low, "fsdp", [(i, i ^ hop) for i in range(size)]).astype(jnp.float32)
+            total = total + lax.ppermute(held, "fsdp", [(i, i ^ hop) for i in range(size)])
     sketch = total.reshape(rank_in, examples, rank_out).transpose(1, 0, 2)
     sketch = sketch.reshape(examples, rank_in * rank_out)
     return score(sketch, queries_t, size)

time: 123 us -> 123 us (level)
  no operation moved by 1% of the time
where the time goes in v7:
time: 123 us
  Pallas kernels  59.2 us (48%)
  starting transfers between devices  25.3 us (21%)
  waiting for transfers between devices  25.2 us (20%)
  local copies, waits for them, and re-layouts  11 us (9%)
    pallas_call x7, Pallas kernels, absorb(): pl.pallas_call(functools.partial(absorb_kernel, parts, state is None, fin...  45.9 us
    ppermute x6, waiting for transfers between devices, on_device(): left[o] = lax.ppermute(left[o], 'fsdp', left_way)  12 us
    ppermute x6, starting transfers between devices, on_device(): right[h] = lax.ppermute(right[h], 'fsdp', right_way)  9.44 us
    unnamed x22, local copies, waits for them, and re-layouts  7.9 us
    ppermute x4, starting transfers between devices, on_device(): lax.ppermute(held, 'fsdp', [(i, i ^ hop) for i in range(size)])  6.3 us
    pallas_call x2, Pallas kernels, finish(): pl.pallas_call(functools.partial(finish_kernel, examples, seq_len, step,...  5.84 us
    ppermute x6, waiting for transfers between devices, on_device(): right[h] = lax.ppermute(right[h], 'fsdp', right_way)  5.28 us
    ppermute x4, waiting for transfers between devices, on_device(): lax.ppermute(held, 'fsdp', [(i, i ^ hop) for i in range(size)])  5.02 us
  transfers between devices with their start and end apart: 21, of which 16 were waited for; matrix products, arithmetic and copies ran while one was open for 3% of the time, Pallas kernels for 43%

profile of v7, /device:TPU:0, one launch (start us, length us, event | category | flops | bytes accessed | tf_op | source)
XLA Modules:
  0.0 122.9 jit_solution(1034483779352358542)
XLA Ops:
  0.6 3.5 %shard_map.95 = (bf16[640,512]{1,0:T(8,128)(2,1)}, bf16[640,512]{1,0:T(8,128)(2,1)}) custom-call(s32[1,4]{1,0:T(1,128)} %lens.5, bf16[1024,1024]{1,0:T(8,128)(2,1)} %bitcast.26), custom_call_target="tpu_custom_call" | custom-call | flops 1342177280 | bytes 3407872 | tf_op jit(solution)/shard_map/pallas_call | solution.py:109
  4.1 3.1 %collective-permute-start = (bf16[640,512]{1,0:T(8,128)(2,1)}, bf16[640,512]{1,0:T(8,128)(2,1)}, u32[]{:S(2)}, u32[]{:S(2)}) collective-permute-start(bf16[640,512]{1,0:T(8,128)(2,1)} %get-tuple-element.46.refs_0_), channel_id=1, source_target_pairs={{0,2},{2,4},{4,6},{6,7},{7,5},{5,3},{3,1},{1,0},{8,10},{10,12},{12... | collective-permute-start | bytes 1966088 | tf_op jit(solution)/shard_map/ppermute | solution.py:306
  7.2 2.0 %collective-permute-start.5 = (bf16[640,512]{1,0:T(8,128)(2,1)}, bf16[640,512]{1,0:T(8,128)(2,1)S(1)}, u32[]{:S(2)}, u32[]{:S(2)}) collective-permute-start(bf16[640,512]{1,0:T(8,128)(2,1)} %get-tuple-element.46.refs_0_), channel_id=1, source_target_pairs={{2,0},{4,2},{6,4},{7,6},{5,7},{3,5},{1,3},{0,1},{10,8},{12,10},{14... | collective-permute-start | bytes 1966088 | tf_op jit(solution)/shard_map/ppermute | solution.py:307
  9.3 2.0 %copy-done.9 = bf16[4,256,1792]{2,1,0:T(8,128)(2,1)S(1)} copy-done((bf16[4,256,1792]{2,1,0:T(8,128)(2,1)S(1)}, bf16[4,256,1792]{2,1,0:T(8,128)(2,1)}, u32[]{:S(2)}) %copy-start.9) | copy-done | bytes 3670040
  11.3 3.2 %shard_map.97.refs_6_ = bf16[640,1792]{1,0:T(8,128)(2,1)S(1)} custom-call(s32[1,4]{1,0:T(1,128)S(1)} %copy-done.8, bf16[1024,1792]{1,0:T(8,128)(2,1)S(1)} %bitcast.24), custom_call_target="tpu_custom_call" | custom-call | flops 2348810240 | bytes 5963776 | tf_op jit(solution)/shard_map/pallas_call | solution.py:60
  16.7 5.6 %shard_map.96 = (f32[640,1792]{1,0:T(8,128)S(1)}, f32[640,64]{1,0:T(8,128)S(1)}) custom-call(s32[8]{0:T(128)S(1)} %dynamic-slice_bitcast_fusion.where, bf16[640,512]{1,0:T(8,128)(2,1)S(1)} %copy-done.7, bf16[640,512]{1,0:T(8,128)(2,1)S(1)} %copy-done.6, bf16[8192,1792]{1,0:T(8,128)(2,1)} %refs_2_.13, bf16[64,8192]{1,0:T(8,128)(2,1)S(1)} %bitcast.13), custom_call_target="tpu_custom_call" | custom-call | flops 2684354560 | bytes 14155776 | tf_op jit(solution)/shard_map/pallas_call | solution.py:178
  23.0 2.2 %collective-permute-done.1.refs_1_ = bf16[640,512]{1,0:T(8,128)(2,1)} collective-permute-done((bf16[640,512]{1,0:T(8,128)(2,1)}, bf16[640,512]{1,0:T(8,128)(2,1)}, u32[]{:S(2)}, u32[]{:S(2)}) %collective-permute-start.1) | collective-permute-done | bytes 655392 | tf_op jit(solution)/shard_map/ppermute | solution.py:307
  25.2 1.6 %collective-permute-start.2 = (bf16[640,512]{1,0:T(8,128)(2,1)}, bf16[640,512]{1,0:T(8,128)(2,1)}, u32[]{:S(2)}, u32[]{:S(2)}) collective-permute-start(bf16[640,512]{1,0:T(8,128)(2,1)} %collective-permute-done.refs_0_), channel_id=1, source_target_pairs={{0,2},{2,4},{4,6},{6,7},{7,5},{5,3},{3,1},{1,0},{8,10},{10,12},{12... | collective-permute-start | bytes 1966088 | tf_op jit(solution)/shard_map/ppermute | solution.py:306
  27.2 7.0 %shard_map.98 = (f32[640,1792]{1,0:T(8,128)S(1)}, f32[640,64]{1,0:T(8,128)S(1)}) custom-call(s32[8]{0:T(128)S(1)} %dynamic-slice_bitcast_fusion.where, bf16[640,512]{1,0:T(8,128)(2,1)} %collective-permute-done.refs_0_, bf16[640,512]{1,0:T(8,128)(2,1)} %collective-permute-done.1.refs_1_, ...), custom_call_target="tpu_custom_call", output_to_operand_aliasing={{0}: (5, {}), {1}: (6, {})} | custom-call | flops 2684354560 | bytes 14155776 | tf_op jit(solution)/shard_map/pallas_call | solution.py:178
  34.3 4.9 %collective-permute-done.5.refs_1_ = bf16[640,512]{1,0:T(8,128)(2,1)S(1)} collective-permute-done((bf16[640,512]{1,0:T(8,128)(2,1)}, bf16[640,512]{1,0:T(8,128)(2,1)S(1)}, u32[]{:S(2)}, u32[]{:S(2)}) %collective-permute-start.5) | collective-permute-done | bytes 655392 | tf_op jit(solution)/shard_map/ppermute | solution.py:307
  39.1 1.6 %collective-permute-start.8 = (bf16[640,512]{1,0:T(8,128)(2,1)}, bf16[640,512]{1,0:T(8,128)(2,1)}, u32[]{:S(2)}, u32[]{:S(2)}) collective-permute-start(bf16[640,512]{1,0:T(8,128)(2,1)} %collective-permute-done.4.refs_0_), channel_id=1, source_target_pairs={{0,2},{2,4},{4,6},{6,7},{7,5},{5,3},{3,1},{1,0},{8,10},{10,12},{12... | collective-permute-start | bytes 1966088 | tf_op jit(solution)/shard_map/ppermute | solution.py:306
  41.2 6.7 %shard_map.99 = (f32[640,1792]{1,0:T(8,128)S(1)}, f32[640,64]{1,0:T(8,128)S(1)}) custom-call(s32[8]{0:T(128)S(1)} %dynamic-slice_bitcast_fusion.where, bf16[640,512]{1,0:T(8,128)(2,1)} %collective-permute-done.4.refs_0_, bf16[640,512]{1,0:T(8,128)(2,1)S(1)} %collective-permute-done.5.refs_1_, ...), custom_call_target="tpu_custom_call", output_to_operand_aliasing={{0}: (5, {}), {1}: (6, {})} | custom-call | flops 2684354560 | bytes 14155776 | tf_op jit(solution)/shard_map/pallas_call | solution.py:178
  47.9 2.1 %copy-done = f32[640,1792]{1,0:T(8,128)} copy-done((f32[640,1792]{1,0:T(8,128)}, f32[640,1792]{1,0:T(8,128)S(1)}, u32[]{:S(2)}) %copy-start) | copy-done | bytes 4587544
  51.1 2.2 %collective-permute-done.3.refs_1_ = bf16[640,512]{1,0:T(8,128)(2,1)} collective-permute-done((bf16[640,512]{1,0:T(8,128)(2,1)}, bf16[640,512]{1,0:T(8,128)(2,1)}, u32[]{:S(2)}, u32[]{:S(2)}) %collective-permute-start.3) | collective-permute-done | bytes 655392 | tf_op jit(solution)/shard_map/ppermute | solution.py:307
  53.3 2.1 %copy.23 = bf16[128,2048]{0,1:T(8,128)(2,1)} copy(bf16[128,2048]{1,0:T(8,128)(2,1)} %param.14) | data formatting | bytes 1048576 | tf_op jit(solution)/shard_map/optimization_barrier | solution.py:300
  57.4 2.3 %copy-done.1 = f32[640,1792]{1,0:T(8,128)S(1)} copy-done((f32[640,1792]{1,0:T(8,128)S(1)}, f32[640,1792]{1,0:T(8,128)}, u32[]{:S(2)}) %copy-start.1) | copy-done | bytes 4587544
  59.7 7.0 %shard_map.100 = (f32[640,1792]{1,0:T(8,128)S(1)}, f32[640,64]{1,0:T(8,128)S(1)}) custom-call(s32[8]{0:T(128)S(1)} %dynamic-slice_bitcast_fusion.where, bf16[640,512]{1,0:T(8,128)(2,1)} %collective-permute-done.2.refs_0_, bf16[640,512]{1,0:T(8,128)(2,1)} %collective-permute-done.3.refs_1_, ...), custom_call_target="tpu_custom_call", output_to_operand_aliasing={{0}: (5, {}), {1}: (6, {})} | custom-call | flops 2684354560 | bytes 14155776 | tf_op jit(solution)/shard_map/pallas_call | solution.py:178
  69.3 6.7 %shard_map.101 = (f32[640,1792]{1,0:T(8,128)S(1)}, f32[640,64]{1,0:T(8,128)S(1)}) custom-call(s32[8]{0:T(128)S(1)} %dynamic-slice_bitcast_fusion.where, bf16[640,512]{1,0:T(8,128)(2,1)} %collective-permute-done.8.refs_0_, bf16[640,512]{1,0:T(8,128)(2,1)S(1)} %collective-permute-done.9.refs_1_, ...), custom_call_target="tpu_custom_call", output_to_operand_aliasing={{0}: (5, {}), {1}: (6, {})} | custom-call | flops 2684354560 | bytes 14155776 | tf_op jit(solution)/shard_map/pallas_call | solution.py:178
  77.2 1.9 %collective-permute-done.6.refs_0_ = bf16[640,512]{1,0:T(8,128)(2,1)S(1)} collective-permute-done((bf16[640,512]{1,0:T(8,128)(2,1)}, bf16[640,512]{1,0:T(8,128)(2,1)S(1)}, u32[]{:S(2)}, u32[]{:S(2)}) %collective-permute-start.6) | collective-permute-done | bytes 655392 | tf_op jit(solution)/shard_map/ppermute | solution.py:306
  79.1 2.2 %collective-permute-done.7.refs_1_ = bf16[640,512]{1,0:T(8,128)(2,1)S(1)} collective-permute-done((bf16[640,512]{1,0:T(8,128)(2,1)}, bf16[640,512]{1,0:T(8,128)(2,1)S(1)}, u32[]{:S(2)}, u32[]{:S(2)}) %collective-permute-start.7) | collective-permute-done | bytes 655392 | tf_op jit(solution)/shard_map/ppermute | solution.py:307
  81.5 2.0 %collective-permute-start.15 = (bf16[384,512]{1,0:T(8,128)(2,1)S(1)}, bf16[384,512]{1,0:T(8,128)(2,1)S(1)}, u32[]{:S(2)}, u32[]{:S(2)}) collective-permute-start(bf16[384,512]{1,0:T(8,128)(2,1)S(1)} %slice.14), channel_id=1, source_target_pairs={{0,2},{2,4},{4,6},{6,7},{7,5},{5,3},{3,1},{1,0},{8,10},{10,12},{12... | collective-permute-start | bytes 1179656 | tf_op jit(solution)/shard_map/ppermute | solution.py:324
  83.5 6.5 %shard_map.102 = (f32[640,1792]{1,0:T(8,128)S(1)}, f32[640,64]{1,0:T(8,128)S(1)}) custom-call(s32[8]{0:T(128)S(1)} %dynamic-slice_bitcast_fusion.where, bf16[640,512]{1,0:T(8,128)(2,1)S(1)} %collective-permute-done.6.refs_0_, bf16[640,512]{1,0:T(8,128)(2,1)S(1)} %collective-permute-done.7.refs_1_, ...), custom_call_target="tpu_custom_call", output_to_operand_aliasing={{0}: (5, {}), {1}: (6, {})} | custom-call | flops 2684354560 | bytes 14155776 | tf_op jit(solution)/shard_map/pallas_call | solution.py:178
  90.0 1.6 %collective-permute-start.11 = (bf16[256,512]{1,0:T(8,128)(2,1)S(1)}, bf16[256,512]{1,0:T(8,128)(2,1)S(1)}, u32[]{:S(2)}, u32[]{:S(2)}) collective-permute-start(bf16[256,512]{1,0:T(8,128)(2,1)S(1)} %slice.12), channel_id=1, source_target_pairs={{0,2},{2,4},{4,6},{6,7},{7,5},{5,3},{3,1},{1,0},{8,10},{10,12},{12... | collective-permute-start | bytes 786440 | tf_op jit(solution)/shard_map/ppermute | solution.py:331
  93.2 2.1 %collective-permute-start.12 = (bf16[256,512]{1,0:T(8,128)(2,1)S(1)}, bf16[256,512]{1,0:T(8,128)(2,1)S(1)}, u32[]{:S(2)}, u32[]{:S(2)}) collective-permute-start(bf16[256,512]{1,0:T(8,128)(2,1)S(1)} %slice.13), channel_id=1, source_target_pairs={{2,0},{4,2},{6,4},{7,6},{5,7},{3,5},{1,3},{0,1},{10,8},{12,10},{14... | collective-permute-start | bytes 786440 | tf_op jit(solution)/shard_map/ppermute | solution.py:331
  95.3 6.3 %shard_map.103 = (f32[640,1792]{1,0:T(8,128)S(1)}, f32[640,64]{1,0:T(8,128)S(1)}, bf16[1024,1792]{1,0:T(8,128)(2,1)S(1)}) custom-call(s32[8]{0:T(128)S(1)} %dynamic-slice_bitcast_fusion.where, bf16[640,512]{1,0:T(8,128)(2,1)S(1)} %collective-permute-done.13.refs_0_, ...), custom_call_target="tpu_custom_call", output_to_operand_aliasing={{0}: (5, {}), {1}: (6, {})} | custom-call | flops 2684354560 | bytes 14155776 | tf_op jit(solution)/shard_map/pallas_call | solution.py:178
  101.6 2.2 %collective-permute-done.16.refs_1_ = bf16[384,512]{1,0:T(8,128)(2,1)S(1)} collective-permute-done((bf16[384,512]{1,0:T(8,128)(2,1)S(1)}, bf16[384,512]{1,0:T(8,128)(2,1)S(1)}, u32[]{:S(2)}, u32[]{:S(2)}) %collective-permute-start.16) | collective-permute-done | bytes 393248 | tf_op jit(solution)/shard_map/ppermute | solution.py:324
  103.8 3.3 %shard_map.104.refs_8_ = f32[64,256]{1,0:T(8,128)S(1)} custom-call(s32[8]{0:T(128)S(1)} %dynamic-slice_bitcast_fusion.where, s32[1,4]{1,0:T(1,128)S(1)} %copy-done.8, bf16[384,512]{1,0:T(8,128)(2,1)S(1)} %collective-permute-done.15.refs_0_, bf16[384,512]{1,0:T(8,128)(2,1)S(1)} %collective-permute-done.16.refs_1_, ...), custom_call_target="tpu_custom_call" | custom-call | flops 2013265920 | bytes 8585216 | tf_op jit(solution)/shard_map/pallas_call | solution.py:233
  107.9 2.5 %shard_map.105 = f32[64,256]{1,0:T(8,128)S(1)} custom-call(s32[8]{0:T(128)S(1)} %dynamic-slice_bitcast_fusion.where, s32[1,4]{1,0:T(1,128)S(1)} %copy-done.8, bf16[256,512]{1,0:T(8,128)(2,1)S(1)} %collective-permute-done.11.refs_0_, bf16[256,512]{1,0:T(8,128)(2,1)S(1)} %collective-permute-done.12.refs_1_, bf16[1024,1792]{1,0:T(8,128)(2,1)S(1)} %get-tuple-element.85.refs_2_, ...), custom_call_target="tpu_custom_call" | custom-call | flops 1342177280 | bytes 6946816 | tf_op jit(solution)/shard_map/pallas_call | solution.py:233
  112.2 1.7 %collective-permute-start.17 = (f32[64,256]{1,0:T(8,128)S(1)}, f32[64,256]{1,0:T(8,128)S(1)}, u32[]{:S(2)}, u32[]{:S(2)}) collective-permute-start(f32[64,256]{1,0:T(8,128)S(1)} %shard_map.105), channel_id=1, source_target_pairs={{0,1},{1,0},{2,3},{3,2},{4,5},{5,4},{6,7},{7,6},{8,9},{9,8},{10,11... | collective-permute-start | bytes 196616 | tf_op jit(solution)/shard_map/ppermute | solution.py:341
  114.0 1.7 %collective-permute-done.19 = f32[64,256]{1,0:T(8,128)S(1)} collective-permute-done((f32[64,256]{1,0:T(8,128)S(1)}, f32[64,256]{1,0:T(8,128)S(1)}, u32[]{:S(2)}, u32[]{:S(2)}) %collective-permute-start.19) | collective-permute-done | bytes 65568 | tf_op jit(solution)/shard_map/ppermute | solution.py:341
  116.5 2.8 %collective-permute-start.20 = (f32[64,256]{1,0:T(8,128)S(1)}, f32[64,256]{1,0:T(8,128)S(1)}, u32[]{:S(2)}, u32[]{:S(2)}) collective-permute-start(f32[64,256]{1,0:T(8,128)S(1)} %add_add_fusion), channel_id=1, source_target_pairs={{0,4},{1,5},{2,6},{3,7},{4,0},{5,1},{6,2},{7,3},{8,12},{9,13},{10,... | collective-permute-start | bytes 196616 | tf_op jit(solution)/shard_map/ppermute | solution.py:341
  119.3 2.5 %collective-permute-done.20 = f32[64,256]{1,0:T(8,128)S(1)} collective-permute-done((f32[64,256]{1,0:T(8,128)S(1)}, f32[64,256]{1,0:T(8,128)S(1)}, u32[]{:S(2)}, u32[]{:S(2)}) %collective-permute-start.20) | collective-permute-done | bytes 65568 | tf_op jit(solution)/shard_map/ppermute | solution.py:341
  (57 shorter events, 17.2 us)
Async XLA Ops:
  0.6 8.7 %copy-start.8 = (s32[1,4]{1,0:T(1,128)S(1)}, s32[1,4]{1,0:T(1,128)}, u32[]{:S(2)}) copy-start(s32[1,4]{1,0:T(1,128)} %lens.5) | copy-start | bytes 52
  4.1 12.6 %copy-start.2 = (bf16[8192,64]{0,1:T(8,128)(2,1)S(1)}, bf16[8192,64]{0,1:T(8,128)(2,1)}, u32[]{:S(2)}) copy-start(bf16[8192,64]{0,1:T(8,128)(2,1)} %param.12) | copy-start | bytes 3145732
  4.1 12.6 %copy-start.6 = (bf16[640,512]{1,0:T(8,128)(2,1)S(1)}, bf16[640,512]{1,0:T(8,128)(2,1)}, u32[]{:S(2)}) copy-start(bf16[640,512]{1,0:T(8,128)(2,1)} %get-tuple-element.47.refs_1_) | copy-start | bytes 1966084
  4.1 12.6 %copy-start.7 = (bf16[640,512]{1,0:T(8,128)(2,1)S(1)}, bf16[640,512]{1,0:T(8,128)(2,1)}, u32[]{:S(2)}) copy-start(bf16[640,512]{1,0:T(8,128)(2,1)} %get-tuple-element.46.refs_0_) | copy-start | bytes 1966084
  4.1 18.9 %collective-permute-start = (bf16[640,512]{1,0:T(8,128)(2,1)}, bf16[640,512]{1,0:T(8,128)(2,1)}, u32[]{:S(2)}, u32[]{:S(2)}) collective-permute-start(bf16[640,512]{1,0:T(8,128)(2,1)} %get-tuple-element.46.refs_0_), channel_id=1, source_target_pairs={{0,2},{2,4},{4,6},{6,7},{7,5},{5,3},{3,1},{1,0},{8,10},{10,12},{12... | collective-permute-start | bytes 1966088 | tf_op jit(solution)/shard_map/ppermute | solution.py:306
  7.2 18.0 %collective-permute-start.1 = (bf16[640,512]{1,0:T(8,128)(2,1)}, bf16[640,512]{1,0:T(8,128)(2,1)}, u32[]{:S(2)}, u32[]{:S(2)}) collective-permute-start(bf16[640,512]{1,0:T(8,128)(2,1)} %get-tuple-element.47.refs_1_), channel_id=1, source_target_pairs={{2,0},{4,2},{6,4},{7,6},{5,7},{3,5},{1,3},{0,1},{10,8},{12,10},{14... | collective-permute-start | bytes 1966088 | tf_op jit(solution)/shard_map/ppermute | solution.py:307
  7.2 31.9 %collective-permute-start.5 = (bf16[640,512]{1,0:T(8,128)(2,1)}, bf16[640,512]{1,0:T(8,128)(2,1)S(1)}, u32[]{:S(2)}, u32[]{:S(2)}) collective-permute-start(bf16[640,512]{1,0:T(8,128)(2,1)} %get-tuple-element.46.refs_0_), channel_id=1, source_target_pairs={{2,0},{4,2},{6,4},{7,6},{5,7},{3,5},{1,3},{0,1},{10,8},{12,10},{14... | collective-permute-start | bytes 1966088 | tf_op jit(solution)/shard_map/ppermute | solution.py:307
  9.2 30.0 %collective-permute-start.4 = (bf16[640,512]{1,0:T(8,128)(2,1)}, bf16[640,512]{1,0:T(8,128)(2,1)}, u32[]{:S(2)}, u32[]{:S(2)}) collective-permute-start(bf16[640,512]{1,0:T(8,128)(2,1)} %get-tuple-element.47.refs_1_), channel_id=1, source_target_pairs={{0,2},{2,4},{4,6},{6,7},{7,5},{5,3},{3,1},{1,0},{8,10},{10,12},{12... | collective-permute-start | bytes 1966088 | tf_op jit(solution)/shard_map/ppermute | solution.py:306
  9.3 2.0 %copy-start.9 = (bf16[4,256,1792]{2,1,0:T(8,128)(2,1)S(1)}, bf16[4,256,1792]{2,1,0:T(8,128)(2,1)}, u32[]{:S(2)}) copy-start(bf16[4,256,1792]{2,1,0:T(8,128)(2,1)} %param.11) | copy-start | bytes 11010052
  14.6 1.4 %copy-start.3 = (bf16[640,1792]{1,0:T(8,128)(2,1)}, bf16[640,1792]{1,0:T(8,128)(2,1)S(1)}, u32[]{:S(2)}) copy-start(bf16[640,1792]{1,0:T(8,128)(2,1)S(1)} %shard_map.97.refs_6_) | copy-start | bytes 6881284
  25.2 25.9 %collective-permute-start.2 = (bf16[640,512]{1,0:T(8,128)(2,1)}, bf16[640,512]{1,0:T(8,128)(2,1)}, u32[]{:S(2)}, u32[]{:S(2)}) collective-permute-start(bf16[640,512]{1,0:T(8,128)(2,1)} %collective-permute-done.refs_0_), channel_id=1, source_target_pairs={{0,2},{2,4},{4,6},{6,7},{7,5},{5,3},{3,1},{1,0},{8,10},{10,12},{12... | collective-permute-start | bytes 1966088 | tf_op jit(solution)/shard_map/ppermute | solution.py:306
  26.8 26.5 %collective-permute-start.3 = (bf16[640,512]{1,0:T(8,128)(2,1)}, bf16[640,512]{1,0:T(8,128)(2,1)}, u32[]{:S(2)}, u32[]{:S(2)}) collective-permute-start(bf16[640,512]{1,0:T(8,128)(2,1)} %collective-permute-done.1.refs_1_), channel_id=1, source_target_pairs={{2,0},{4,2},{6,4},{7,6},{5,7},{3,5},{1,3},{0,1},{10,8},{12,10},{14... | collective-permute-start | bytes 1966088 | tf_op jit(solution)/shard_map/ppermute | solution.py:307
  39.1 27.6 %collective-permute-start.8 = (bf16[640,512]{1,0:T(8,128)(2,1)}, bf16[640,512]{1,0:T(8,128)(2,1)}, u32[]{:S(2)}, u32[]{:S(2)}) collective-permute-start(bf16[640,512]{1,0:T(8,128)(2,1)} %collective-permute-done.4.refs_0_), channel_id=1, source_target_pairs={{0,2},{2,4},{4,6},{6,7},{7,5},{5,3},{3,1},{1,0},{8,10},{10,12},{12... | collective-permute-start | bytes 1966088 | tf_op jit(solution)/shard_map/ppermute | solution.py:306
  40.7 26.5 %collective-permute-start.9 = (bf16[640,512]{1,0:T(8,128)(2,1)S(1)}, bf16[640,512]{1,0:T(8,128)(2,1)S(1)}, u32[]{:S(2)}, u32[]{:S(2)}) collective-permute-start(bf16[640,512]{1,0:T(8,128)(2,1)S(1)} %collective-permute-done.5.refs_1_), channel_id=1, source_target_pairs={{2,0},{4,2},{6,4},{7,6},{5,7},{3,5},{1,3},{0,1},{10,8},{12,10},{14... | collective-permute-start | bytes 1966088 | tf_op jit(solution)/shard_map/ppermute | solution.py:307
  47.9 2.1 %copy-start = (f32[640,1792]{1,0:T(8,128)}, f32[640,1792]{1,0:T(8,128)S(1)}, u32[]{:S(2)}) copy-start(f32[640,1792]{1,0:T(8,128)S(1)} %get-tuple-element.64.refs_4_) | copy-start | bytes 13762564
  55.4 20.7 %collective-permute-start.10 = (bf16[128,2048]{0,1:T(8,128)(2,1)}, bf16[128,2048]{0,1:T(8,128)(2,1)}, u32[]{:S(2)}, u32[]{:S(2)}) collective-permute-start(bf16[128,2048]{0,1:T(8,128)(2,1)} %copy.23), channel_id=1, source_target_pairs={{0,8},{8,0},{1,9},{9,1},{2,10},{10,2},{3,11},{11,3},{4,12},{12,4},... | collective-permute-start | bytes 1572872 | tf_op jit(solution)/shard_map/ppermute | solution.py:315
  55.4 23.8 %collective-permute-start.6 = (bf16[640,512]{1,0:T(8,128)(2,1)}, bf16[640,512]{1,0:T(8,128)(2,1)S(1)}, u32[]{:S(2)}, u32[]{:S(2)}) collective-permute-start(bf16[640,512]{1,0:T(8,128)(2,1)} %collective-permute-done.2.refs_0_), channel_id=1, source_target_pairs={{0,2},{2,4},{4,6},{6,7},{7,5},{5,3},{3,1},{1,0},{8,10},{10,12},{12... | collective-permute-start | bytes 1966088 | tf_op jit(solution)/shard_map/ppermute | solution.py:306
  56.9 24.4 %collective-permute-start.7 = (bf16[640,512]{1,0:T(8,128)(2,1)}, bf16[640,512]{1,0:T(8,128)(2,1)S(1)}, u32[]{:S(2)}, u32[]{:S(2)}) collective-permute-start(bf16[640,512]{1,0:T(8,128)(2,1)} %collective-permute-done.3.refs_1_), channel_id=1, source_target_pairs={{2,0},{4,2},{6,4},{7,6},{5,7},{3,5},{1,3},{0,1},{10,8},{12,10},{14... | collective-permute-start | bytes 1966088 | tf_op jit(solution)/shard_map/ppermute | solution.py:307
  57.4 2.3 %copy-start.1 = (f32[640,1792]{1,0:T(8,128)S(1)}, f32[640,1792]{1,0:T(8,128)}, u32[]{:S(2)}) copy-start(f32[640,1792]{1,0:T(8,128)} %copy-done) | copy-start | bytes 13762564
  67.2 8.8 %copy-start.10 = (bf16[128,2048]{0,1:T(8,128)(2,1)S(1)}, bf16[128,2048]{0,1:T(8,128)(2,1)}, u32[]{:S(2)}) copy-start(bf16[128,2048]{0,1:T(8,128)(2,1)} %copy.23) | copy-start | bytes 1572868
  67.2 25.9 %collective-permute-start.13 = (bf16[640,512]{1,0:T(8,128)(2,1)}, bf16[640,512]{1,0:T(8,128)(2,1)S(1)}, u32[]{:S(2)}, u32[]{:S(2)}) collective-permute-start(bf16[640,512]{1,0:T(8,128)(2,1)} %collective-permute-done.8.refs_0_), channel_id=1, source_target_pairs={{0,2},{2,4},{4,6},{6,7},{7,5},{5,3},{3,1},{1,0},{8,10},{10,12},{12... | collective-permute-start | bytes 1966088 | tf_op jit(solution)/shard_map/ppermute | solution.py:306
  68.8 26.5 %collective-permute-start.14 = (bf16[640,512]{1,0:T(8,128)(2,1)S(1)}, bf16[640,512]{1,0:T(8,128)(2,1)S(1)}, u32[]{:S(2)}, u32[]{:S(2)}) collective-permute-start(bf16[640,512]{1,0:T(8,128)(2,1)S(1)} %collective-permute-done.9.refs_1_), channel_id=1, source_target_pairs={{2,0},{4,2},{6,4},{7,6},{5,7},{3,5},{1,3},{0,1},{10,8},{12,10},{14... | collective-permute-start | bytes 1966088 | tf_op jit(solution)/shard_map/ppermute | solution.py:307
  81.4 22.4 %collective-permute-start.16 = (bf16[384,512]{1,0:T(8,128)(2,1)S(1)}, bf16[384,512]{1,0:T(8,128)(2,1)S(1)}, u32[]{:S(2)}, u32[]{:S(2)}) collective-permute-start(bf16[384,512]{1,0:T(8,128)(2,1)S(1)} %slice.15), channel_id=1, source_target_pairs={{2,0},{4,2},{6,4},{7,6},{5,7},{3,5},{1,3},{0,1},{10,8},{12,10},{14... | collective-permute-start | bytes 1179656 | tf_op jit(solution)/shard_map/ppermute | solution.py:324
  81.5 22.3 %collective-permute-start.15 = (bf16[384,512]{1,0:T(8,128)(2,1)S(1)}, bf16[384,512]{1,0:T(8,128)(2,1)S(1)}, u32[]{:S(2)}, u32[]{:S(2)}) collective-permute-start(bf16[384,512]{1,0:T(8,128)(2,1)S(1)} %slice.14), channel_id=1, source_target_pairs={{0,2},{2,4},{4,6},{6,7},{7,5},{5,3},{3,1},{1,0},{8,10},{10,12},{12... | collective-permute-start | bytes 1179656 | tf_op jit(solution)/shard_map/ppermute | solution.py:324
  90.0 13.8 %copy-start.4 = (bf16[640,1792]{1,0:T(8,128)(2,1)S(1)}, bf16[640,1792]{1,0:T(8,128)(2,1)}, u32[]{:S(2)}) copy-start(bf16[640,1792]{1,0:T(8,128)(2,1)} %copy-done.3) | copy-start | bytes 6881284
  90.0 13.8 %copy-start.5 = (bf16[1792,64]{0,1:T(8,128)(2,1)S(1)}, bf16[1792,64]{0,1:T(8,128)(2,1)}, u32[]{:S(2)}) copy-start(bf16[1792,64]{0,1:T(8,128)(2,1)} %param.13) | copy-start | bytes 688132
  90.0 17.1 %collective-permute-start.11 = (bf16[256,512]{1,0:T(8,128)(2,1)S(1)}, bf16[256,512]{1,0:T(8,128)(2,1)S(1)}, u32[]{:S(2)}, u32[]{:S(2)}) collective-permute-start(bf16[256,512]{1,0:T(8,128)(2,1)S(1)} %slice.12), channel_id=1, source_target_pairs={{0,2},{2,4},{4,6},{6,7},{7,5},{5,3},{3,1},{1,0},{8,10},{10,12},{12... | collective-permute-start | bytes 786440 | tf_op jit(solution)/shard_map/ppermute | solution.py:331
  93.2 14.7 %collective-permute-start.12 = (bf16[256,512]{1,0:T(8,128)(2,1)S(1)}, bf16[256,512]{1,0:T(8,128)(2,1)S(1)}, u32[]{:S(2)}, u32[]{:S(2)}) collective-permute-start(bf16[256,512]{1,0:T(8,128)(2,1)S(1)} %slice.13), channel_id=1, source_target_pairs={{2,0},{4,2},{6,4},{7,6},{5,7},{3,5},{1,3},{0,1},{10,8},{12,10},{14... | collective-permute-start | bytes 786440 | tf_op jit(solution)/shard_map/ppermute | solution.py:331
  110.4 5.2 %collective-permute-start.19 = (f32[64,256]{1,0:T(8,128)S(1)}, f32[64,256]{1,0:T(8,128)S(1)}, u32[]{:S(2)}, u32[]{:S(2)}) collective-permute-start(f32[64,256]{1,0:T(8,128)S(1)} %shard_map.105), channel_id=1, source_target_pairs={{0,3},{1,2},{2,1},{3,0},{4,7},{5,6},{6,5},{7,4},{8,11},{9,10},{10,... | collective-permute-start | bytes 196616 | tf_op jit(solution)/shard_map/ppermute | solution.py:341
  111.9 4.3 %collective-permute-start.18 = (f32[64,256]{1,0:T(8,128)S(1)}, f32[64,256]{1,0:T(8,128)S(1)}, u32[]{:S(2)}, u32[]{:S(2)}) collective-permute-start(f32[64,256]{1,0:T(8,128)S(1)} %shard_map.105), channel_id=1, source_target_pairs={{0,2},{1,3},{2,0},{3,1},{4,6},{5,7},{6,4},{7,5},{8,10},{9,11},{10,... | collective-permute-start | bytes 196616 | tf_op jit(solution)/shard_map/ppermute | solution.py:341
  112.2 4.3 %collective-permute-start.17 = (f32[64,256]{1,0:T(8,128)S(1)}, f32[64,256]{1,0:T(8,128)S(1)}, u32[]{:S(2)}, u32[]{:S(2)}) collective-permute-start(f32[64,256]{1,0:T(8,128)S(1)} %shard_map.105), channel_id=1, source_target_pairs={{0,1},{1,0},{2,3},{3,2},{4,5},{5,4},{6,7},{7,6},{8,9},{9,8},{10,11... | collective-permute-start | bytes 196616 | tf_op jit(solution)/shard_map/ppermute | solution.py:341
  116.5 5.2 %collective-permute-start.20 = (f32[64,256]{1,0:T(8,128)S(1)}, f32[64,256]{1,0:T(8,128)S(1)}, u32[]{:S(2)}, u32[]{:S(2)}) collective-permute-start(f32[64,256]{1,0:T(8,128)S(1)} %add_add_fusion), channel_id=1, source_target_pairs={{0,4},{1,5},{2,6},{3,7},{4,0},{5,1},{6,2},{7,3},{8,12},{9,13},{10,... | collective-permute-start | bytes 196616 | tf_op jit(solution)/shard_map/ppermute | solution.py:341

commit v8 on v6

--- a/solution.py
+++ b/solution.py
@@ -9,7 +9,7 @@
 from jax.sharding import PartitionSpec as P
 
 LIVE = 640
-CUT = 384
+CUT = 416
 WHOLE = 60 << 20
 SMALL = 12 << 20
 LARGE = 38 << 20
@@ -201,6 +201,15 @@
     )(*args)
 
 
+def two_terms(a):
+    high = a.astype(jnp.bfloat16)
+    return high, (a - high.astype(jnp.float32)).astype(jnp.bfloat16)
+
+
+def turned(a, b):
+    return lax.dot_general(a, b, TN, preferred_element_type=jnp.float32)
+
+
 def finish_kernel(examples, seq_len, step, first, where, lens, *refs):
     xs, refs = refs[:2], refs[2:]
     weight, proj_t, gate_in, left_in, grads, out_t, *before, sketch, block = refs
@@ -216,13 +225,12 @@
     _, owner = row_sources(lens, examples, seq_len)
     owner = owner[rows, :]
     weighted = jnp.concatenate([jnp.where(owner == e, right, 0.0) for e in range(examples)], axis=1)
-    term = lax.dot_general(
-        left * (1.0 / math.sqrt(seq_len)),
-        weighted,
-        TN,
-        precision=lax.Precision.HIGHEST,
-        preferred_element_type=jnp.float32,
-    )
+    left = left * (1.0 / math.sqrt(seq_len))
+    rank = left.shape[1]
+    left_high, left_low = two_terms(left)
+    high, low = two_terms(weighted)
+    both = turned(jnp.concatenate([left_high, left_low], axis=1), high)
+    term = both[:rank, :] + both[rank:, :] + turned(left_high, low)
     sketch[...] = before[0][...] + term if before else term
 
 

time: 123 us -> 123 us (level)
  transfers between devices with their start and end apart: 21 -> 21, of which waited for: 16 -> 15; matrix products, arithmetic and copies ran while one was open for 3% -> 3% of each run, Pallas kernels for 43% -> 43%
where the time goes in v8:
time: 123 us; the launch traced here: 122 us
  Pallas kernels  59.1 us (48%)
  starting transfers between devices  25.3 us (21%)
  waiting for transfers between devices  24.4 us (20%)
  local copies, waits for them, and re-layouts  11 us (9%)
  other arithmetic  1.24 us (1%)
    pallas_call x7, Pallas kernels, absorb(): pl.pallas_call(functools.partial(absorb_kernel, parts, state is None, fin...  45.9 us
    ppermute x6, waiting for transfers between devices, on_device(): left[o] = lax.ppermute(left[o], 'fsdp', left_way)  12 us
    ppermute x6, starting transfers between devices, on_device(): right[h] = lax.ppermute(right[h], 'fsdp', right_way)  9.44 us
    unnamed x22, local copies, waits for them, and re-layouts  7.9 us
    ppermute x4, starting transfers between devices, on_device(): lax.ppermute(low, 'fsdp', [(i, i ^ hop) for i in range(size)])  6.31 us
    pallas_call x2, Pallas kernels, finish(): pl.pallas_call(functools.partial(finish_kernel, examples, seq_len, step,...  5.68 us
    ppermute x6, waiting for transfers between devices, on_device(): right[h] = lax.ppermute(right[h], 'fsdp', right_way)  5.28 us
    ppermute x4, waiting for transfers between devices, on_device(): lax.ppermute(low, 'fsdp', [(i, i ^ hop) for i in range(size)])  4.31 us
  transfers between devices with their start and end apart: 21, of which 15 were waited for; matrix products, arithmetic and copies ran while one was open for 3% of the time, Pallas kernels for 43%

profile of v8, /device:TPU:0, one launch (start us, length us, event | category | flops | bytes accessed | tf_op | source)
XLA Modules:
  0.0 121.9 jit_solution(18250522466635973863)
XLA Ops:
  0.6 3.5 %shard_map.95 = (bf16[640,512]{1,0:T(8,128)(2,1)}, bf16[640,512]{1,0:T(8,128)(2,1)}) custom-call(s32[1,4]{1,0:T(1,128)} %lens.5, bf16[1024,1024]{1,0:T(8,128)(2,1)} %bitcast.26), custom_call_target="tpu_custom_call" | custom-call | flops 1342177280 | bytes 3407872 | tf_op jit(solution)/shard_map/pallas_call | solution.py:109
  4.1 3.1 %collective-permute-start = (bf16[640,512]{1,0:T(8,128)(2,1)}, bf16[640,512]{1,0:T(8,128)(2,1)}, u32[]{:S(2)}, u32[]{:S(2)}) collective-permute-start(bf16[640,512]{1,0:T(8,128)(2,1)} %get-tuple-element.46.refs_0_), channel_id=1, source_target_pairs={{0,2},{2,4},{4,6},{6,7},{7,5},{5,3},{3,1},{1,0},{8,10},{10,12},{12... | collective-permute-start | bytes 1966088 | tf_op jit(solution)/shard_map/ppermute | solution.py:314
  7.2 2.0 %collective-permute-start.5 = (bf16[640,512]{1,0:T(8,128)(2,1)}, bf16[640,512]{1,0:T(8,128)(2,1)S(1)}, u32[]{:S(2)}, u32[]{:S(2)}) collective-permute-start(bf16[640,512]{1,0:T(8,128)(2,1)} %get-tuple-element.46.refs_0_), channel_id=1, source_target_pairs={{2,0},{4,2},{6,4},{7,6},{5,7},{3,5},{1,3},{0,1},{10,8},{12,10},{14... | collective-permute-start | bytes 1966088 | tf_op jit(solution)/shard_map/ppermute | solution.py:315
  9.3 2.0 %copy-done.9 = bf16[4,256,1792]{2,1,0:T(8,128)(2,1)S(1)} copy-done((bf16[4,256,1792]{2,1,0:T(8,128)(2,1)S(1)}, bf16[4,256,1792]{2,1,0:T(8,128)(2,1)}, u32[]{:S(2)}) %copy-start.9) | copy-done | bytes 3670040
  11.3 3.2 %shard_map.97.refs_6_ = bf16[640,1792]{1,0:T(8,128)(2,1)S(1)} custom-call(s32[1,4]{1,0:T(1,128)S(1)} %copy-done.8, bf16[1024,1792]{1,0:T(8,128)(2,1)S(1)} %bitcast.24), custom_call_target="tpu_custom_call" | custom-call | flops 2348810240 | bytes 5963776 | tf_op jit(solution)/shard_map/pallas_call | solution.py:60
  16.7 5.6 %shard_map.96 = (f32[640,1792]{1,0:T(8,128)S(1)}, f32[640,64]{1,0:T(8,128)S(1)}) custom-call(s32[8]{0:T(128)S(1)} %dynamic-slice_bitcast_fusion.where, bf16[640,512]{1,0:T(8,128)(2,1)S(1)} %copy-done.7, bf16[640,512]{1,0:T(8,128)(2,1)S(1)} %copy-done.6, bf16[8192,1792]{1,0:T(8,128)(2,1)} %refs_2_.13, bf16[64,8192]{1,0:T(8,128)(2,1)S(1)} %bitcast.13), custom_call_target="tpu_custom_call" | custom-call | flops 2684354560 | bytes 14155776 | tf_op jit(solution)/shard_map/pallas_call | solution.py:178
  23.0 2.2 %collective-permute-done.1.refs_1_ = bf16[640,512]{1,0:T(8,128)(2,1)} collective-permute-done((bf16[640,512]{1,0:T(8,128)(2,1)}, bf16[640,512]{1,0:T(8,128)(2,1)}, u32[]{:S(2)}, u32[]{:S(2)}) %collective-permute-start.1) | collective-permute-done | bytes 655392 | tf_op jit(solution)/shard_map/ppermute | solution.py:315
  25.2 1.6 %collective-permute-start.2 = (bf16[640,512]{1,0:T(8,128)(2,1)}, bf16[640,512]{1,0:T(8,128)(2,1)}, u32[]{:S(2)}, u32[]{:S(2)}) collective-permute-start(bf16[640,512]{1,0:T(8,128)(2,1)} %collective-permute-done.refs_0_), channel_id=1, source_target_pairs={{0,2},{2,4},{4,6},{6,7},{7,5},{5,3},{3,1},{1,0},{8,10},{10,12},{12... | collective-permute-start | bytes 1966088 | tf_op jit(solution)/shard_map/ppermute | solution.py:314
  27.2 7.0 %shard_map.98 = (f32[640,1792]{1,0:T(8,128)S(1)}, f32[640,64]{1,0:T(8,128)S(1)}) custom-call(s32[8]{0:T(128)S(1)} %dynamic-slice_bitcast_fusion.where, bf16[640,512]{1,0:T(8,128)(2,1)} %collective-permute-done.refs_0_, bf16[640,512]{1,0:T(8,128)(2,1)} %collective-permute-done.1.refs_1_, ...), custom_call_target="tpu_custom_call", output_to_operand_aliasing={{0}: (5, {}), {1}: (6, {})} | custom-call | flops 2684354560 | bytes 14155776 | tf_op jit(solution)/shard_map/pallas_call | solution.py:178
  34.3 4.9 %collective-permute-done.5.refs_1_ = bf16[640,512]{1,0:T(8,128)(2,1)S(1)} collective-permute-done((bf16[640,512]{1,0:T(8,128)(2,1)}, bf16[640,512]{1,0:T(8,128)(2,1)S(1)}, u32[]{:S(2)}, u32[]{:S(2)}) %collective-permute-start.5) | collective-permute-done | bytes 655392 | tf_op jit(solution)/shard_map/ppermute | solution.py:315
  39.1 1.6 %collective-permute-start.8 = (bf16[640,512]{1,0:T(8,128)(2,1)}, bf16[640,512]{1,0:T(8,128)(2,1)}, u32[]{:S(2)}, u32[]{:S(2)}) collective-permute-start(bf16[640,512]{1,0:T(8,128)(2,1)} %collective-permute-done.4.refs_0_), channel_id=1, source_target_pairs={{0,2},{2,4},{4,6},{6,7},{7,5},{5,3},{3,1},{1,0},{8,10},{10,12},{12... | collective-permute-start | bytes 1966088 | tf_op jit(solution)/shard_map/ppermute | solution.py:314
  41.2 6.7 %shard_map.99 = (f32[640,1792]{1,0:T(8,128)S(1)}, f32[640,64]{1,0:T(8,128)S(1)}) custom-call(s32[8]{0:T(128)S(1)} %dynamic-slice_bitcast_fusion.where, bf16[640,512]{1,0:T(8,128)(2,1)} %collective-permute-done.4.refs_0_, bf16[640,512]{1,0:T(8,128)(2,1)S(1)} %collective-permute-done.5.refs_1_, ...), custom_call_target="tpu_custom_call", output_to_operand_aliasing={{0}: (5, {}), {1}: (6, {})} | custom-call | flops 2684354560 | bytes 14155776 | tf_op jit(solution)/shard_map/pallas_call | solution.py:178
  47.9 2.1 %copy-done = f32[640,1792]{1,0:T(8,128)} copy-done((f32[640,1792]{1,0:T(8,128)}, f32[640,1792]{1,0:T(8,128)S(1)}, u32[]{:S(2)}) %copy-start) | copy-done | bytes 4587544
  51.1 2.2 %collective-permute-done.3.refs_1_ = bf16[640,512]{1,0:T(8,128)(2,1)} collective-permute-done((bf16[640,512]{1,0:T(8,128)(2,1)}, bf16[640,512]{1,0:T(8,128)(2,1)}, u32[]{:S(2)}, u32[]{:S(2)}) %collective-permute-start.3) | collective-permute-done | bytes 655392 | tf_op jit(solution)/shard_map/ppermute | solution.py:315
  53.3 2.1 %copy.23 = bf16[128,2048]{0,1:T(8,128)(2,1)} copy(bf16[128,2048]{1,0:T(8,128)(2,1)} %param.14) | data formatting | bytes 1048576 | tf_op jit(solution)/shard_map/optimization_barrier | solution.py:308
  55.4 1.6 %collective-permute-start.6 = (bf16[640,512]{1,0:T(8,128)(2,1)}, bf16[640,512]{1,0:T(8,128)(2,1)S(1)}, u32[]{:S(2)}, u32[]{:S(2)}) collective-permute-start(bf16[640,512]{1,0:T(8,128)(2,1)} %collective-permute-done.2.refs_0_), channel_id=1, source_target_pairs={{0,2},{2,4},{4,6},{6,7},{7,5},{5,3},{3,1},{1,0},{8,10},{10,12},{12... | collective-permute-start | bytes 1966088 | tf_op jit(solution)/shard_map/ppermute | solution.py:314
  57.4 2.3 %copy-done.1 = f32[640,1792]{1,0:T(8,128)S(1)} copy-done((f32[640,1792]{1,0:T(8,128)S(1)}, f32[640,1792]{1,0:T(8,128)}, u32[]{:S(2)}) %copy-start.1) | copy-done | bytes 4587544
  59.7 7.0 %shard_map.100 = (f32[640,1792]{1,0:T(8,128)S(1)}, f32[640,64]{1,0:T(8,128)S(1)}) custom-call(s32[8]{0:T(128)S(1)} %dynamic-slice_bitcast_fusion.where, bf16[640,512]{1,0:T(8,128)(2,1)} %collective-permute-done.2.refs_0_, bf16[640,512]{1,0:T(8,128)(2,1)} %collective-permute-done.3.refs_1_, ...), custom_call_target="tpu_custom_call", output_to_operand_aliasing={{0}: (5, {}), {1}: (6, {})} | custom-call | flops 2684354560 | bytes 14155776 | tf_op jit(solution)/shard_map/pallas_call | solution.py:178
  69.3 6.7 %shard_map.101 = (f32[640,1792]{1,0:T(8,128)S(1)}, f32[640,64]{1,0:T(8,128)S(1)}) custom-call(s32[8]{0:T(128)S(1)} %dynamic-slice_bitcast_fusion.where, bf16[640,512]{1,0:T(8,128)(2,1)} %collective-permute-done.8.refs_0_, bf16[640,512]{1,0:T(8,128)(2,1)S(1)} %collective-permute-done.9.refs_1_, ...), custom_call_target="tpu_custom_call", output_to_operand_aliasing={{0}: (5, {}), {1}: (6, {})} | custom-call | flops 2684354560 | bytes 14155776 | tf_op jit(solution)/shard_map/pallas_call | solution.py:178
  77.2 1.9 %collective-permute-done.6.refs_0_ = bf16[640,512]{1,0:T(8,128)(2,1)S(1)} collective-permute-done((bf16[640,512]{1,0:T(8,128)(2,1)}, bf16[640,512]{1,0:T(8,128)(2,1)S(1)}, u32[]{:S(2)}, u32[]{:S(2)}) %collective-permute-start.6) | collective-permute-done | bytes 655392 | tf_op jit(solution)/shard_map/ppermute | solution.py:314
  79.1 2.2 %collective-permute-done.7.refs_1_ = bf16[640,512]{1,0:T(8,128)(2,1)S(1)} collective-permute-done((bf16[640,512]{1,0:T(8,128)(2,1)}, bf16[640,512]{1,0:T(8,128)(2,1)S(1)}, u32[]{:S(2)}, u32[]{:S(2)}) %collective-permute-start.7) | collective-permute-done | bytes 655392 | tf_op jit(solution)/shard_map/ppermute | solution.py:315
  81.5 2.0 %collective-permute-start.15 = (bf16[416,512]{1,0:T(8,128)(2,1)S(1)}, bf16[416,512]{1,0:T(8,128)(2,1)S(1)}, u32[]{:S(2)}, u32[]{:S(2)}) collective-permute-start(bf16[416,512]{1,0:T(8,128)(2,1)S(1)} %slice.14), channel_id=1, source_target_pairs={{0,2},{2,4},{4,6},{6,7},{7,5},{5,3},{3,1},{1,0},{8,10},{10,12},{12... | collective-permute-start | bytes 1277960 | tf_op jit(solution)/shard_map/ppermute | solution.py:332
  83.5 6.5 %shard_map.102 = (f32[640,1792]{1,0:T(8,128)S(1)}, f32[640,64]{1,0:T(8,128)S(1)}) custom-call(s32[8]{0:T(128)S(1)} %dynamic-slice_bitcast_fusion.where, bf16[640,512]{1,0:T(8,128)(2,1)S(1)} %collective-permute-done.6.refs_0_, bf16[640,512]{1,0:T(8,128)(2,1)S(1)} %collective-permute-done.7.refs_1_, ...), custom_call_target="tpu_custom_call", output_to_operand_aliasing={{0}: (5, {}), {1}: (6, {})} | custom-call | flops 2684354560 | bytes 14155776 | tf_op jit(solution)/shard_map/pallas_call | solution.py:178
  90.0 1.6 %collective-permute-start.11 = (bf16[224,512]{1,0:T(8,128)(2,1)S(1)}, bf16[224,512]{1,0:T(8,128)(2,1)S(1)}, u32[]{:S(2)}, u32[]{:S(2)}) collective-permute-start(bf16[224,512]{1,0:T(8,128)(2,1)S(1)} %slice.12), channel_id=1, source_target_pairs={{0,2},{2,4},{4,6},{6,7},{7,5},{5,3},{3,1},{1,0},{8,10},{10,12},{12... | collective-permute-start | bytes 688136 | tf_op jit(solution)/shard_map/ppermute | solution.py:339
  93.2 2.1 %collective-permute-start.12 = (bf16[224,512]{1,0:T(8,128)(2,1)S(1)}, bf16[224,512]{1,0:T(8,128)(2,1)S(1)}, u32[]{:S(2)}, u32[]{:S(2)}) collective-permute-start(bf16[224,512]{1,0:T(8,128)(2,1)S(1)} %slice.13), channel_id=1, source_target_pairs={{2,0},{4,2},{6,4},{7,6},{5,7},{3,5},{1,3},{0,1},{10,8},{12,10},{14... | collective-permute-start | bytes 688136 | tf_op jit(solution)/shard_map/ppermute | solution.py:339
  95.3 6.3 %shard_map.103 = (f32[640,1792]{1,0:T(8,128)S(1)}, f32[640,64]{1,0:T(8,128)S(1)}, bf16[1024,1792]{1,0:T(8,128)(2,1)S(1)}) custom-call(s32[8]{0:T(128)S(1)} %dynamic-slice_bitcast_fusion.where, bf16[640,512]{1,0:T(8,128)(2,1)S(1)} %collective-permute-done.13.refs_0_, ...), custom_call_target="tpu_custom_call", output_to_operand_aliasing={{0}: (5, {}), {1}: (6, {})} | custom-call | flops 2684354560 | bytes 14155776 | tf_op jit(solution)/shard_map/pallas_call | solution.py:178
  101.6 2.9 %collective-permute-done.16.refs_1_ = bf16[416,512]{1,0:T(8,128)(2,1)S(1)} collective-permute-done((bf16[416,512]{1,0:T(8,128)(2,1)S(1)}, bf16[416,512]{1,0:T(8,128)(2,1)S(1)}, u32[]{:S(2)}, u32[]{:S(2)}) %collective-permute-start.16) | collective-permute-done | bytes 426016 | tf_op jit(solution)/shard_map/ppermute | solution.py:332
  104.5 3.4 %shard_map.104.refs_8_ = f32[64,256]{1,0:T(8,128)S(1)} custom-call(s32[8]{0:T(128)S(1)} %dynamic-slice_bitcast_fusion.where, s32[1,4]{1,0:T(1,128)S(1)} %copy-done.8, bf16[416,512]{1,0:T(8,128)(2,1)S(1)} %collective-permute-done.15.refs_0_, bf16[416,512]{1,0:T(8,128)(2,1)S(1)} %collective-permute-done.16.refs_1_, ...), custom_call_target="tpu_custom_call" | custom-call | flops 2181038080 | bytes 8994816 | tf_op jit(solution)/shard_map/pallas_call | solution.py:241
  107.9 2.3 %shard_map.105 = f32[64,256]{1,0:T(8,128)S(1)} custom-call(s32[8]{0:T(128)S(1)} %dynamic-slice_bitcast_fusion.where, s32[1,4]{1,0:T(1,128)S(1)} %copy-done.8, bf16[224,512]{1,0:T(8,128)(2,1)S(1)} %collective-permute-done.11.refs_0_, bf16[224,512]{1,0:T(8,128)(2,1)S(1)} %collective-permute-done.12.refs_1_, bf16[1024,1792]{1,0:T(8,128)(2,1)S(1)} %get-tuple-element.85.refs_2_, ...), custom_call_target="tpu_custom_call" | custom-call | flops 1174405120 | bytes 6537216 | tf_op jit(solution)/shard_map/pallas_call | solution.py:241
  112.0 1.7 %collective-permute-start.17 = (bf16[64,256]{1,0:T(8,128)(2,1)S(1)}, bf16[64,256]{1,0:T(8,128)(2,1)S(1)}, u32[]{:S(2)}, u32[]{:S(2)}) collective-permute-start(bf16[64,256]{1,0:T(8,128)(2,1)S(1)} %convert_element_type.18), channel_id=1, source_target_pairs={{0,1},{1,0},{2,3},{3,2},{4,5},{5,4},{6,7},{7,6},{8,9},{9,8},{10,11... | collective-permute-start | bytes 98312 | tf_op jit(solution)/shard_map/ppermute | solution.py:349
  116.0 2.8 %collective-permute-start.20 = (bf16[64,256]{1,0:T(8,128)(2,1)S(1)}, bf16[64,256]{1,0:T(8,128)(2,1)S(1)}, u32[]{:S(2)}, u32[]{:S(2)}) collective-permute-start(bf16[64,256]{1,0:T(8,128)(2,1)S(1)} %fusion), channel_id=1, source_target_pairs={{0,4},{1,5},{2,6},{3,7},{4,0},{5,1},{6,2},{7,3},{8,12},{9,13},{10,... | collective-permute-start | bytes 98312 | tf_op jit(solution)/shard_map/ppermute | solution.py:349
  118.7 2.1 %collective-permute-done.20 = bf16[64,256]{1,0:T(8,128)(2,1)S(1)} collective-permute-done((bf16[64,256]{1,0:T(8,128)(2,1)S(1)}, bf16[64,256]{1,0:T(8,128)(2,1)S(1)}, u32[]{:S(2)}, u32[]{:S(2)}) %collective-permute-start.20) | collective-permute-done | bytes 32800 | tf_op jit(solution)/shard_map/ppermute | solution.py:349
  (58 shorter events, 16.2 us)
Async XLA Ops:
  0.6 8.7 %copy-start.8 = (s32[1,4]{1,0:T(1,128)S(1)}, s32[1,4]{1,0:T(1,128)}, u32[]{:S(2)}) copy-start(s32[1,4]{1,0:T(1,128)} %lens.5) | copy-start | bytes 52
  4.1 12.6 %copy-start.2 = (bf16[8192,64]{0,1:T(8,128)(2,1)S(1)}, bf16[8192,64]{0,1:T(8,128)(2,1)}, u32[]{:S(2)}) copy-start(bf16[8192,64]{0,1:T(8,128)(2,1)} %param.12) | copy-start | bytes 3145732
  4.1 12.6 %copy-start.6 = (bf16[640,512]{1,0:T(8,128)(2,1)S(1)}, bf16[640,512]{1,0:T(8,128)(2,1)}, u32[]{:S(2)}) copy-start(bf16[640,512]{1,0:T(8,128)(2,1)} %get-tuple-element.47.refs_1_) | copy-start | bytes 1966084
  4.1 12.6 %copy-start.7 = (bf16[640,512]{1,0:T(8,128)(2,1)S(1)}, bf16[640,512]{1,0:T(8,128)(2,1)}, u32[]{:S(2)}) copy-start(bf16[640,512]{1,0:T(8,128)(2,1)} %get-tuple-element.46.refs_0_) | copy-start | bytes 1966084
  4.1 18.9 %collective-permute-start = (bf16[640,512]{1,0:T(8,128)(2,1)}, bf16[640,512]{1,0:T(8,128)(2,1)}, u32[]{:S(2)}, u32[]{:S(2)}) collective-permute-start(bf16[640,512]{1,0:T(8,128)(2,1)} %get-tuple-element.46.refs_0_), channel_id=1, source_target_pairs={{0,2},{2,4},{4,6},{6,7},{7,5},{5,3},{3,1},{1,0},{8,10},{10,12},{12... | collective-permute-start | bytes 1966088 | tf_op jit(solution)/shard_map/ppermute | solution.py:314
  7.2 18.0 %collective-permute-start.1 = (bf16[640,512]{1,0:T(8,128)(2,1)}, bf16[640,512]{1,0:T(8,128)(2,1)}, u32[]{:S(2)}, u32[]{:S(2)}) collective-permute-start(bf16[640,512]{1,0:T(8,128)(2,1)} %get-tuple-element.47.refs_1_), channel_id=1, source_target_pairs={{2,0},{4,2},{6,4},{7,6},{5,7},{3,5},{1,3},{0,1},{10,8},{12,10},{14... | collective-permute-start | bytes 1966088 | tf_op jit(solution)/shard_map/ppermute | solution.py:315
  7.2 31.9 %collective-permute-start.5 = (bf16[640,512]{1,0:T(8,128)(2,1)}, bf16[640,512]{1,0:T(8,128)(2,1)S(1)}, u32[]{:S(2)}, u32[]{:S(2)}) collective-permute-start(bf16[640,512]{1,0:T(8,128)(2,1)} %get-tuple-element.46.refs_0_), channel_id=1, source_target_pairs={{2,0},{4,2},{6,4},{7,6},{5,7},{3,5},{1,3},{0,1},{10,8},{12,10},{14... | collective-permute-start | bytes 1966088 | tf_op jit(solution)/shard_map/ppermute | solution.py:315
  9.2 30.0 %collective-permute-start.4 = (bf16[640,512]{1,0:T(8,128)(2,1)}, bf16[640,512]{1,0:T(8,128)(2,1)}, u32[]{:S(2)}, u32[]{:S(2)}) collective-permute-start(bf16[640,512]{1,0:T(8,128)(2,1)} %get-tuple-element.47.refs_1_), channel_id=1, source_target_pairs={{0,2},{2,4},{4,6},{6,7},{7,5},{5,3},{3,1},{1,0},{8,10},{10,12},{12... | collective-permute-start | bytes 1966088 | tf_op jit(solution)/shard_map/ppermute | solution.py:314
  9.3 2.0 %copy-start.9 = (bf16[4,256,1792]{2,1,0:T(8,128)(2,1)S(1)}, bf16[4,256,1792]{2,1,0:T(8,128)(2,1)}, u32[]{:S(2)}) copy-start(bf16[4,256,1792]{2,1,0:T(8,128)(2,1)} %param.11) | copy-start | bytes 11010052
  14.6 1.4 %copy-start.3 = (bf16[640,1792]{1,0:T(8,128)(2,1)}, bf16[640,1792]{1,0:T(8,128)(2,1)S(1)}, u32[]{:S(2)}) copy-start(bf16[640,1792]{1,0:T(8,128)(2,1)S(1)} %shard_map.97.refs_6_) | copy-start | bytes 6881284
  25.2 25.9 %collective-permute-start.2 = (bf16[640,512]{1,0:T(8,128)(2,1)}, bf16[640,512]{1,0:T(8,128)(2,1)}, u32[]{:S(2)}, u32[]{:S(2)}) collective-permute-start(bf16[640,512]{1,0:T(8,128)(2,1)} %collective-permute-done.refs_0_), channel_id=1, source_target_pairs={{0,2},{2,4},{4,6},{6,7},{7,5},{5,3},{3,1},{1,0},{8,10},{10,12},{12... | collective-permute-start | bytes 1966088 | tf_op jit(solution)/shard_map/ppermute | solution.py:314
  26.8 26.5 %collective-permute-start.3 = (bf16[640,512]{1,0:T(8,128)(2,1)}, bf16[640,512]{1,0:T(8,128)(2,1)}, u32[]{:S(2)}, u32[]{:S(2)}) collective-permute-start(bf16[640,512]{1,0:T(8,128)(2,1)} %collective-permute-done.1.refs_1_), channel_id=1, source_target_pairs={{2,0},{4,2},{6,4},{7,6},{5,7},{3,5},{1,3},{0,1},{10,8},{12,10},{14... | collective-permute-start | bytes 1966088 | tf_op jit(solution)/shard_map/ppermute | solution.py:315
  39.1 27.6 %collective-permute-start.8 = (bf16[640,512]{1,0:T(8,128)(2,1)}, bf16[640,512]{1,0:T(8,128)(2,1)}, u32[]{:S(2)}, u32[]{:S(2)}) collective-permute-start(bf16[640,512]{1,0:T(8,128)(2,1)} %collective-permute-done.4.refs_0_), channel_id=1, source_target_pairs={{0,2},{2,4},{4,6},{6,7},{7,5},{5,3},{3,1},{1,0},{8,10},{10,12},{12... | collective-permute-start | bytes 1966088 | tf_op jit(solution)/shard_map/ppermute | solution.py:314
  40.7 26.5 %collective-permute-start.9 = (bf16[640,512]{1,0:T(8,128)(2,1)S(1)}, bf16[640,512]{1,0:T(8,128)(2,1)S(1)}, u32[]{:S(2)}, u32[]{:S(2)}) collective-permute-start(bf16[640,512]{1,0:T(8,128)(2,1)S(1)} %collective-permute-done.5.refs_1_), channel_id=1, source_target_pairs={{2,0},{4,2},{6,4},{7,6},{5,7},{3,5},{1,3},{0,1},{10,8},{12,10},{14... | collective-permute-start | bytes 1966088 | tf_op jit(solution)/shard_map/ppermute | solution.py:315
  47.9 2.1 %copy-start = (f32[640,1792]{1,0:T(8,128)}, f32[640,1792]{1,0:T(8,128)S(1)}, u32[]{:S(2)}) copy-start(f32[640,1792]{1,0:T(8,128)S(1)} %get-tuple-element.64.refs_4_) | copy-start | bytes 13762564
  55.4 20.7 %collective-permute-start.10 = (bf16[128,2048]{0,1:T(8,128)(2,1)}, bf16[128,2048]{0,1:T(8,128)(2,1)}, u32[]{:S(2)}, u32[]{:S(2)}) collective-permute-start(bf16[128,2048]{0,1:T(8,128)(2,1)} %copy.23), channel_id=1, source_target_pairs={{0,8},{8,0},{1,9},{9,1},{2,10},{10,2},{3,11},{11,3},{4,12},{12,4},... | collective-permute-start | bytes 1572872 | tf_op jit(solution)/shard_map/ppermute | solution.py:323
  55.4 23.8 %collective-permute-start.6 = (bf16[640,512]{1,0:T(8,128)(2,1)}, bf16[640,512]{1,0:T(8,128)(2,1)S(1)}, u32[]{:S(2)}, u32[]{:S(2)}) collective-permute-start(bf16[640,512]{1,0:T(8,128)(2,1)} %collective-permute-done.2.refs_0_), channel_id=1, source_target_pairs={{0,2},{2,4},{4,6},{6,7},{7,5},{5,3},{3,1},{1,0},{8,10},{10,12},{12... | collective-permute-start | bytes 1966088 | tf_op jit(solution)/shard_map/ppermute | solution.py:314
  56.9 24.4 %collective-permute-start.7 = (bf16[640,512]{1,0:T(8,128)(2,1)}, bf16[640,512]{1,0:T(8,128)(2,1)S(1)}, u32[]{:S(2)}, u32[]{:S(2)}) collective-permute-start(bf16[640,512]{1,0:T(8,128)(2,1)} %collective-permute-done.3.refs_1_), channel_id=1, source_target_pairs={{2,0},{4,2},{6,4},{7,6},{5,7},{3,5},{1,3},{0,1},{10,8},{12,10},{14... | collective-permute-start | bytes 1966088 | tf_op jit(solution)/shard_map/ppermute | solution.py:315
  57.4 2.3 %copy-start.1 = (f32[640,1792]{1,0:T(8,128)S(1)}, f32[640,1792]{1,0:T(8,128)}, u32[]{:S(2)}) copy-start(f32[640,1792]{1,0:T(8,128)} %copy-done) | copy-start | bytes 13762564
  67.2 8.8 %copy-start.10 = (bf16[128,2048]{0,1:T(8,128)(2,1)S(1)}, bf16[128,2048]{0,1:T(8,128)(2,1)}, u32[]{:S(2)}) copy-start(bf16[128,2048]{0,1:T(8,128)(2,1)} %copy.23) | copy-start | bytes 1572868
  67.2 25.9 %collective-permute-start.13 = (bf16[640,512]{1,0:T(8,128)(2,1)}, bf16[640,512]{1,0:T(8,128)(2,1)S(1)}, u32[]{:S(2)}, u32[]{:S(2)}) collective-permute-start(bf16[640,512]{1,0:T(8,128)(2,1)} %collective-permute-done.8.refs_0_), channel_id=1, source_target_pairs={{0,2},{2,4},{4,6},{6,7},{7,5},{5,3},{3,1},{1,0},{8,10},{10,12},{12... | collective-permute-start | bytes 1966088 | tf_op jit(solution)/shard_map/ppermute | solution.py:314
  68.8 26.5 %collective-permute-start.14 = (bf16[640,512]{1,0:T(8,128)(2,1)S(1)}, bf16[640,512]{1,0:T(8,128)(2,1)S(1)}, u32[]{:S(2)}, u32[]{:S(2)}) collective-permute-start(bf16[640,512]{1,0:T(8,128)(2,1)S(1)} %collective-permute-done.9.refs_1_), channel_id=1, source_target_pairs={{2,0},{4,2},{6,4},{7,6},{5,7},{3,5},{1,3},{0,1},{10,8},{12,10},{14... | collective-permute-start | bytes 1966088 | tf_op jit(solution)/shard_map/ppermute | solution.py:315
  81.4 23.1 %collective-permute-start.16 = (bf16[416,512]{1,0:T(8,128)(2,1)S(1)}, bf16[416,512]{1,0:T(8,128)(2,1)S(1)}, u32[]{:S(2)}, u32[]{:S(2)}) collective-permute-start(bf16[416,512]{1,0:T(8,128)(2,1)S(1)} %slice.15), channel_id=1, source_target_pairs={{2,0},{4,2},{6,4},{7,6},{5,7},{3,5},{1,3},{0,1},{10,8},{12,10},{14... | collective-permute-start | bytes 1277960 | tf_op jit(solution)/shard_map/ppermute | solution.py:332
  81.5 23.0 %collective-permute-start.15 = (bf16[416,512]{1,0:T(8,128)(2,1)S(1)}, bf16[416,512]{1,0:T(8,128)(2,1)S(1)}, u32[]{:S(2)}, u32[]{:S(2)}) collective-permute-start(bf16[416,512]{1,0:T(8,128)(2,1)S(1)} %slice.14), channel_id=1, source_target_pairs={{0,2},{2,4},{4,6},{6,7},{7,5},{5,3},{3,1},{1,0},{8,10},{10,12},{12... | collective-permute-start | bytes 1277960 | tf_op jit(solution)/shard_map/ppermute | solution.py:332
  90.0 14.5 %copy-start.4 = (bf16[640,1792]{1,0:T(8,128)(2,1)S(1)}, bf16[640,1792]{1,0:T(8,128)(2,1)}, u32[]{:S(2)}) copy-start(bf16[640,1792]{1,0:T(8,128)(2,1)} %copy-done.3) | copy-start | bytes 6881284
  90.0 14.5 %copy-start.5 = (bf16[1792,64]{0,1:T(8,128)(2,1)S(1)}, bf16[1792,64]{0,1:T(8,128)(2,1)}, u32[]{:S(2)}) copy-start(bf16[1792,64]{0,1:T(8,128)(2,1)} %param.13) | copy-start | bytes 688132
  90.0 17.9 %collective-permute-start.11 = (bf16[224,512]{1,0:T(8,128)(2,1)S(1)}, bf16[224,512]{1,0:T(8,128)(2,1)S(1)}, u32[]{:S(2)}, u32[]{:S(2)}) collective-permute-start(bf16[224,512]{1,0:T(8,128)(2,1)S(1)} %slice.12), channel_id=1, source_target_pairs={{0,2},{2,4},{4,6},{6,7},{7,5},{5,3},{3,1},{1,0},{8,10},{10,12},{12... | collective-permute-start | bytes 688136 | tf_op jit(solution)/shard_map/ppermute | solution.py:339
  93.2 14.7 %collective-permute-start.12 = (bf16[224,512]{1,0:T(8,128)(2,1)S(1)}, bf16[224,512]{1,0:T(8,128)(2,1)S(1)}, u32[]{:S(2)}, u32[]{:S(2)}) collective-permute-start(bf16[224,512]{1,0:T(8,128)(2,1)S(1)} %slice.13), channel_id=1, source_target_pairs={{2,0},{4,2},{6,4},{7,6},{5,7},{3,5},{1,3},{0,1},{10,8},{12,10},{14... | collective-permute-start | bytes 688136 | tf_op jit(solution)/shard_map/ppermute | solution.py:339
  110.2 4.9 %collective-permute-start.19 = (bf16[64,256]{1,0:T(8,128)(2,1)S(1)}, bf16[64,256]{1,0:T(8,128)(2,1)S(1)}, u32[]{:S(2)}, u32[]{:S(2)}) collective-permute-start(bf16[64,256]{1,0:T(8,128)(2,1)S(1)} %convert_element_type.18), channel_id=1, source_target_pairs={{0,3},{1,2},{2,1},{3,0},{4,7},{5,6},{6,5},{7,4},{8,11},{9,10},{10,... | collective-permute-start | bytes 98312 | tf_op jit(solution)/shard_map/ppermute | solution.py:349
  111.7 3.9 %collective-permute-start.18 = (bf16[64,256]{1,0:T(8,128)(2,1)S(1)}, bf16[64,256]{1,0:T(8,128)(2,1)S(1)}, u32[]{:S(2)}, u32[]{:S(2)}) collective-permute-start(bf16[64,256]{1,0:T(8,128)(2,1)S(1)} %convert_element_type.18), channel_id=1, source_target_pairs={{0,2},{1,3},{2,0},{3,1},{4,6},{5,7},{6,4},{7,5},{8,10},{9,11},{10,... | collective-permute-start | bytes 98312 | tf_op jit(solution)/shard_map/ppermute | solution.py:349
  112.0 3.9 %collective-permute-start.17 = (bf16[64,256]{1,0:T(8,128)(2,1)S(1)}, bf16[64,256]{1,0:T(8,128)(2,1)S(1)}, u32[]{:S(2)}, u32[]{:S(2)}) collective-permute-start(bf16[64,256]{1,0:T(8,128)(2,1)S(1)} %convert_element_type.18), channel_id=1, source_target_pairs={{0,1},{1,0},{2,3},{3,2},{4,5},{5,4},{6,7},{7,6},{8,9},{9,8},{10,11... | collective-permute-start | bytes 98312 | tf_op jit(solution)/shard_map/ppermute | solution.py:349
  116.0 4.9 %collective-permute-start.20 = (bf16[64,256]{1,0:T(8,128)(2,1)S(1)}, bf16[64,256]{1,0:T(8,128)(2,1)S(1)}, u32[]{:S(2)}, u32[]{:S(2)}) collective-permute-start(bf16[64,256]{1,0:T(8,128)(2,1)S(1)} %fusion), channel_id=1, source_target_pairs={{0,4},{1,5},{2,6},{3,7},{4,0},{5,1},{6,2},{7,3},{8,12},{9,13},{10,... | collective-permute-start | bytes 98312 | tf_op jit(solution)/shard_map/ppermute | solution.py:349
